TPU v7x, 128 devices: a whole 4x4x4 slice. The times are simulated.
128 devices in a mesh: section: 2 (over core), dp: 64 (over x, y, z).
Axes of the slice: x: 4, y: 4, z: 4, core: 2. Of those that a mesh axis runs over, the one named last changes fastest.
Arguments:
- inputs: bfloat16 [2, 4096, 1088], P(None, 'dp'), may hold values from -6 to 6
- cotangent: bfloat16 [2, 4096, 1088], P(None, 'dp'), may hold values from -6 to 6
- lengths: int32 [2, 64, 4], P(None, 'dp'), may hold values from 1 to 32, as said below
- vectors: bfloat16 [2, 1088, 8], P('section', 'dp'), may hold values from -1.5 to 1.5, as said below
- qkv_weight: bfloat16 [2, 1088, 3264], P('section', 'dp'), may hold values from -0.1875 to 0.1875
- out_weight: bfloat16 [2, 1088, 1088], P('section', 'dp'), may hold values from -0.75 to 0.75
- up_weight: bfloat16 [2, 1088, 4352], P('section', 'dp'), may hold values from -0.1875 to 0.1875
- up_bias: bfloat16 [2, 4352], P('section', 'dp'), may hold values from -1.5 to 1.5
- down_weight: bfloat16 [2, 4352, 1088], P('section', 'dp'), may hold values from -0.09375 to 0.09375
Outputs:
- acts_out: bfloat16 [2, 2, 4096, 1088], P('section', None, 'dp')
- grad_in: bfloat16 [2, 2, 4096, 1088], P('section', None, 'dp')
- grad_vectors: float32 [2, 1088, 8], P('section', 'dp')
- grad_qkv: float32 [2, 1088, 3264], P('section', 'dp')
- grad_out: float32 [2, 1088, 1088], P('section', 'dp')
- grad_up: float32 [2, 1088, 4352], P('section', 'dp')
- grad_up_bias: float32 [2, 4352], P('section', 'dp')
- grad_down: float32 [2, 4352, 1088], P('section', 'dp')
Inputs may be any that keep to these rules, and one draw needn't show every extreme that they name: The 4 lengths of each block sum to 64, and exactly one of them is 32. `vectors`: columns 0 and 5 lie in 0.6 to 1.4.
All inputs are finite; a program needn't handle non-finite values.
Results may differ from a plain program's by a relative error of at most 0.017.
Values may be sent and summed in bfloat16 or wider, within the bound.
No kernel may reach another device: no remote copies, remote signals or barrier semaphores. Data moves between devices by JAX's collectives and lax.ppermute only.
A program may use at most 192 MiB of HBM per device.

v0:
```python
import functools

import jax
import jax.numpy as jnp
import numpy as np
from jax import lax
from jax.experimental import pallas as pl
from jax.experimental.pallas import tpu as pltpu
from jax.sharding import Mesh, PartitionSpec as P

HEADS = 17
HDIM = 64
D = HEADS * HDIM
FF = 4 * D
SHARD = 17
NDP = 64
MAIN = 16 * NDP
PAD = 1152
ROWS = 128
PAIRS = PAD // 128

UP, DOWN, QKV, OUT, BLOCKS = 0, 4, 8, 11, 12
TAIL0 = BLOCKS * PAD
TAILW = 896
WIDTH = TAIL0 + TAILW
SMALLS = 256

NORM_EPSILON = 1e-05
SCORE_SCALE = 0.125
GELU_C = float(np.sqrt(2 / np.pi))
GELU_A = 0.044715
BF = jnp.bfloat16
F32 = jnp.float32
VMEM_BYTES = 58 * 1024 * 1024


def constants():
    n = np.arange(D)
    shard_of = np.where(n < MAIN, n // 16, n - MAIN)
    row_of = np.where(n < MAIN, n % 16, 16)
    order = np.zeros((PAD, D), np.float32)
    order[shard_of * SHARD + row_of, n] = 1
    f = np.arange(D)
    s, a, r = f // 68, (f % 68) // SHARD, f % SHARD
    hid = np.zeros((D, D), np.float32)
    hid[f, np.where(r < 16, a * 256 + s * 16 + r, 1024 + a * 16 + s)] = 1
    k = np.arange(SMALLS)
    is_vec, is_up = k < 136, (k >= 136) & (k < 204)
    k_row = np.where(is_vec, k // 8, np.where(is_up, (k - 136) % SHARD, -1))
    k_out = np.where(is_vec, k % 8, np.where(is_up, 8 + (k - 136) // SHARD, -1))
    pick = (k_out[None, :] == np.arange(16)[:, None]).astype(np.float32)
    spread = (np.arange(NDP)[:, None] == shard_of[None, :]).astype(np.float32)
    keep = (k_row[:, None] == row_of[None, :]).astype(np.float32)
    nat = np.arange(PAD)
    spread_nat = (np.arange(NDP)[:, None] == nat[None, :] // SHARD).astype(np.float32)
    keep_nat = (k_row[:, None] == nat[None, :] % SHARD).astype(np.float32)
    m = np.arange(MAIN)
    turn = np.zeros((MAIN, MAIN), np.float32)
    turn[(m % 16) * NDP + m // 16, m] = 1
    names = ("order", "hid", "pick", "spread", "keep", "spread_nat", "keep_nat", "turn")
    values = (order, hid, pick, spread, keep, spread_nat, keep_nat, turn)
    found = {name: jnp.asarray(value, BF) for name, value in zip(names, values)}
    found["order_d"] = jnp.asarray(order[:D], BF)
    found["hid_t"] = jnp.asarray(hid.T, BF)
    return found


def matmul(a, b):
    return jnp.dot(a, b, preferred_element_type=F32)


def dot_t(a, b):
    return lax.dot_general(a, b, (((1,), (1,)), ((), ())), preferred_element_type=F32)


def t_dot(a, b):
    return lax.dot_general(a, b, (((0,), (0,)), ((), ())), preferred_element_type=F32)


def norm_parts(features):
    centred = features - jnp.mean(features, axis=-1, keepdims=True)
    inverse = lax.rsqrt(jnp.mean(centred * centred, axis=-1, keepdims=True) + NORM_EPSILON)
    return centred * inverse, inverse


def norm_back(gradient, normed, inverse, gain):
    scaled = gradient * gain
    centred = scaled - jnp.mean(scaled, axis=-1, keepdims=True)
    return inverse * (centred - normed * jnp.mean(scaled * normed, axis=-1, keepdims=True))


def col_sum(v):
    return jnp.sum(v, axis=0, keepdims=True)


def unpack_kernel(whole, pick, spread, keep, spread_nat, keep_nat, turn, tails, vecs, nat, raw, sem):
    copy = pltpu.make_async_copy(whole.at[:, pl.ds(TAIL0, TAILW)], raw, sem)
    copy.start()
    copy.wait()
    turned = matmul(turn[...], raw[...]).astype(BF)
    for j in range(16):
        tails[:, j * TAILW : (j + 1) * TAILW] = turned[j * NDP : (j + 1) * NDP]
    small = tails[:, TAIL0 : TAIL0 + SMALLS]
    for out, s, k in ((vecs, spread, keep), (nat, spread_nat, keep_nat)):
        wide = t_dot(small, s[...]) * k[...].astype(F32)
        out[...] = matmul(pick[...], wide.astype(BF))


def unpack(whole, c):
    vm = pl.BlockSpec(memory_space=pltpu.VMEM)
    return pl.pallas_call(
        unpack_kernel,
        in_specs=[pl.BlockSpec(memory_space=pl.ANY)] + [vm] * 6,
        out_specs=[vm] * 3,
        out_shape=[
            jax.ShapeDtypeStruct((NDP, 16 * TAILW), BF),
            jax.ShapeDtypeStruct((16, D), F32),
            jax.ShapeDtypeStruct((16, PAD), F32),
        ],
        scratch_shapes=[pltpu.VMEM((MAIN, TAILW), BF), pltpu.SemaphoreType.DMA],
        compiler_params=pltpu.CompilerParams(vmem_limit_bytes=VMEM_BYTES),
        name="unpack",
    )(whole, c["pick"], c["spread"], c["keep"], c["spread_nat"], c["keep_nat"], c["turn"])


class Weights:
    def __init__(self, whole, tails, buf, sems):
        self.whole, self.tails, self.buf, self.sems = whole, tails, buf, sems

    def copies(self, b):
        cols = pl.ds(b * PAD, PAD)
        return (
            pltpu.make_async_copy(
                self.whole.at[:, cols], self.buf.at[b, pl.ds(0, MAIN)], self.sems.at[b, 0]
            ),
            pltpu.make_async_copy(
                self.tails.at[:, cols], self.buf.at[b, pl.ds(MAIN, NDP)], self.sems.at[b, 1]
            ),
        )

    def start(self, blocks):
        for b in blocks:
            for copy in self.copies(b):
                copy.start()

    def wait(self, b):
        for copy in self.copies(b):
            copy.wait()


def pair_masks():
    lane = lax.broadcasted_iota(jnp.int32, (ROWS, 128), 1)
    first = (lane < HDIM).astype(F32)
    return first, 1.0 - first


def stacked(v, masks):
    return jnp.concatenate([(v * m).astype(BF) for m in masks], axis=0)


def soft_pair(q, kk, allowed):
    scores = dot_t(q, kk) * SCORE_SCALE
    halves = []
    for h in range(2):
        s = jnp.where(allowed, scores[:, h * ROWS : (h + 1) * ROWS], -1e30)
        e = jnp.exp(s - jnp.max(s, axis=-1, keepdims=True))
        halves.append(e / jnp.sum(e, axis=-1, keepdims=True))
    return halves


def forward_part(w, wait, x_ref, place, pairs_ref, vecs, nat, order, r):
    x = x_ref[...].astype(F32)
    normed, _ = norm_parts(x)
    r["attn_in"][0] = (normed * vecs[0:1] + vecs[1:2]).astype(BF)

    def project(i, carry):
        if wait:
            w.wait(QKV + i)
        shift = jnp.where(i == 0, nat[2:3], jnp.where(i == 2, nat[3:4], 0.0))
        r["packed"][i] = (matmul(r["attn_in"][0], w.buf[QKV + i]) + shift).astype(BF)
        return carry

    lax.fori_loop(0, 3, project, 0)
    masks = pair_masks()
    allowed = pairs_ref[...] > 0
    for p in range(PAIRS):
        cols = pl.ds(p * 128, 128)
        kk = stacked(r["packed"][1, :, cols].astype(F32), masks)
        vv = stacked(r["packed"][2, :, cols].astype(F32), masks)
        halves = soft_pair(r["packed"][0, :, cols], kk, allowed)
        soft = jnp.concatenate([h.astype(BF) for h in halves], axis=1)
        r["heads"][:, cols] = matmul(soft, vv).astype(BF)
    r["attn_in"][1] = matmul(r["heads"][...], order[...]).astype(BF)
    if wait:
        w.wait(OUT)
    branch = matmul(r["attn_in"][1], w.buf[OUT])[:, :D]
    middle = x + branch + vecs[4:5]
    r["middle"][...] = middle
    normed, _ = norm_parts(middle)
    r["second"][...] = (normed * vecs[5:6] + vecs[6:7]).astype(BF)
    r["acc"][...] = jnp.zeros((ROWS, PAD), F32)

    def feed(a, carry):
        if wait:
            w.wait(UP + a)
        hidden = matmul(r["second"][...], w.buf[UP + a])[:, :D] + vecs[pl.ds(8 + a, 1)]
        r["hidden"][a] = hidden
        bent = jnp.tanh(GELU_C * (hidden + GELU_A * (hidden * hidden * hidden)))
        r["active"][a] = (0.5 * hidden * (1.0 + bent)).astype(BF)
        if wait:
            w.wait(DOWN + a)
        r["acc"][...] += matmul(r["active"][a], w.buf[DOWN + a])
        return carry

    lax.fori_loop(0, 4, feed, 0)
    r["result"][...] = (r["middle"][...] + r["acc"][:, :D] + vecs[7:8]).astype(BF)
    for d in range(4):
        z = lax.rem(place[2] + d, 4)
        out = r[f"early{d}"]
        out[0, :, :D] = r["second"][...]
        out[1, :, :D] = r["active"][z]
        out[2, :, :D] = r["attn_in"][z // 3]


def backward_part(w, wait, grad_ref, x_ref, place, pairs_ref, vecs, order, r):
    grad = grad_ref[...]
    dres = grad.astype(F32)
    r["acc"][...] = jnp.zeros((ROWS, PAD), F32)

    def feed(a, carry):
        if wait:
            w.wait(DOWN + a)
        dactive = dot_t(grad_ref[...], w.buf[DOWN + a, :, :D])
        h = r["hidden"][a]
        square = h * h
        bent = jnp.tanh(GELU_C * (h + GELU_A * (square * h)))
        slope = 0.5 * (1.0 + bent) + (0.5 * GELU_C) * h * (1.0 - bent * bent) * (
            1.0 + (3 * GELU_A) * square
        )
        dhidden = (dactive * slope).astype(BF)
        r["dhidden"][a] = dhidden
        r["small"][pl.ds(8 + a, 1)] = col_sum(dhidden.astype(F32))
        if wait:
            w.wait(UP + a)
        r["acc"][:, :D] += dot_t(dhidden, w.buf[UP + a, :, :D])
        return carry

    lax.fori_loop(0, 4, feed, 0)
    dsecond = r["acc"][:, :D]
    normed, inverse = norm_parts(r["middle"][...])
    r["small"][5:6] = col_sum(dsecond * normed)
    r["small"][6:7] = col_sum(dsecond)
    r["small"][7:8] = col_sum(dres)
    dmiddle = dres + norm_back(dsecond, normed, inverse, vecs[5:6])
    r["middle"][...] = dmiddle
    dattn = dmiddle.astype(BF)
    r["dpacked"][3] = dattn
    r["small"][4:5] = col_sum(dattn.astype(F32))
    if wait:
        w.wait(OUT)
    dmixed = dot_t(dattn, w.buf[OUT, :, :D]).astype(BF)
    r["heads"][...] = dot_t(dmixed, order[...]).astype(BF)
    masks = pair_masks()
    allowed = pairs_ref[...] > 0
    for p in range(PAIRS):
        cols = pl.ds(p * 128, 128)
        width = min(D - p * 128, 128)
        live = pl.ds(p * 128, width)
        q = r["packed"][0, :, cols]
        kk = stacked(r["packed"][1, :, cols].astype(F32), masks)
        vv = stacked(r["packed"][2, :, cols].astype(F32), masks)
        dm = r["heads"][:, cols]
        halves = soft_pair(q, kk, allowed)
        dsoft = dot_t(dm, vv)
        dscores = []
        for h, p_half in enumerate(halves):
            d_half = dsoft[:, h * ROWS : (h + 1) * ROWS]
            centre = jnp.sum(d_half * p_half, axis=-1, keepdims=True)
            dscores.append((p_half * (d_half - centre)).astype(BF))
        ds = jnp.concatenate(dscores, axis=1)
        soft = jnp.concatenate([h.astype(BF) for h in halves], axis=1)
        dq = matmul(ds, kk) * SCORE_SCALE
        dk = t_dot(ds, q) * SCORE_SCALE
        dv = t_dot(soft, dm)
        dk = dk[:ROWS] * masks[0] + dk[ROWS:] * masks[1]
        dv = dv[:ROWS] * masks[0] + dv[ROWS:] * masks[1]
        for i, v in enumerate((dq, dk, dv)):
            r["dpacked"][i, :, live] = v[:, :width].astype(BF)
    sums = [col_sum(r["dpacked"][i].astype(F32)) for i in (0, 2)]
    sums = jnp.concatenate(sums + [jnp.zeros((14, D), F32)], axis=0).astype(BF)
    r["small"][2:4] = matmul(sums, order[:D])[:2]
    r["acc"][...] = jnp.zeros((ROWS, PAD), F32)

    def project(i, carry):
        if wait:
            w.wait(QKV + i)
        r["acc"][:, :D] += dot_t(r["dpacked"][i], w.buf[QKV + i, :, :D])
        return carry

    lax.fori_loop(0, 3, project, 0)
    dentry = r["acc"][:, :D]
    normed, inverse = norm_parts(x_ref[...].astype(F32))
    r["small"][0:1] = col_sum(dentry * normed)
    r["small"][1:2] = col_sum(dentry)
    r["small"][12:16] = jnp.zeros((4, D), F32)
    r["dx"][...] = (r["middle"][...] + norm_back(dentry, normed, inverse, vecs[0:1])).astype(BF)
    for d in range(4):
        z = lax.rem(place[2] + d, 4)
        r[f"late{d}"][0, :, :D] = r["dhidden"][z]
        r[f"late{d}"][1, :, :D] = r["dpacked"][z]


ROW = (ROWS, D)
KEPT = {
    "packed": ((3, ROWS, PAD), BF),
    "middle": (ROW, F32),
    "hidden": ((4,) + ROW, F32),
}
FWD_OUT = {"result": (ROW, BF), **{f"early{d}": ((3, ROWS, PAD), BF) for d in range(4)}}
BWD_OUT = {
    "dx": (ROW, BF),
    **{f"late{d}": ((2, ROWS, PAD), BF) for d in range(4)},
    "small": ((16, D), F32),
}
FWD_WORK = {
    "attn_in": ((2,) + ROW, BF),
    "second": (ROW, BF),
    "active": ((4,) + ROW, BF),
}
BWD_WORK = {
    "dhidden": ((4,) + ROW, BF),
    "dpacked": ((4,) + ROW, BF),
}
WORK = {"heads": ((ROWS, PAD), BF), "acc": ((ROWS, PAD), F32)}


def layer_call(kind, whole, tails, vecs, nat, pairs, order, place, x, grad=None, old=None):
    outs = dict(FWD_OUT) if kind != "bwd" else {}
    work = dict(WORK)
    if kind == "fwd":
        outs.update(KEPT)
    else:
        outs.update(BWD_OUT)
        work.update(BWD_WORK)
    if kind != "bwd":
        work.update(FWD_WORK)
    else:
        work["active"] = FWD_WORK["active"]
    if kind != "fwd":
        work.update(KEPT)
    passed = {"fwd": {}, "both": FWD_OUT, "bwd": BWD_OUT}[kind]
    loaded = KEPT if kind == "bwd" else {}
    far = [whole, tails] + [old[k] for k in (*passed, *loaded)]
    near = [vecs, nat, pairs, order, x] + ([] if grad is None else [grad])
    section = 1 if kind == "both" else 0

    def kernel(place_ref, *refs):
        far_refs, refs = refs[: len(far)], refs[len(far) :]
        near_refs, refs = refs[: len(near)], refs[len(near) :]
        r = dict(zip(outs, refs))
        refs = refs[len(outs) :]
        r.update(zip(work, refs))
        buf, sems, old_sems = refs[len(work) :]
        w = Weights(far_refs[0], far_refs[1], buf, sems)
        vecs_ref, nat_ref, pairs_ref, order_ref, x_ref = near_refs[:5]
        old_refs = dict(zip((*passed, *loaded), far_refs[2:]))

        def fetch(names):
            return [
                pltpu.make_async_copy(old_refs[k], r[k], old_sems.at[i])
                for i, k in enumerate(names)
            ]

        @pl.when(place_ref[3] == section)
        def _():
            if kind == "bwd":
                w.start([DOWN])
                copies = fetch(loaded)
                for copy in copies:
                    copy.start()
                w.start([UP] + [b for a in range(1, 4) for b in (DOWN + a, UP + a)])
                w.start([OUT, 8, 9, 10])
                for copy in copies:
                    copy.wait()
            else:
                w.start([8, 9, 10, OUT] + [b for a in range(4) for b in (UP + a, DOWN + a)])
                forward_part(w, True, x_ref, place_ref, pairs_ref, vecs_ref, nat_ref, order_ref, r)
            if kind != "fwd":
                backward_part(
                    w,
                    kind == "bwd",
                    near_refs[5],
                    x_ref,
                    place_ref,
                    pairs_ref,
                    vecs_ref,
                    order_ref,
                    r,
                )

        if passed:

            @pl.when(place_ref[3] != section)
            def _():
                copies = fetch(passed)
                for copy in copies:
                    copy.start()
                for copy in copies:
                    copy.wait()

    vm = pl.BlockSpec(memory_space=pltpu.VMEM)
    results = pl.pallas_call(
        kernel,
        in_specs=[pl.BlockSpec(memory_space=pltpu.SMEM)]
        + [pl.BlockSpec(memory_space=pl.ANY)] * len(far)
        + [vm] * len(near),
        out_specs=[vm] * len(outs),
        out_shape=[jax.ShapeDtypeStruct(s, t) for s, t in outs.values()],
        scratch_shapes=[pltpu.VMEM(s, t) for s, t in work.values()]
        + [
            pltpu.VMEM((BLOCKS, D, PAD), BF),
            pltpu.SemaphoreType.DMA((BLOCKS, 2)),
            pltpu.SemaphoreType.DMA((16,)),
        ],
        compiler_params=pltpu.CompilerParams(vmem_limit_bytes=VMEM_BYTES),
        cost_estimate=pl.CostEstimate(
            flops={"fwd": 4, "both": 12, "bwd": 8}[kind] * 10**9,
            bytes_accessed=BLOCKS * D * PAD * 2,
            transcendentals=10**6,
        ),
        name="layer_" + kind,
    )(place, *far, *near)
    return dict(zip(outs, results))


CHUNK = 72
HALF = 768
WIDE = (PAD + HALF, PAD + PAD - HALF)


def local_call(kernel, name, place, ins, out_shapes, scratch=(), far=()):
    vm = pl.BlockSpec(memory_space=pltpu.VMEM)
    hbm = pl.BlockSpec(memory_space=pl.ANY)
    return pl.pallas_call(
        kernel,
        in_specs=[pl.BlockSpec(memory_space=pltpu.SMEM)] + [hbm] * len(far) + [vm] * len(ins),
        out_specs=[vm] * len(out_shapes),
        out_shape=[jax.ShapeDtypeStruct(s, t) for s, t in out_shapes],
        scratch_shapes=list(scratch),
        compiler_params=pltpu.CompilerParams(vmem_limit_bytes=VMEM_BYTES),
        name=name,
    )(place, *far, *ins)


def products_kernel(place, *refs):
    given, small, outs = refs[:12], refs[12], refs[13:21]
    first, second, early, late, branch, sems = refs[21:]
    copies = []
    for g, held in enumerate((early, late, branch)):
        for d in range(4):
            i = 4 * g + d
            copies.append(pltpu.make_async_copy(given[i], held.at[d], sems.at[i]))
    for i in (8, 9, 10, 11, 0, 1, 2, 3, 4, 5, 6, 7):
        copies[i].start()

    def wait(g):
        for copy in copies[4 * g : 4 * g + 4]:
            copy.wait()

    def rows_of(held, i=None):
        parts = [held[d] if i is None else held[d, i, :, :D] for d in range(4)]
        return jnp.concatenate(parts, axis=0)

    gap = jnp.zeros((4 * ROWS, PAD - D), BF)
    slot = lax.broadcasted_iota(jnp.int32, (16, PAD), 1) - D
    unit = (slot == lax.broadcasted_iota(jnp.int32, (16, PAD), 0)).astype(F32).astype(BF)
    nothing = jnp.zeros((4, PAD), F32)

    def product(a, b, store):
        last = t_dot(a[:, MAIN:], b)
        for x in range(4):
            main = t_dot(a[:, x * 256 : (x + 1) * 256], b)
            for y in range(4):
                at = (x * 4 + y) * 4
                rows = [main[y * 64 : (y + 1) * 64], last[at : at + 4], nothing]
                store(x, y, jnp.concatenate(rows, axis=0).astype(BF))

    def store_up(x, y, v):
        first[x, y, :, :PAD] = v

    def store_down(x, y, v):
        second[y, x, :, :PAD] = v

    def store_attn(x, y, v):
        first[x, y, :, PAD:] = v[:, :HALF]
        second[y, x, :, PAD:] = v[:, HALF:]

    def wide(v):
        return jnp.concatenate([v, gap], axis=1)

    wait(2)
    wait(0)
    product(rows_of(early, 1), wide(rows_of(branch)), store_down)
    wait(1)
    product(rows_of(early, 0), wide(rows_of(late, 0)), store_up)
    a = jnp.concatenate([rows_of(early, 2), small[...].astype(BF)], axis=0)
    b = jnp.concatenate([wide(rows_of(late, 1)), unit], axis=0)
    product(a, b, store_attn)
    for d in range(4):
        outs[d][...] = first[lax.rem(place[0] + d, 4)]
        outs[4 + d][...] = second[lax.rem(place[1] + d, 4)]


def total(parts):
    return sum((p.astype(F32) for p in parts[1:]), parts[0].astype(F32))


def first_sum_kernel(place, *refs):
    for h, other in ((0, 1), (1, 0)):
        parts, outs = refs[4 * h : 4 * h + 4], refs[8 + 4 * h : 12 + 4 * h]
        for d in range(4):
            i = lax.rem(place[other] + d, 4)
            outs[d][...] = total([p[i] for p in parts]).astype(BF)


def second_sum_kernel(place, *refs):
    outs, held = refs[8:12], refs[12]
    for h in range(2):
        full = total([p[...] for p in refs[4 * h : 4 * h + 4]])
        start = h * WIDE[0]
        empty = jnp.zeros((7, WIDE[h]), F32)
        for z in range(4):
            rows = [full[z * 16 : (z + 1) * 16], full[64 + z : 65 + z], empty]
            held[z, :, start : start + WIDE[h]] = jnp.concatenate(rows, axis=0).astype(BF)
    for d in range(4):
        outs[d][...] = held[lax.rem(place[2] + d, 4)]


def final_kernel(place, *refs):
    parts, (hid, order), outs, held = refs[:4], refs[4:6], refs[6:11], refs[11]
    g_up, g_down, g_out, g_qkv, sums = outs
    for d in range(4):
        held[lax.rem(place[2] + 4 - d, 4)] = parts[d][...]
    up = []
    for j in range(4):
        pieces = [held[a, :, j * 256 : (j + 1) * 256] for a in range(4)]
        pieces += [held[a, :, MAIN + j * 16 : MAIN + (j + 1) * 16] for a in range(4)]
        up.append(jnp.concatenate(pieces, axis=1))
    up = matmul(jnp.concatenate(up, axis=0), hid[...])
    up = jnp.concatenate([up[j * 24 : (j + 1) * 24] for j in range(4)], axis=1)
    for i in range(SHARD):
        g_up[i] = up[i : i + 1]
    start = WIDE[0]
    attn = [
        jnp.concatenate([held[a, :, PAD:start], held[a, :, start + PAD :]], axis=1)
        for a in range(4)
    ]
    rows = [held[a, :, start : start + D] for a in range(4)] + [attn[3][:, :D]]
    rows = dot_t(jnp.concatenate(rows, axis=0), order[:D])
    qkv = jnp.concatenate([v[:, :D].astype(F32) for v in attn[:3]], axis=1)
    for i in range(SHARD):
        for a in range(4):
            g_down[a * SHARD + i] = rows[a * 24 + i : a * 24 + i + 1]
        g_out[i] = rows[96 + i : 97 + i]
        g_qkv[i] = qkv[i : i + 1]
    sums[...] = total([v[:SHARD, D:] for v in attn])


def ring(v, axis, d):
    return lax.ppermute(v, axis, [(i, (i + d) % 4) for i in range(4)])


def restore_kernel(place, order, result, dx, acts, grads):
    acts[...] = dot_t(result[...], order[:D]).astype(BF)
    grads[...] = dot_t(dx[...], order[:D]).astype(BF)


def pad_cols(v, width):
    return jnp.pad(v, ((0, 0), (0, width - v.shape[1])))


def body(inputs, cotangent, lengths, vectors, qkv_w, out_w, up_w, up_b, down_w):
    section = lax.axis_index("section")
    mb, rows, _ = inputs.shape
    n = mb * rows
    c = constants()
    order = c["order"]

    outdown = matmul(jnp.concatenate([out_w[0], down_w[0]], axis=0), c["order_d"]).astype(BF)
    hid = matmul(up_w[0].reshape(SHARD * 4, D), c["hid"]).astype(BF).reshape(SHARD, 4, D)
    hid_main = hid[:, :, :MAIN].reshape(SHARD, 4, 4, 256).transpose(0, 2, 1, 3)
    hid_last = hid[:, :, MAIN:].reshape(SHARD, 4, 4, 16).transpose(0, 2, 1, 3)
    hid = jnp.concatenate(
        [
            hid_main.reshape(SHARD, 4, MAIN),
            hid_last.reshape(SHARD, 4, NDP),
            jnp.zeros((SHARD, 4, PAD - D), BF),
        ],
        axis=2,
    )
    shard = [hid.reshape(SHARD, 4 * PAD)]
    shard += [pad_cols(outdown[SHARD * (1 + a) : SHARD * (2 + a)], PAD) for a in range(4)]
    shard += [pad_cols(qkv_w[0][:, i * D : (i + 1) * D], PAD) for i in range(3)]
    shard += [pad_cols(outdown[:SHARD], PAD)]
    shard = jnp.concatenate(shard, axis=1)
    tail = jnp.concatenate([shard[16], vectors[0].reshape(-1), up_b[0]])
    tail = jnp.pad(tail, (0, 16 * TAILW - tail.shape[0])).reshape(16, TAILW)
    sent = jnp.concatenate([shard[:16], tail], axis=1)
    whole = lax.all_gather(sent, ("x", "y", "z"), axis=0, tiled=True)
    tails, vecs, nat = unpack(whole, c)

    ends = jnp.cumsum(lengths[:, 0], axis=1)
    place = jnp.arange(rows, dtype=jnp.int32)
    seg = jnp.sum((place[None, :, None] >= ends[:, None, :]).astype(jnp.int32), axis=2)
    seg = (seg + 8 * jnp.arange(mb, dtype=jnp.int32)[:, None]).reshape(n)
    at = jnp.arange(n, dtype=jnp.int32)
    pairs = ((seg[:, None] == seg[None, :]) & (at[:, None] >= at[None, :])).astype(F32)

    order_d = c["order_d"]
    x0 = matmul(inputs.reshape(n, D), order_d).astype(BF)
    cot = matmul(cotangent.reshape(n, D), order_d).astype(BF)
    place = jnp.stack([lax.axis_index("x"), lax.axis_index("y"), lax.axis_index("z"), section])
    call = functools.partial(
        layer_call,
        whole=whole,
        tails=tails,
        vecs=vecs,
        nat=nat,
        pairs=pairs,
        order=order,
        place=place,
    )

    first = call("fwd", x=x0)
    arrived = lax.ppermute(first["result"], "section", [(0, 1)])
    top = call("both", x=arrived, grad=cot, old=first)
    coming = lax.ppermute(top["dx"], "section", [(1, 0)])
    early = [top["early0"]] + [ring(top[f"early{d}"], "z", d) for d in (1, 3, 2)]
    coming, *early = lax.optimization_barrier((coming, *early))
    branch = jnp.where(section == 0, coming, cot)
    branches = [branch] + [ring(branch, "z", d) for d in (1, 3, 2)]
    kept = {k: first[k] for k in KEPT}
    bwd = call("bwd", x=x0, grad=coming, old={**{k: top[k] for k in BWD_OUT}, **kept})
    late = [bwd["late0"]] + [ring(bwd[f"late{d}"], "z", d) for d in (1, 3, 2)]

    vmem = pltpu.VMEM
    out = local_call(
        products_kernel,
        "products",
        place,
        [bwd["small"]],
        [((4, CHUNK, WIDE[h]), BF) for h in (0, 1) for _ in range(4)],
        [vmem((4, 4, CHUNK, WIDE[h]), BF) for h in (0, 1)]
        + [vmem((4, k, ROWS, PAD), BF) for k in (3, 2)]
        + [vmem((4,) + ROW, BF), pltpu.SemaphoreType.DMA((12,))],
        far=[*early, *late, *branches],
    )
    got = [out[0]] + [ring(out[d], "x", d) for d in (2, 1, 3)]
    after = ring(out[5], "y", 1)
    held, after = lax.optimization_barrier((out[7], after))
    got += [out[4], ring(out[6], "y", 2), after, ring(held, "y", 3)]
    out = local_call(
        first_sum_kernel,
        "first_sum",
        place,
        got,
        [((CHUNK, WIDE[h]), BF) for h in (0, 1) for _ in range(4)],
    )
    got = []
    for h, axis in ((0, "y"), (1, "x")):
        got += [out[4 * h]] + [ring(out[4 * h + d], axis, d) for d in (1, 3, 2)]
    out = local_call(
        second_sum_kernel,
        "second_sum",
        place,
        got,
        [((24, sum(WIDE)), BF)] * 4,
        [vmem((4, 24, sum(WIDE)), BF)],
    )
    got = [out[0]] + [ring(out[d], "z", d) for d in (1, 2, 3)]
    g_up, g_down, g_out, g_qkv, sums = local_call(
        final_kernel,
        "owners",
        place,
        [*got, c["hid_t"], order],
        [
            ((SHARD, 1, FF), F32),
            ((4 * SHARD, 1, D), F32),
            ((SHARD, 1, D), F32),
            ((SHARD, 1, 3 * D), F32),
            ((SHARD, PAD - D), F32),
        ],
        [vmem((4, 24, sum(WIDE)), BF)],
    )
    acts, grads = local_call(
        restore_kernel, "restore", place, [order, top["result"], bwd["dx"]], [(ROW, BF)] * 2
    )
    return (
        acts.reshape(1, mb, rows, D),
        grads.reshape(1, mb, rows, D),
        sums[None, :, :8],
        g_qkv.reshape(1, SHARD, 3 * D),
        g_out.reshape(1, SHARD, D),
        g_up.reshape(1, SHARD, FF),
        sums[:, 8:12].T.reshape(1, 4 * SHARD),
        g_down.reshape(1, 4 * SHARD, D),
    )


def solution(mesh):
    grid = Mesh(mesh.devices.reshape(2, 4, 4, 4), ("section", "x", "y", "z"))
    dp = ("x", "y", "z")
    tokens = P(None, dp, None)
    rows = P("section", dp, None)
    in_specs = (tokens, tokens, tokens, rows, rows, rows, rows, P("section", dp), rows)
    stacks = P("section", None, dp, None)
    out_specs = (stacks, stacks, rows, rows, rows, rows, P("section", dp), rows)
    return jax.shard_map(body, mesh=grid, in_specs=in_specs, out_specs=out_specs, check_vma=False)
```

profile of v0, /device:TPU:0, one launch (start us, length us, event | category | flops | bytes accessed | tf_op | source)
XLA Modules:
  0.0 421.2 jit_solution(11415315368966270712)
XLA Ops:
  20.4 148.2 %all-gather.2.cloned.1.call-done.whole.refs_0_ = bf16[1024,14720]{1,0:T(8,128)(2,1)} async-done(((bf16[16,14720]{1,0:T(8,128)(2,1)}), bf16[1024,14720]{1,0:T(8,128)(2,1)}) %all-gather.2.cloned.1.call-update) | async-done | bytes 30146576 | tf_op jit(solution)/shard_map/all_gather | solution.py:609
  168.6 7.4 %unpack.1 = (bf16[64,14336]{1,0:T(8,128)(2,1)}, f32[16,1088]{1,0:T(8,128)}, f32[16,1152]{1,0:T(8,128)}) custom-call(bf16[1024,14720]{1,0:T(8,128)(2,1)} %all-gather.2.cloned.1.call-done.whole.refs_0_, bf16[16,256]{1,0:T(8,128)(2,1)} %constant.51.clone.pick, bf16[64,1088]{1,0:T(8,128)(2,1)} %constant.52.clone.spread, bf16[256,1088]{1,0:T(8,128)(2,1)} %constant.53.clone.keep, ...), custom_call_target="tpu_custom_call" | custom-call | tf_op jit(solution)/shard_map/unpack/pallas_call | solution.py:111
  176.0 16.9 %layer_fwd.1 = (bf16[128,1088]{1,0:T(8,128)(2,1)}, bf16[3,128,1152]{2,1,0:T(8,128)(2,1)}, bf16[3,128,1152]{2,1,0:T(8,128)(2,1)}, bf16[3,128,1152]{2,1,0:T(8,128)...) custom-call(s32[4]{0:T(128)} %pad_add_fusion.place_ref.place, ...), custom_call_target="tpu_custom_call" | custom-call | flops 4000000000 | bytes 30081024 | tf_op jit(solution)/shard_map/layer_fwd/pallas_call | solution.py:412
  196.7 7.5 %layer_both.1 = (bf16[128,1088]{1,0:T(8,128)(2,1)}, bf16[3,128,1152]{2,1,0:T(8,128)(2,1)}, bf16[3,128,1152]{2,1,0:T(8,128)(2,1)}, bf16[3,128,1152]{2,1,0:T(8,128...) custom-call(s32[4]{0:T(128)} %pad_add_fusion.place_ref.place, ...), custom_call_target="tpu_custom_call" | custom-call | flops 12000000000 | bytes 30081024 | tf_op jit(solution)/shard_map/layer_both/pallas_call | solution.py:412
  205.2 3.6 collective-permute-start.3
  210.7 26.6 %collective-permute-done.1.refs_16_ = bf16[128,1088]{1,0:T(8,128)(2,1)S(1)} collective-permute-done((bf16[128,1088]{1,0:T(8,128)(2,1)}, bf16[128,1088]{1,0:T(8,128)(2,1)S(1)}, u32[]{:S(2)}, u32[]{:S(2)}) %collective-permute-start.1) | collective-permute-done | bytes 278560 | tf_op jit(solution)/shard_map/ppermute | solution.py:637
  238.0 33.7 %layer_bwd.1 = (bf16[128,1088]{1,0:T(8,128)(2,1)}, bf16[2,128,1152]{2,1,0:T(8,128)(2,1)}, bf16[2,128,1152]{2,1,0:T(8,128)(2,1)}, bf16[2,128,1152]{2,1,0:T(8,128)...) custom-call(s32[4]{0:T(128)} %pad_add_fusion.place_ref.place, ...), custom_call_target="tpu_custom_call" | custom-call | flops 8000000000 | bytes 30081024 | tf_op jit(solution)/shard_map/layer_bwd/pallas_call | solution.py:412
  272.5 2.5 collective-permute-start.6
  277.2 2.5 collective-permute-start.10
  279.7 20.6 %collective-permute-done.10.refs_11_ = bf16[128,1088]{1,0:T(8,128)(2,1)S(1)} collective-permute-done((bf16[128,1088]{1,0:T(8,128)(2,1)S(1)}, bf16[128,1088]{1,0:T(8,128)(2,1)S(1)}, u32[]{:S(2)}, u32[]{:S(2)}) %collective-permute-start.10) | collective-permute-done | bytes 278560 | tf_op jit(solution)/shard_map/ppermute | solution.py:570
  302.0 6.4 %collective-permute-done.8.refs_9_ = bf16[128,1088]{1,0:T(8,128)(2,1)S(1)} collective-permute-done((bf16[128,1088]{1,0:T(8,128)(2,1)S(1)}, bf16[128,1088]{1,0:T(8,128)(2,1)S(1)}, u32[]{:S(2)}, u32[]{:S(2)}) %collective-permute-start.8) | collective-permute-done | bytes 278560 | tf_op jit(solution)/shard_map/ppermute | solution.py:570
  309.7 12.5 %products.1 = (bf16[4,72,1920]{2,1,0:T(8,128)(2,1)}, bf16[4,72,1920]{2,1,0:T(8,128)(2,1)}, bf16[4,72,1920]{2,1,0:T(8,128)(2,1)}, bf16[4,72,1920]{2,1,0:T(8,128)(...) custom-call(s32[4]{0:T(128)} %pad_add_fusion.place_ref.place, ...), custom_call_target="tpu_custom_call" | custom-call | tf_op jit(solution)/shard_map/products/pallas_call | solution.py:444
  323.7 3.0 collective-permute-start.11
  327.3 2.7 collective-permute-start.13
  330.0 2.7 collective-permute-start.14
  332.7 12.6 %collective-permute-done.15.refs_6_ = bf16[4,72,1536]{2,1,0:T(8,128)(2,1)S(1)} collective-permute-done((bf16[4,72,1536]{2,1,0:T(8,128)(2,1)}, bf16[4,72,1536]{2,1,0:T(8,128)(2,1)S(1)}, u32[]{:S(2)}, u32[]{:S(2)}) %collective-permute-start.15) | collective-permute-done | bytes 884768 | tf_op jit(solution)/shard_map/ppermute | solution.py:570
  345.2 2.5 collective-permute-start.16
  347.8 10.0 %collective-permute-done.14.refs_5_ = bf16[4,72,1536]{2,1,0:T(8,128)(2,1)S(1)} collective-permute-done((bf16[4,72,1536]{2,1,0:T(8,128)(2,1)}, bf16[4,72,1536]{2,1,0:T(8,128)(2,1)S(1)}, u32[]{:S(2)}, u32[]{:S(2)}) %collective-permute-start.14) | collective-permute-done | bytes 884768 | tf_op jit(solution)/shard_map/ppermute | solution.py:570
  357.7 10.0 %collective-permute-done.12.refs_2_ = bf16[4,72,1920]{2,1,0:T(8,128)(2,1)S(1)} collective-permute-done((bf16[4,72,1920]{2,1,0:T(8,128)(2,1)}, bf16[4,72,1920]{2,1,0:T(8,128)(2,1)S(1)}, u32[]{:S(2)}, u32[]{:S(2)}) %collective-permute-start.12) | collective-permute-done | bytes 1105952 | tf_op jit(solution)/shard_map/ppermute | solution.py:570
  369.4 5.1 %first_sum.1 = (bf16[72,1920]{1,0:T(8,128)(2,1)}, bf16[72,1920]{1,0:T(8,128)(2,1)}, bf16[72,1920]{1,0:T(8,128)(2,1)}, bf16[72,1920]{1,0:T(8,128)(2,1)}, bf16[72,...) custom-call(s32[4]{0:T(128)} %pad_add_fusion.place_ref.place, ...), custom_call_target="tpu_custom_call" | custom-call | tf_op jit(solution)/shard_map/first_sum/pallas_call | solution.py:444
  383.4 7.8 %collective-permute-done.21.refs_6_ = bf16[72,1536]{1,0:T(8,128)(2,1)S(1)} collective-permute-done((bf16[72,1536]{1,0:T(8,128)(2,1)}, bf16[72,1536]{1,0:T(8,128)(2,1)S(1)}, u32[]{:S(2)}, u32[]{:S(2)}) %collective-permute-start.21) | collective-permute-done | bytes 221216 | tf_op jit(solution)/shard_map/ppermute | solution.py:570
  392.4 2.8 second_sum.1
  398.7 4.3 %restore.1 = (bf16[128,1088]{1,0:T(8,128)(2,1)}, bf16[128,1088]{1,0:T(8,128)(2,1)}) custom-call(s32[4]{0:T(128)} %pad_add_fusion.place_ref.place, bf16[1152,1088]{1,0:T(8,128)(2,1)} %constant.49.clone.refs_5_.refs_10_.refs_14_.order, bf16[128,1088]{1,0:T(8,128)(2,1)} %get-tuple-element.78.result, bf16[128,1088]{1,0:T(8,128)(2,1)} %get-tuple-element.93.dx), custom_call_target="tpu_custom_call" | custom-call | tf_op jit(solution)/shard_map/restore/pallas_call | solution.py:444
  406.1 5.0 %owners.1 = (f32[17,1,4352]{2,1,0:T(1,128)}, f32[68,1,1088]{2,1,0:T(1,128)}, f32[17,1,1088]{2,1,0:T(1,128)}, f32[17,1,3264]{2,1,0:T(1,128)}, f32[17,64]{1,0:T(8,128)}) custom-call(s32[4]{0:T(128)} %pad_add_fusion.place_ref.place, bf16[24,3456]{1,0:T(8,128)(2,1)} %get-tuple-element.123.refs_0_, bf16[24,3456]{1,0:T(8,128)(2,1)} %copy-done.29, ...), custom_call_target="tpu_custom_call" | custom-call | tf_op jit(solution)/shard_map/owners/pallas_call | solution.py:444
  (166 shorter events, 49.5 us)
Async XLA Ops:
  7.2 161.4 %all-gather.2.cloned.1.call-start = ((), (), s32[]{:S(2)}) async-start(), calls=%async_computation | async-start | bytes 30617600 | tf_op jit(solution)/shard_map/all_gather | solution.py:609
  204.3 33.0 %collective-permute-start.2 = (bf16[3,128,1152]{2,1,0:T(8,128)(2,1)}, bf16[3,128,1152]{2,1,0:T(8,128)(2,1)S(1)}, u32[]{:S(2)}, u32[]{:S(2)}) collective-permute-start(bf16[3,128,1152]{2,1,0:T(8,128)(2,1)} %get-tuple-element.89), channel_id=1, source_target_pairs={{0,1},{1,2},{2,3},{3,0},{4,5},{5,6},{6,7},{7,4},{8,9},{9,10},{10,1... | collective-permute-start | bytes 2654216 | tf_op jit(solution)/shard_map/ppermute | solution.py:570
  205.2 32.1 %collective-permute-start.3 = (bf16[3,128,1152]{2,1,0:T(8,128)(2,1)}, bf16[3,128,1152]{2,1,0:T(8,128)(2,1)S(1)}, u32[]{:S(2)}, u32[]{:S(2)}) collective-permute-start(bf16[3,128,1152]{2,1,0:T(8,128)(2,1)} %get-tuple-element.90), channel_id=1, source_target_pairs={{0,3},{1,0},{2,1},{3,2},{4,7},{5,4},{6,5},{7,6},{8,11},{9,8},{10,9... | collective-permute-start | bytes 2654216 | tf_op jit(solution)/shard_map/ppermute | solution.py:570
  208.7 28.5 %collective-permute-start.4 = (bf16[3,128,1152]{2,1,0:T(8,128)(2,1)}, bf16[3,128,1152]{2,1,0:T(8,128)(2,1)S(1)}, u32[]{:S(2)}, u32[]{:S(2)}) collective-permute-start(bf16[3,128,1152]{2,1,0:T(8,128)(2,1)} %get-tuple-element.91), channel_id=1, source_target_pairs={{0,2},{1,3},{2,0},{3,1},{4,6},{5,7},{6,4},{7,5},{8,10},{9,11},{10,... | collective-permute-start | bytes 2654216 | tf_op jit(solution)/shard_map/ppermute | solution.py:570
  209.4 27.9 %collective-permute-start.1 = (bf16[128,1088]{1,0:T(8,128)(2,1)}, bf16[128,1088]{1,0:T(8,128)(2,1)S(1)}, u32[]{:S(2)}, u32[]{:S(2)}) collective-permute-start(bf16[128,1088]{1,0:T(8,128)(2,1)} %get-tuple-element.79.refs_2_), channel_id=1, source_target_pairs={{64,0},{65,1},{66,2},{67,3},{68,4},{69,5},{70,6},{71,7},{72,8},{73... | collective-permute-start | bytes 835592 | tf_op jit(solution)/shard_map/ppermute | solution.py:637
  271.7 36.6 %collective-permute-start.5 = (bf16[2,128,1152]{2,1,0:T(8,128)(2,1)}, bf16[2,128,1152]{2,1,0:T(8,128)(2,1)S(1)}, u32[]{:S(2)}, u32[]{:S(2)}) collective-permute-start(bf16[2,128,1152]{2,1,0:T(8,128)(2,1)} %get-tuple-element.101), channel_id=1, source_target_pairs={{0,1},{1,2},{2,3},{3,0},{4,5},{5,6},{6,7},{7,4},{8,9},{9,10},{10,1... | collective-permute-start | bytes 1769480 | tf_op jit(solution)/shard_map/ppermute | solution.py:570
  272.5 35.9 %collective-permute-start.6 = (bf16[2,128,1152]{2,1,0:T(8,128)(2,1)}, bf16[2,128,1152]{2,1,0:T(8,128)(2,1)S(1)}, u32[]{:S(2)}, u32[]{:S(2)}) collective-permute-start(bf16[2,128,1152]{2,1,0:T(8,128)(2,1)} %get-tuple-element.102), channel_id=1, source_target_pairs={{0,3},{1,0},{2,1},{3,2},{4,7},{5,4},{6,5},{7,6},{8,11},{9,8},{10,9... | collective-permute-start | bytes 1769480 | tf_op jit(solution)/shard_map/ppermute | solution.py:570
  275.0 33.3 %collective-permute-start.7 = (bf16[2,128,1152]{2,1,0:T(8,128)(2,1)}, bf16[2,128,1152]{2,1,0:T(8,128)(2,1)S(1)}, u32[]{:S(2)}, u32[]{:S(2)}) collective-permute-start(bf16[2,128,1152]{2,1,0:T(8,128)(2,1)} %get-tuple-element.103), channel_id=1, source_target_pairs={{0,2},{1,3},{2,0},{3,1},{4,6},{5,7},{6,4},{7,5},{8,10},{9,11},{10,... | collective-permute-start | bytes 1769480 | tf_op jit(solution)/shard_map/ppermute | solution.py:570
  277.2 23.0 %collective-permute-start.10 = (bf16[128,1088]{1,0:T(8,128)(2,1)S(1)}, bf16[128,1088]{1,0:T(8,128)(2,1)S(1)}, u32[]{:S(2)}, u32[]{:S(2)}) collective-permute-start(bf16[128,1088]{1,0:T(8,128)(2,1)S(1)} %broadcast_select_fusion.refs_8_), channel_id=1, source_target_pairs={{0,2},{1,3},{2,0},{3,1},{4,6},{5,7},{6,4},{7,5},{8,10},{9,11},{10,... | collective-permute-start | bytes 835592 | tf_op jit(solution)/shard_map/ppermute | solution.py:570
  279.7 22.3 %collective-permute-start.9 = (bf16[128,1088]{1,0:T(8,128)(2,1)S(1)}, bf16[128,1088]{1,0:T(8,128)(2,1)S(1)}, u32[]{:S(2)}, u32[]{:S(2)}) collective-permute-start(bf16[128,1088]{1,0:T(8,128)(2,1)S(1)} %broadcast_select_fusion.refs_8_), channel_id=1, source_target_pairs={{0,3},{1,0},{2,1},{3,2},{4,7},{5,4},{6,5},{7,6},{8,11},{9,8},{10,9... | collective-permute-start | bytes 835592 | tf_op jit(solution)/shard_map/ppermute | solution.py:570
  322.1 23.1 %collective-permute-start.15 = (bf16[4,72,1536]{2,1,0:T(8,128)(2,1)}, bf16[4,72,1536]{2,1,0:T(8,128)(2,1)S(1)}, u32[]{:S(2)}, u32[]{:S(2)}) collective-permute-start(bf16[4,72,1536]{2,1,0:T(8,128)(2,1)} %get-tuple-element.112), channel_id=1, source_target_pairs={{0,4},{4,8},{8,12},{12,0},{1,5},{5,9},{9,13},{13,1},{2,6},{6,10},{... | collective-permute-start | bytes 2654216 | tf_op jit(solution)/shard_map/ppermute | solution.py:570
  323.7 34.0 %collective-permute-start.11 = (bf16[4,72,1920]{2,1,0:T(8,128)(2,1)}, bf16[4,72,1920]{2,1,0:T(8,128)(2,1)S(1)}, u32[]{:S(2)}, u32[]{:S(2)}) collective-permute-start(bf16[4,72,1920]{2,1,0:T(8,128)(2,1)} %get-tuple-element.106), channel_id=1, source_target_pairs={{0,32},{16,48},{32,0},{48,16},{1,33},{17,49},{33,1},{49,17},{2,34}... | collective-permute-start | bytes 3317768 | tf_op jit(solution)/shard_map/ppermute | solution.py:570
  326.7 41.0 %collective-permute-start.12 = (bf16[4,72,1920]{2,1,0:T(8,128)(2,1)}, bf16[4,72,1920]{2,1,0:T(8,128)(2,1)S(1)}, u32[]{:S(2)}, u32[]{:S(2)}) collective-permute-start(bf16[4,72,1920]{2,1,0:T(8,128)(2,1)} %get-tuple-element.107), channel_id=1, source_target_pairs={{0,16},{16,32},{32,48},{48,0},{1,17},{17,33},{33,49},{49,1},{2,18}... | collective-permute-start | bytes 3317768 | tf_op jit(solution)/shard_map/ppermute | solution.py:570
  327.3 40.5 %collective-permute-start.13 = (bf16[4,72,1920]{2,1,0:T(8,128)(2,1)}, bf16[4,72,1920]{2,1,0:T(8,128)(2,1)S(1)}, u32[]{:S(2)}, u32[]{:S(2)}) collective-permute-start(bf16[4,72,1920]{2,1,0:T(8,128)(2,1)} %get-tuple-element.108), channel_id=1, source_target_pairs={{0,48},{16,0},{32,16},{48,32},{1,49},{17,1},{33,17},{49,33},{2,50}... | collective-permute-start | bytes 3317768 | tf_op jit(solution)/shard_map/ppermute | solution.py:570
  330.0 27.8 %collective-permute-start.14 = (bf16[4,72,1536]{2,1,0:T(8,128)(2,1)}, bf16[4,72,1536]{2,1,0:T(8,128)(2,1)S(1)}, u32[]{:S(2)}, u32[]{:S(2)}) collective-permute-start(bf16[4,72,1536]{2,1,0:T(8,128)(2,1)} %get-tuple-element.110), channel_id=1, source_target_pairs={{0,8},{4,12},{8,0},{12,4},{1,9},{5,13},{9,1},{13,5},{2,10},{6,14},... | collective-permute-start | bytes 2654216 | tf_op jit(solution)/shard_map/ppermute | solution.py:570
  345.2 22.5 %collective-permute-start.16 = (bf16[4,72,1536]{2,1,0:T(8,128)(2,1)}, bf16[4,72,1536]{2,1,0:T(8,128)(2,1)S(1)}, u32[]{:S(2)}, u32[]{:S(2)}) collective-permute-start(bf16[4,72,1536]{2,1,0:T(8,128)(2,1)} %get-tuple-element.114), channel_id=1, source_target_pairs={{0,12},{4,0},{8,4},{12,8},{1,13},{5,1},{9,5},{13,9},{2,14},{6,2},{... | collective-permute-start | bytes 2654216 | tf_op jit(solution)/shard_map/ppermute | solution.py:570
  374.4 8.8 %collective-permute-start.20 = (bf16[72,1536]{1,0:T(8,128)(2,1)}, bf16[72,1536]{1,0:T(8,128)(2,1)S(1)}, u32[]{:S(2)}, u32[]{:S(2)}) collective-permute-start(bf16[72,1536]{1,0:T(8,128)(2,1)} %get-tuple-element.120), channel_id=1, source_target_pairs={{0,16},{16,32},{32,48},{48,0},{1,17},{17,33},{33,49},{49,1},{2,18}... | collective-permute-start | bytes 663560 | tf_op jit(solution)/shard_map/ppermute | solution.py:570
  375.9 15.5 %collective-permute-start.17 = (bf16[72,1920]{1,0:T(8,128)(2,1)}, bf16[72,1920]{1,0:T(8,128)(2,1)S(1)}, u32[]{:S(2)}, u32[]{:S(2)}) collective-permute-start(bf16[72,1920]{1,0:T(8,128)(2,1)} %get-tuple-element.116), channel_id=1, source_target_pairs={{0,4},{4,8},{8,12},{12,0},{1,5},{5,9},{9,13},{13,1},{2,6},{6,10},{... | collective-permute-start | bytes 829448 | tf_op jit(solution)/shard_map/ppermute | solution.py:570
  377.4 14.0 %collective-permute-start.18 = (bf16[72,1920]{1,0:T(8,128)(2,1)}, bf16[72,1920]{1,0:T(8,128)(2,1)S(1)}, u32[]{:S(2)}, u32[]{:S(2)}) collective-permute-start(bf16[72,1920]{1,0:T(8,128)(2,1)} %get-tuple-element.117), channel_id=1, source_target_pairs={{0,12},{4,0},{8,4},{12,8},{1,13},{5,1},{9,5},{13,9},{2,14},{6,2},{... | collective-permute-start | bytes 829448 | tf_op jit(solution)/shard_map/ppermute | solution.py:570
  379.1 12.3 %collective-permute-start.19 = (bf16[72,1920]{1,0:T(8,128)(2,1)}, bf16[72,1920]{1,0:T(8,128)(2,1)S(1)}, u32[]{:S(2)}, u32[]{:S(2)}) collective-permute-start(bf16[72,1920]{1,0:T(8,128)(2,1)} %get-tuple-element.118), channel_id=1, source_target_pairs={{0,8},{4,12},{8,0},{12,4},{1,9},{5,13},{9,1},{13,5},{2,10},{6,14},... | collective-permute-start | bytes 829448 | tf_op jit(solution)/shard_map/ppermute | solution.py:570
  380.7 10.6 %collective-permute-start.21 = (bf16[72,1536]{1,0:T(8,128)(2,1)}, bf16[72,1536]{1,0:T(8,128)(2,1)S(1)}, u32[]{:S(2)}, u32[]{:S(2)}) collective-permute-start(bf16[72,1536]{1,0:T(8,128)(2,1)} %get-tuple-element.121), channel_id=1, source_target_pairs={{0,48},{16,0},{32,16},{48,32},{1,49},{17,1},{33,17},{49,33},{2,50}... | collective-permute-start | bytes 663560 | tf_op jit(solution)/shard_map/ppermute | solution.py:570
  395.2 9.4 %collective-permute-start.23 = (bf16[24,3456]{1,0:T(8,128)(2,1)}, bf16[24,3456]{1,0:T(8,128)(2,1)S(1)}, u32[]{:S(2)}, u32[]{:S(2)}) collective-permute-start(bf16[24,3456]{1,0:T(8,128)(2,1)} %get-tuple-element.124), channel_id=1, source_target_pairs={{0,1},{1,2},{2,3},{3,0},{4,5},{5,6},{6,7},{7,4},{8,9},{9,10},{10,1... | collective-permute-start | bytes 497672 | tf_op jit(solution)/shard_map/ppermute | solution.py:570
  395.2 9.4 %collective-permute-start.24 = (bf16[24,3456]{1,0:T(8,128)(2,1)}, bf16[24,3456]{1,0:T(8,128)(2,1)S(1)}, u32[]{:S(2)}, u32[]{:S(2)}) collective-permute-start(bf16[24,3456]{1,0:T(8,128)(2,1)} %get-tuple-element.125), channel_id=1, source_target_pairs={{0,2},{1,3},{2,0},{3,1},{4,6},{5,7},{6,4},{7,5},{8,10},{9,11},{10,... | collective-permute-start | bytes 497672 | tf_op jit(solution)/shard_map/ppermute | solution.py:570
  396.7 8.7 %collective-permute-start.25 = (bf16[24,3456]{1,0:T(8,128)(2,1)}, bf16[24,3456]{1,0:T(8,128)(2,1)S(1)}, u32[]{:S(2)}, u32[]{:S(2)}) collective-permute-start(bf16[24,3456]{1,0:T(8,128)(2,1)} %get-tuple-element.126), channel_id=1, source_target_pairs={{0,3},{1,0},{2,1},{3,2},{4,7},{5,4},{6,5},{7,6},{8,11},{9,8},{10,9... | collective-permute-start | bytes 497672 | tf_op jit(solution)/shard_map/ppermute | solution.py:570
  (41 other events, 330.8 us)
Sparse Core Ops, SparseCore 0:
  16.9 151.5 all-gather.1
where the time goes:
time: 430 us; the launch traced here: 421 us
  waiting for transfers between devices  246 us (57%)
  Pallas kernels  95.2 us (22%)
  starting transfers between devices  40.8 us (9%)
  local copies, waits for them, and re-layouts  15.2 us (4%)
  between operations  15.1 us (4%)
  matrix products  5.57 us (1%)
    all_gather x1, waiting for transfers between devices, body(): whole = lax.all_gather(sent, ('x', 'y', 'z'), axis=0, tiled=True)  148 us
    ppermute x24, waiting for transfers between devices, ring(): return lax.ppermute(v, axis, [(i, (i + d) % 4) for i in range(4)])  71.1 us
    pallas_call x3, Pallas kernels, layer_call(): pl.pallas_call(kernel, in_specs=[pl.BlockSpec(memory_space=pltpu.SMEM)] +...  58.2 us
    ppermute x24, starting transfers between devices, ring(): return lax.ppermute(v, axis, [(i, (i + d) % 4) for i in range(4)])  38.2 us
    pallas_call x5, Pallas kernels, local_call(): pl.pallas_call(kernel, in_specs=[pl.BlockSpec(memory_space=pltpu.SMEM)] +...  29.6 us
    ppermute x1, waiting for transfers between devices, body(): coming = lax.ppermute(top['dx'], 'section', [(1, 0)])  26.6 us
  transfers between devices with their start and end apart: 27, of which 13 were waited for; matrix products, arithmetic and copies ran while one was open for 2% of the time, Pallas kernels for 1%

commit v1 on v0

--- a/solution.py
+++ b/solution.py
@@ -31,6 +31,7 @@
 GELU_A = 0.044715
 BF = jnp.bfloat16
 F32 = jnp.float32
+WINDOW = 4
 VMEM_BYTES = 58 * 1024 * 1024
 
 
@@ -124,11 +125,20 @@
 
 
 class Weights:
-    def __init__(self, whole, tails, buf, sems):
-        self.whole, self.tails, self.buf, self.sems = whole, tails, buf, sems
-
-    def copies(self, b):
-        cols = pl.ds(b * PAD, PAD)
+    def __init__(self, whole, tails, buf, sems, kind):
+        self.whole, self.tails, self.buf, self.sems, self.kind = whole, tails, buf, sems, kind
+
+    def block(self, p):
+        if self.kind == "bwd":
+            pair = (p % 2 == 0) * DOWN + p // 2
+            rest = OUT * (p == 8) + (p - 1) * (p > 8)
+            return pair * (p < 8) + rest * (p >= 8)
+        q = p - 4
+        return (p < 4) * (QKV + p) + (p >= 4) * ((q % 2) * DOWN + q // 2)
+
+    def copies(self, p):
+        b = self.block(p)
+        cols = pl.ds(pl.multiple_of(b * PAD, 128), PAD)
         return (
             pltpu.make_async_copy(
                 self.whole.at[:, cols], self.buf.at[b, pl.ds(0, MAIN)], self.sems.at[b, 0]
@@ -138,14 +148,25 @@
             ),
         )
 
-    def start(self, blocks):
-        for b in blocks:
-            for copy in self.copies(b):
-                copy.start()
-
-    def wait(self, b):
-        for copy in self.copies(b):
+    def start(self, p):
+        for copy in self.copies(p):
+            copy.start()
+
+    def begin(self):
+        for p in range(WINDOW):
+            self.start(p)
+
+    def wait(self, p):
+        for copy in self.copies(p):
             copy.wait()
+        if isinstance(p, int):
+            if p + WINDOW < BLOCKS:
+                self.start(p + WINDOW)
+        else:
+
+            @pl.when(p + WINDOW < BLOCKS)
+            def _():
+                self.start(p + WINDOW)
 
 
 def pair_masks():
@@ -168,19 +189,19 @@
     return halves
 
 
-def forward_part(w, wait, x_ref, place, pairs_ref, vecs, nat, order, r):
+def forward_part(w, send, x_ref, place, pairs_ref, vecs, nat, order, r):
     x = x_ref[...].astype(F32)
     normed, _ = norm_parts(x)
-    r["attn_in"][0] = (normed * vecs[0:1] + vecs[1:2]).astype(BF)
+    r["attn_in"][0, :, :D] = (normed * vecs[0:1] + vecs[1:2]).astype(BF)
 
     def project(i, carry):
-        if wait:
-            w.wait(QKV + i)
+        w.wait(i)
         shift = jnp.where(i == 0, nat[2:3], jnp.where(i == 2, nat[3:4], 0.0))
-        r["packed"][i] = (matmul(r["attn_in"][0], w.buf[QKV + i]) + shift).astype(BF)
+        r["packed"][i] = (matmul(r["attn_in"][0, :, :D], w.buf[QKV + i]) + shift).astype(BF)
         return carry
 
     lax.fori_loop(0, 3, project, 0)
+    send("packed")
     masks = pair_masks()
     allowed = pairs_ref[...] > 0
     for p in range(PAIRS):
@@ -190,46 +211,43 @@
         halves = soft_pair(r["packed"][0, :, cols], kk, allowed)
         soft = jnp.concatenate([h.astype(BF) for h in halves], axis=1)
         r["heads"][:, cols] = matmul(soft, vv).astype(BF)
-    r["attn_in"][1] = matmul(r["heads"][...], order[...]).astype(BF)
-    if wait:
-        w.wait(OUT)
-    branch = matmul(r["attn_in"][1], w.buf[OUT])[:, :D]
+    order.wait()
+    mixed = matmul(r["heads"][...], order.ref[...]).astype(BF)
+    r["attn_in"][1, :, :D] = mixed
+    w.wait(3)
+    branch = matmul(mixed, w.buf[OUT])[:, :D]
     middle = x + branch + vecs[4:5]
     r["middle"][...] = middle
+    send("middle")
     normed, _ = norm_parts(middle)
-    r["second"][...] = (normed * vecs[5:6] + vecs[6:7]).astype(BF)
+    r["second"][:, :D] = (normed * vecs[5:6] + vecs[6:7]).astype(BF)
+    r["acc"][...] = jnp.zeros((ROWS, PAD), F32)
+
+    def feed(a, carry):
+        w.wait(4 + 2 * a)
+        hidden = matmul(r["second"][:, :D], w.buf[UP + a])[:, :D] + vecs[pl.ds(8 + a, 1)]
+        r["hidden"][a] = hidden
+        bent = jnp.tanh(GELU_C * (hidden + GELU_A * (hidden * hidden * hidden)))
+        r["active"][a, :, :D] = (0.5 * hidden * (1.0 + bent)).astype(BF)
+        w.wait(5 + 2 * a)
+        r["acc"][...] += matmul(r["active"][a, :, :D], w.buf[DOWN + a])
+        return carry
+
+    lax.fori_loop(0, 4, feed, 0)
+    r["result"][...] = (r["middle"][...] + r["acc"][:, :D] + vecs[7:8]).astype(BF)
+    send("hidden")
+    send("early")
+
+
+def backward_part(w, wait, send, grad_ref, x_ref, place, pairs_ref, vecs, order, r):
+    grad = grad_ref[...]
+    dres = grad.astype(F32)
+    r["branch"][:, :D] = grad
     r["acc"][...] = jnp.zeros((ROWS, PAD), F32)
 
     def feed(a, carry):
         if wait:
-            w.wait(UP + a)
-        hidden = matmul(r["second"][...], w.buf[UP + a])[:, :D] + vecs[pl.ds(8 + a, 1)]
-        r["hidden"][a] = hidden
-        bent = jnp.tanh(GELU_C * (hidden + GELU_A * (hidden * hidden * hidden)))
-        r["active"][a] = (0.5 * hidden * (1.0 + bent)).astype(BF)
-        if wait:
-            w.wait(DOWN + a)
-        r["acc"][...] += matmul(r["active"][a], w.buf[DOWN + a])
-        return carry
-
-    lax.fori_loop(0, 4, feed, 0)
-    r["result"][...] = (r["middle"][...] + r["acc"][:, :D] + vecs[7:8]).astype(BF)
-    for d in range(4):
-        z = lax.rem(place[2] + d, 4)
-        out = r[f"early{d}"]
-        out[0, :, :D] = r["second"][...]
-        out[1, :, :D] = r["active"][z]
-        out[2, :, :D] = r["attn_in"][z // 3]
-
-
-def backward_part(w, wait, grad_ref, x_ref, place, pairs_ref, vecs, order, r):
-    grad = grad_ref[...]
-    dres = grad.astype(F32)
-    r["acc"][...] = jnp.zeros((ROWS, PAD), F32)
-
-    def feed(a, carry):
-        if wait:
-            w.wait(DOWN + a)
+            w.wait(2 * a)
         dactive = dot_t(grad_ref[...], w.buf[DOWN + a, :, :D])
         h = r["hidden"][a]
         square = h * h
@@ -238,14 +256,15 @@
             1.0 + (3 * GELU_A) * square
         )
         dhidden = (dactive * slope).astype(BF)
-        r["dhidden"][a] = dhidden
+        r["dhidden"][a, :, :D] = dhidden
         r["small"][pl.ds(8 + a, 1)] = col_sum(dhidden.astype(F32))
         if wait:
-            w.wait(UP + a)
+            w.wait(2 * a + 1)
         r["acc"][:, :D] += dot_t(dhidden, w.buf[UP + a, :, :D])
         return carry
 
     lax.fori_loop(0, 4, feed, 0)
+    send("late_first")
     dsecond = r["acc"][:, :D]
     normed, inverse = norm_parts(r["middle"][...])
     r["small"][5:6] = col_sum(dsecond * normed)
@@ -254,12 +273,14 @@
     dmiddle = dres + norm_back(dsecond, normed, inverse, vecs[5:6])
     r["middle"][...] = dmiddle
     dattn = dmiddle.astype(BF)
-    r["dpacked"][3] = dattn
+    r["dpacked"][3, :, :D] = dattn
     r["small"][4:5] = col_sum(dattn.astype(F32))
     if wait:
-        w.wait(OUT)
+        w.wait(8)
     dmixed = dot_t(dattn, w.buf[OUT, :, :D]).astype(BF)
-    r["heads"][...] = dot_t(dmixed, order[...]).astype(BF)
+    if wait:
+        order.wait()
+    r["heads"][...] = dot_t(dmixed, order.ref[...]).astype(BF)
     masks = pair_masks()
     allowed = pairs_ref[...] > 0
     for p in range(PAIRS):
@@ -286,15 +307,16 @@
         dv = dv[:ROWS] * masks[0] + dv[ROWS:] * masks[1]
         for i, v in enumerate((dq, dk, dv)):
             r["dpacked"][i, :, live] = v[:, :width].astype(BF)
-    sums = [col_sum(r["dpacked"][i].astype(F32)) for i in (0, 2)]
+    send("late_second")
+    sums = [col_sum(r["dpacked"][i, :, :D].astype(F32)) for i in (0, 2)]
     sums = jnp.concatenate(sums + [jnp.zeros((14, D), F32)], axis=0).astype(BF)
-    r["small"][2:4] = matmul(sums, order[:D])[:2]
+    r["small"][2:4] = matmul(sums, order.ref[:D])[:2]
     r["acc"][...] = jnp.zeros((ROWS, PAD), F32)
 
     def project(i, carry):
         if wait:
-            w.wait(QKV + i)
-        r["acc"][:, :D] += dot_t(r["dpacked"][i], w.buf[QKV + i, :, :D])
+            w.wait(9 + i)
+        r["acc"][:, :D] += dot_t(r["dpacked"][i, :, :D], w.buf[QKV + i, :, :D])
         return carry
 
     lax.fori_loop(0, 3, project, 0)
@@ -304,123 +326,150 @@
     r["small"][1:2] = col_sum(dentry)
     r["small"][12:16] = jnp.zeros((4, D), F32)
     r["dx"][...] = (r["middle"][...] + norm_back(dentry, normed, inverse, vecs[0:1])).astype(BF)
-    for d in range(4):
-        z = lax.rem(place[2] + d, 4)
-        r[f"late{d}"][0, :, :D] = r["dhidden"][z]
-        r[f"late{d}"][1, :, :D] = r["dpacked"][z]
 
 
 ROW = (ROWS, D)
+WIDEROW = (ROWS, PAD)
 KEPT = {
-    "packed": ((3, ROWS, PAD), BF),
+    "packed": ((3,) + WIDEROW, BF),
     "middle": (ROW, F32),
     "hidden": ((4,) + ROW, F32),
 }
-FWD_OUT = {"result": (ROW, BF), **{f"early{d}": ((3, ROWS, PAD), BF) for d in range(4)}}
-BWD_OUT = {
-    "dx": (ROW, BF),
-    **{f"late{d}": ((2, ROWS, PAD), BF) for d in range(4)},
-    "small": ((16, D), F32),
-}
+EARLY = {f"early{d}": ((3,) + WIDEROW, BF) for d in range(4)}
+LATE = {f"late{d}": ((3,) + WIDEROW, BF) for d in range(4)}
+RESULT = {"result": (ROW, BF)}
+GRADS = {"dx": (ROW, BF), "small": ((16, D), F32)}
 FWD_WORK = {
-    "attn_in": ((2,) + ROW, BF),
-    "second": (ROW, BF),
-    "active": ((4,) + ROW, BF),
+    "attn_in": ((2,) + WIDEROW, BF),
+    "second": (WIDEROW, BF),
+    "active": ((4,) + WIDEROW, BF),
 }
 BWD_WORK = {
-    "dhidden": ((4,) + ROW, BF),
-    "dpacked": ((4,) + ROW, BF),
+    "dhidden": ((4,) + WIDEROW, BF),
+    "dpacked": ((4,) + WIDEROW, BF),
+    "branch": (WIDEROW, BF),
 }
-WORK = {"heads": ((ROWS, PAD), BF), "acc": ((ROWS, PAD), F32)}
+WORK = {"heads": (WIDEROW, BF), "acc": (WIDEROW, F32)}
+
+
+class Fetched:
+    def __init__(self, source, ref, sem):
+        self.ref, self.copy = ref, pltpu.make_async_copy(source, ref, sem)
+
+    def start(self):
+        self.copy.start()
+
+    def wait(self):
+        self.copy.wait()
 
 
 def layer_call(kind, whole, tails, vecs, nat, pairs, order, place, x, grad=None, old=None):
-    outs = dict(FWD_OUT) if kind != "bwd" else {}
-    work = dict(WORK)
-    if kind == "fwd":
-        outs.update(KEPT)
-    else:
-        outs.update(BWD_OUT)
-        work.update(BWD_WORK)
+    near_out = {"fwd": RESULT, "both": {**RESULT, **GRADS}, "bwd": GRADS}[kind]
+    far_out = {"fwd": {**EARLY, **KEPT}, "both": {**EARLY, **LATE}, "bwd": LATE}[kind]
+    outs = {**near_out, **far_out}
+    work = {**WORK, **KEPT}
     if kind != "bwd":
         work.update(FWD_WORK)
-    else:
-        work["active"] = FWD_WORK["active"]
     if kind != "fwd":
-        work.update(KEPT)
-    passed = {"fwd": {}, "both": FWD_OUT, "bwd": BWD_OUT}[kind]
+        work.update(BWD_WORK)
+    passed = {"fwd": {}, "both": {**RESULT, **EARLY}, "bwd": {**GRADS, **LATE}}[kind]
     loaded = KEPT if kind == "bwd" else {}
-    far = [whole, tails] + [old[k] for k in (*passed, *loaded)]
-    near = [vecs, nat, pairs, order, x] + ([] if grad is None else [grad])
+    far = [whole, tails, order] + [old[k] for k in (*passed, *loaded)]
+    near = [vecs, nat, pairs, x] + ([] if grad is None else [grad])
     section = 1 if kind == "both" else 0
 
     def kernel(place_ref, *refs):
         far_refs, refs = refs[: len(far)], refs[len(far) :]
         near_refs, refs = refs[: len(near)], refs[len(near) :]
-        r = dict(zip(outs, refs))
+        out = dict(zip(outs, refs))
         refs = refs[len(outs) :]
-        r.update(zip(work, refs))
-        buf, sems, old_sems = refs[len(work) :]
-        w = Weights(far_refs[0], far_refs[1], buf, sems)
-        vecs_ref, nat_ref, pairs_ref, order_ref, x_ref = near_refs[:5]
-        old_refs = dict(zip((*passed, *loaded), far_refs[2:]))
-
-        def fetch(names):
-            return [
-                pltpu.make_async_copy(old_refs[k], r[k], old_sems.at[i])
-                for i, k in enumerate(names)
-            ]
+        r = {**dict(zip(work, refs)), **{k: out[k] for k in near_out}}
+        buf, order_buf, sems, old_sems, order_sem, out_sems = refs[len(work) :]
+        w = Weights(far_refs[0], far_refs[1], buf, sems, kind)
+        order_in = Fetched(far_refs[2], order_buf, order_sem)
+        vecs_ref, nat_ref, pairs_ref, x_ref = near_refs[:4]
+        old_refs = dict(zip((*passed, *loaded), far_refs[3:]))
+        sent = []
+
+        def send(name):
+            if name in KEPT:
+                moves = [(r[name], out[name])] if name in out else []
+            else:
+                moves = []
+                for d in range(4):
+                    z = lax.rem(place_ref[2] + d, 4)
+                    if name == "early":
+                        sources = (r["second"], r["active"].at[z], r["attn_in"].at[z // 3])
+                        moves += [(v, out[f"early{d}"].at[i]) for i, v in enumerate(sources)]
+                    elif name == "late_first":
+                        moves.append((r["branch"], out[f"late{d}"].at[0]))
+                        moves.append((r["dhidden"].at[z], out[f"late{d}"].at[1]))
+                    else:
+                        moves.append((r["dpacked"].at[z], out[f"late{d}"].at[2]))
+            for source, target in moves:
+                copy = pltpu.make_async_copy(source, target, out_sems.at[len(sent)])
+                copy.start()
+                sent.append(copy)
 
         @pl.when(place_ref[3] == section)
         def _():
-            if kind == "bwd":
-                w.start([DOWN])
-                copies = fetch(loaded)
-                for copy in copies:
-                    copy.start()
-                w.start([UP] + [b for a in range(1, 4) for b in (DOWN + a, UP + a)])
-                w.start([OUT, 8, 9, 10])
-                for copy in copies:
-                    copy.wait()
-            else:
-                w.start([8, 9, 10, OUT] + [b for a in range(4) for b in (UP + a, DOWN + a)])
-                forward_part(w, True, x_ref, place_ref, pairs_ref, vecs_ref, nat_ref, order_ref, r)
+            fetched = [
+                Fetched(old_refs[k], r[k], old_sems.at[i]) for i, k in enumerate(loaded)
+            ]
+            for copy in fetched:
+                copy.start()
+            w.begin()
+            order_in.start()
+            if kind != "bwd":
+                forward_part(
+                    w, send, x_ref, place_ref, pairs_ref, vecs_ref, nat_ref, order_in, r
+                )
+            for copy in fetched:
+                copy.wait()
             if kind != "fwd":
                 backward_part(
                     w,
                     kind == "bwd",
-                    near_refs[5],
+                    send,
+                    near_refs[4],
                     x_ref,
                     place_ref,
                     pairs_ref,
                     vecs_ref,
-                    order_ref,
+                    order_in,
                     r,
                 )
+            for copy in sent:
+                copy.wait()
 
         if passed:
 
             @pl.when(place_ref[3] != section)
             def _():
-                copies = fetch(passed)
+                copies = [
+                    pltpu.make_async_copy(old_refs[k], out[k], old_sems.at[i])
+                    for i, k in enumerate(passed)
+                ]
                 for copy in copies:
                     copy.start()
                 for copy in copies:
                     copy.wait()
 
     vm = pl.BlockSpec(memory_space=pltpu.VMEM)
+    hbm = pl.BlockSpec(memory_space=pl.ANY)
     results = pl.pallas_call(
         kernel,
-        in_specs=[pl.BlockSpec(memory_space=pltpu.SMEM)]
-        + [pl.BlockSpec(memory_space=pl.ANY)] * len(far)
-        + [vm] * len(near),
-        out_specs=[vm] * len(outs),
+        in_specs=[pl.BlockSpec(memory_space=pltpu.SMEM)] + [hbm] * len(far) + [vm] * len(near),
+        out_specs=[vm] * len(near_out) + [hbm] * len(far_out),
         out_shape=[jax.ShapeDtypeStruct(s, t) for s, t in outs.values()],
         scratch_shapes=[pltpu.VMEM(s, t) for s, t in work.values()]
         + [
             pltpu.VMEM((BLOCKS, D, PAD), BF),
+            pltpu.VMEM((PAD, D), BF),
             pltpu.SemaphoreType.DMA((BLOCKS, 2)),
-            pltpu.SemaphoreType.DMA((16,)),
+            pltpu.SemaphoreType.DMA((8,)),
+            pltpu.SemaphoreType.DMA,
+            pltpu.SemaphoreType.DMA((32,)),
         ],
         compiler_params=pltpu.CompilerParams(vmem_limit_bytes=VMEM_BYTES),
         cost_estimate=pl.CostEstimate(
@@ -438,13 +487,13 @@
 WIDE = (PAD + HALF, PAD + PAD - HALF)
 
 
-def local_call(kernel, name, place, ins, out_shapes, scratch=(), far=()):
+def local_call(kernel, name, place, ins, out_shapes, scratch=(), far=(), far_out=False):
     vm = pl.BlockSpec(memory_space=pltpu.VMEM)
     hbm = pl.BlockSpec(memory_space=pl.ANY)
     return pl.pallas_call(
         kernel,
         in_specs=[pl.BlockSpec(memory_space=pltpu.SMEM)] + [hbm] * len(far) + [vm] * len(ins),
-        out_specs=[vm] * len(out_shapes),
+        out_specs=[hbm if far_out else vm] * len(out_shapes),
         out_shape=[jax.ShapeDtypeStruct(s, t) for s, t in out_shapes],
         scratch_shapes=list(scratch),
         compiler_params=pltpu.CompilerParams(vmem_limit_bytes=VMEM_BYTES),
@@ -453,23 +502,22 @@
 
 
 def products_kernel(place, *refs):
-    given, small, outs = refs[:12], refs[12], refs[13:21]
-    first, second, early, late, branch, sems = refs[21:]
-    copies = []
-    for g, held in enumerate((early, late, branch)):
-        for d in range(4):
-            i = 4 * g + d
-            copies.append(pltpu.make_async_copy(given[i], held.at[d], sems.at[i]))
-    for i in (8, 9, 10, 11, 0, 1, 2, 3, 4, 5, 6, 7):
-        copies[i].start()
-
-    def wait(g):
-        for copy in copies[4 * g : 4 * g + 4]:
+    given, small, outs = refs[:8], refs[8], refs[9:17]
+    first, second, early, late, sems, out_sems = refs[17:]
+    copies = {}
+    for i, v in ((1, 0), (0, 1), (1, 1), (0, 0), (0, 2), (1, 2)):
+        held, source = ((early, given[:4]), (late, given[4:]))[i]
+        copies[i, v] = [
+            pltpu.make_async_copy(source[d].at[v], held.at[d, v], sems.at[i, v, d])
+            for d in range(4)
+        ]
+        for copy in copies[i, v]:
+            copy.start()
+
+    def rows_of(i, v):
+        for copy in copies[i, v]:
             copy.wait()
-
-    def rows_of(held, i=None):
-        parts = [held[d] if i is None else held[d, i, :, :D] for d in range(4)]
-        return jnp.concatenate(parts, axis=0)
+        return jnp.concatenate([(early, late)[i][d, v, :, :D] for d in range(4)], axis=0)
 
     gap = jnp.zeros((4 * ROWS, PAD - D), BF)
     slot = lax.broadcasted_iota(jnp.int32, (16, PAD), 1) - D
@@ -498,17 +546,30 @@
     def wide(v):
         return jnp.concatenate([v, gap], axis=1)
 
-    wait(2)
-    wait(0)
-    product(rows_of(early, 1), wide(rows_of(branch)), store_down)
-    wait(1)
-    product(rows_of(early, 0), wide(rows_of(late, 0)), store_up)
-    a = jnp.concatenate([rows_of(early, 2), small[...].astype(BF)], axis=0)
-    b = jnp.concatenate([wide(rows_of(late, 1)), unit], axis=0)
+    sent = []
+
+    def send(h, start, size):
+        held = (first, second)[h]
+        for d in range(4):
+            cols = pl.ds(start, size)
+            source = held.at[lax.rem(place[h] + d, 4), :, :, cols]
+            copy = pltpu.make_async_copy(
+                source, outs[4 * h + d].at[:, :, cols], out_sems.at[len(sent)]
+            )
+            copy.start()
+            sent.append(copy)
+
+    product(rows_of(0, 1), wide(rows_of(1, 0)), store_down)
+    send(1, 0, PAD)
+    product(rows_of(0, 0), wide(rows_of(1, 1)), store_up)
+    send(0, 0, PAD)
+    a = jnp.concatenate([rows_of(0, 2), small[...].astype(BF)], axis=0)
+    b = jnp.concatenate([wide(rows_of(1, 2)), unit], axis=0)
     product(a, b, store_attn)
-    for d in range(4):
-        outs[d][...] = first[lax.rem(place[0] + d, 4)]
-        outs[4 + d][...] = second[lax.rem(place[1] + d, 4)]
+    send(0, PAD, HALF)
+    send(1, PAD, PAD - HALF)
+    for copy in sent:
+        copy.wait()
 
 
 def total(parts):
@@ -516,11 +577,24 @@
 
 
 def first_sum_kernel(place, *refs):
-    for h, other in ((0, 1), (1, 0)):
-        parts, outs = refs[4 * h : 4 * h + 4], refs[8 + 4 * h : 12 + 4 * h]
-        for d in range(4):
+    given, outs, held, sems = refs[:8], refs[8:16], refs[16:18], refs[18]
+    copies = {}
+    for d in range(4):
+        for h, other in ((0, 1), (1, 0)):
             i = lax.rem(place[other] + d, 4)
-            outs[d][...] = total([p[i] for p in parts]).astype(BF)
+            copies[h, d] = [
+                pltpu.make_async_copy(
+                    given[4 * h + k].at[i], held[h].at[d, k], sems.at[h, d, k]
+                )
+                for k in range(4)
+            ]
+            for copy in copies[h, d]:
+                copy.start()
+    for d in range(4):
+        for h in range(2):
+            for copy in copies[h, d]:
+                copy.wait()
+            outs[4 * h + d][...] = total([held[h][d, k] for k in range(4)]).astype(BF)
 
 
 def second_sum_kernel(place, *refs):
@@ -537,8 +611,13 @@
 
 
 def final_kernel(place, *refs):
-    parts, (hid, order), outs, held = refs[:4], refs[4:6], refs[6:11], refs[11]
+    hid_in, order_in, parts, outs = refs[0], refs[1], refs[2:6], refs[6:11]
+    held, hid, order, sems = refs[11:]
     g_up, g_down, g_out, g_qkv, sums = outs
+    hid_copy = pltpu.make_async_copy(hid_in, hid, sems.at[0])
+    order_copy = pltpu.make_async_copy(order_in, order, sems.at[1])
+    hid_copy.start()
+    order_copy.start()
     for d in range(4):
         held[lax.rem(place[2] + 4 - d, 4)] = parts[d][...]
     up = []
@@ -546,6 +625,7 @@
         pieces = [held[a, :, j * 256 : (j + 1) * 256] for a in range(4)]
         pieces += [held[a, :, MAIN + j * 16 : MAIN + (j + 1) * 16] for a in range(4)]
         up.append(jnp.concatenate(pieces, axis=1))
+    hid_copy.wait()
     up = matmul(jnp.concatenate(up, axis=0), hid[...])
     up = jnp.concatenate([up[j * 24 : (j + 1) * 24] for j in range(4)], axis=1)
     for i in range(SHARD):
@@ -556,6 +636,7 @@
         for a in range(4)
     ]
     rows = [held[a, :, start : start + D] for a in range(4)] + [attn[3][:, :D]]
+    order_copy.wait()
     rows = dot_t(jnp.concatenate(rows, axis=0), order[:D])
     qkv = jnp.concatenate([v[:, :D].astype(F32) for v in attn[:3]], axis=1)
     for i in range(SHARD):
@@ -636,14 +717,14 @@
     top = call("both", x=arrived, grad=cot, old=first)
     coming = lax.ppermute(top["dx"], "section", [(1, 0)])
     early = [top["early0"]] + [ring(top[f"early{d}"], "z", d) for d in (1, 3, 2)]
-    coming, *early = lax.optimization_barrier((coming, *early))
-    branch = jnp.where(section == 0, coming, cot)
-    branches = [branch] + [ring(branch, "z", d) for d in (1, 3, 2)]
     kept = {k: first[k] for k in KEPT}
-    bwd = call("bwd", x=x0, grad=coming, old={**{k: top[k] for k in BWD_OUT}, **kept})
-    late = [bwd["late0"]] + [ring(bwd[f"late{d}"], "z", d) for d in (1, 3, 2)]
-
-    vmem = pltpu.VMEM
+    old = {**{k: top[k] for k in (*GRADS, *LATE)}, **kept}
+    bwd = call("bwd", x=x0, grad=coming, old=old)
+    sends = [bwd[f"late{d}"] for d in (1, 3, 2)]
+    early, sends = lax.optimization_barrier((early, sends))
+    late = [bwd["late0"]] + [ring(v, "z", d) for v, d in zip(sends, (1, 3, 2))]
+
+    vmem, sem = pltpu.VMEM, pltpu.SemaphoreType.DMA
     out = local_call(
         products_kernel,
         "products",
@@ -651,9 +732,10 @@
         [bwd["small"]],
         [((4, CHUNK, WIDE[h]), BF) for h in (0, 1) for _ in range(4)],
         [vmem((4, 4, CHUNK, WIDE[h]), BF) for h in (0, 1)]
-        + [vmem((4, k, ROWS, PAD), BF) for k in (3, 2)]
-        + [vmem((4,) + ROW, BF), pltpu.SemaphoreType.DMA((12,))],
-        far=[*early, *late, *branches],
+        + [vmem((4, 3) + WIDEROW, BF)] * 2
+        + [sem((2, 3, 4)), sem((16,))],
+        far=[*early, *late],
+        far_out=True,
     )
     got = [out[0]] + [ring(out[d], "x", d) for d in (2, 1, 3)]
     after = ring(out[5], "y", 1)
@@ -663,8 +745,10 @@
         first_sum_kernel,
         "first_sum",
         place,
-        got,
+        [],
         [((CHUNK, WIDE[h]), BF) for h in (0, 1) for _ in range(4)],
+        [vmem((4, 4, CHUNK, WIDE[h]), BF) for h in (0, 1)] + [sem((2, 4, 4))],
+        far=got,
     )
     got = []
     for h, axis in ((0, "y"), (1, "x")):
@@ -682,7 +766,7 @@
         final_kernel,
         "owners",
         place,
-        [*got, c["hid_t"], order],
+        got,
         [
             ((SHARD, 1, FF), F32),
             ((4 * SHARD, 1, D), F32),
@@ -690,7 +774,13 @@
             ((SHARD, 1, 3 * D), F32),
             ((SHARD, PAD - D), F32),
         ],
-        [vmem((4, 24, sum(WIDE)), BF)],
+        [
+            vmem((4, 24, sum(WIDE)), BF),
+            vmem((D, D), BF),
+            vmem((PAD, D), BF),
+            pltpu.SemaphoreType.DMA((2,)),
+        ],
+        far=[c["hid_t"], order],
     )
     acts, grads = local_call(
         restore_kernel, "restore", place, [order, top["result"], bwd["dx"]], [(ROW, BF)] * 2

time: 430 us -> 551 us (1.28)
  the two profiles are of different devices: /device:TPU:0 before, /device:TPU:1 now
where the time goes in v1:
time: 551 us; the launch traced here: 543 us
  waiting for transfers between devices  207 us (38%)
  Pallas kernels  180 us (33%)
  starting transfers between devices  117 us (21%)
  local copies, waits for them, and re-layouts  15.3 us (3%)
  between operations  14.8 us (3%)
  matrix products  5.57 us (1%)
    all_gather x1, waiting for transfers between devices, body(): whole = lax.all_gather(sent, ('x', 'y', 'z'), axis=0, tiled=True)  149 us
    pallas_call x3, Pallas kernels, layer_call(): pl.pallas_call(kernel, in_specs=[pl.BlockSpec(memory_space=pltpu.SMEM)] +...  145 us
    ppermute x1, starting transfers between devices, body(): coming = lax.ppermute(top['dx'], 'section', [(1, 0)])  82.2 us
    ppermute x21, waiting for transfers between devices, ring(): return lax.ppermute(v, axis, [(i, (i + d) % 4) for i in range(4)])  44.6 us
    ppermute x21, starting transfers between devices, ring(): return lax.ppermute(v, axis, [(i, (i + d) % 4) for i in range(4)])  33.4 us
    pallas_call x5, Pallas kernels, local_call(): pl.pallas_call(kernel, in_specs=[pl.BlockSpec(memory_space=pltpu.SMEM)] +...  28.3 us
    ppermute x1, waiting for transfers between devices, body(): arrived = lax.ppermute(first['result'], 'section', [(0, 1)])  13.9 us
  transfers between devices with their start and end apart: 24, of which 11 were waited for; matrix products, arithmetic and copies ran while one was open for 1% of the time, Pallas kernels for 21%

profile of v1, /device:TPU:1, one launch (start us, length us, event | category | flops | bytes accessed | tf_op | source)
XLA Modules:
  0.0 542.8 jit_solution(4772050991968682942)
XLA Ops:
  8.5 2.4 fusion
  20.3 148.9 %all-gather.2.cloned.1.call-done.whole.refs_0_ = bf16[1024,14720]{1,0:T(8,128)(2,1)} async-done(((bf16[16,14720]{1,0:T(8,128)(2,1)}), bf16[1024,14720]{1,0:T(8,128)(2,1)}) %all-gather.2.cloned.1.call-update) | async-done | bytes 30146576 | tf_op jit(solution)/shard_map/all_gather | solution.py:690
  169.3 7.4 %unpack.1 = (bf16[64,14336]{1,0:T(8,128)(2,1)}, f32[16,1088]{1,0:T(8,128)}, f32[16,1152]{1,0:T(8,128)}) custom-call(bf16[1024,14720]{1,0:T(8,128)(2,1)} %all-gather.2.cloned.1.call-done.whole.refs_0_, bf16[16,256]{1,0:T(8,128)(2,1)} %constant.51.clone.pick, bf16[64,1088]{1,0:T(8,128)(2,1)} %constant.52.clone.spread, bf16[256,1088]{1,0:T(8,128)(2,1)} %constant.53.clone.keep, ...), custom_call_target="tpu_custom_call" | custom-call | tf_op jit(solution)/shard_map/unpack/pallas_call | solution.py:112
  176.7 2.4 layer_fwd.1
  182.2 13.9 %collective-permute-done.refs_11_ = bf16[128,1088]{1,0:T(8,128)(2,1)S(1)} collective-permute-done((bf16[128,1088]{1,0:T(8,128)(2,1)}, bf16[128,1088]{1,0:T(8,128)(2,1)S(1)}, u32[]{:S(2)}, u32[]{:S(2)}) %collective-permute-start) | collective-permute-done | bytes 278560 | tf_op jit(solution)/shard_map/ppermute | solution.py:716
  196.8 31.4 %layer_both.1 = (bf16[128,1088]{1,0:T(8,128)(2,1)}, bf16[128,1088]{1,0:T(8,128)(2,1)}, f32[16,1088]{1,0:T(8,128)}, bf16[3,128,1152]{2,1,0:T(8,128)(2,1)}, bf16[3...) custom-call(s32[4]{0:T(128)} %pad_add_fusion.place_ref.place, ...), custom_call_target="tpu_custom_call" | custom-call | flops 12000000000 | bytes 30081024 | tf_op jit(solution)/shard_map/layer_both/pallas_call | solution.py:460
  228.2 82.2 %collective-permute-start.1 = (bf16[128,1088]{1,0:T(8,128)(2,1)}, bf16[128,1088]{1,0:T(8,128)(2,1)S(1)}, u32[]{:S(2)}, u32[]{:S(2)}) collective-permute-start(bf16[128,1088]{1,0:T(8,128)(2,1)} %get-tuple-element.81.refs_3_), channel_id=1, source_target_pairs={{64,0},{65,1},{66,2},{67,3},{68,4},{69,5},{70,6},{71,7},{72,8},{73... | collective-permute-start | bytes 835592 | tf_op jit(solution)/shard_map/ppermute | solution.py:718
  315.3 110.8 %layer_bwd.1 = (bf16[128,1088]{1,0:T(8,128)(2,1)}, f32[16,1088]{1,0:T(8,128)}, bf16[3,128,1152]{2,1,0:T(8,128)(2,1)}, bf16[3,128,1152]{2,1,0:T(8,128)(2,1)}, bf1...) custom-call(s32[4]{0:T(128)} %pad_add_fusion.place_ref.place, ...), custom_call_target="tpu_custom_call" | custom-call | flops 8000000000 | bytes 30081024 | tf_op jit(solution)/shard_map/layer_bwd/pallas_call | solution.py:460
  426.6 2.3 collective-permute-start.6
  429.9 19.2 %collective-permute-done.5.refs_5_ = bf16[3,128,1152]{2,1,0:T(8,128)(2,1)S(1)} collective-permute-done((bf16[3,128,1152]{2,1,0:T(8,128)(2,1)}, bf16[3,128,1152]{2,1,0:T(8,128)(2,1)S(1)}, u32[]{:S(2)}, u32[]{:S(2)}) %collective-permute-start.5) | collective-permute-done | bytes 884768 | tf_op jit(solution)/shard_map/ppermute | solution.py:651
  450.6 10.3 %products.1 = (bf16[4,72,1920]{2,1,0:T(8,128)(2,1)}, bf16[4,72,1920]{2,1,0:T(8,128)(2,1)}, bf16[4,72,1920]{2,1,0:T(8,128)(2,1)}, bf16[4,72,1920]{2,1,0:T(8,128)(...) custom-call(s32[4]{0:T(128)} %pad_add_fusion.place_ref.place, ...), custom_call_target="tpu_custom_call" | custom-call | tf_op jit(solution)/shard_map/products/pallas_call | solution.py:493
  462.1 2.2 collective-permute-start.8
  464.3 2.7 collective-permute-start.10
  469.1 5.2 collective-permute-done.12.refs_6_
  475.4 9.2 %collective-permute-done.11.refs_5_ = bf16[4,72,1536]{2,1,0:T(8,128)(2,1)S(1)} collective-permute-done((bf16[4,72,1536]{2,1,0:T(8,128)(2,1)}, bf16[4,72,1536]{2,1,0:T(8,128)(2,1)S(1)}, u32[]{:S(2)}, u32[]{:S(2)}) %collective-permute-start.11) | collective-permute-done | bytes 884768 | tf_op jit(solution)/shard_map/ppermute | solution.py:651
  484.6 5.3 collective-permute-done.9.refs_2_
  491.7 5.5 %first_sum.1 = (bf16[72,1920]{1,0:T(8,128)(2,1)}, bf16[72,1920]{1,0:T(8,128)(2,1)}, bf16[72,1920]{1,0:T(8,128)(2,1)}, bf16[72,1920]{1,0:T(8,128)(2,1)}, bf16[72,...) custom-call(s32[4]{0:T(128)} %pad_add_fusion.place_ref.place, ...), custom_call_target="tpu_custom_call" | custom-call | tf_op jit(solution)/shard_map/first_sum/pallas_call | solution.py:493
  497.1 6.4 %collective-permute-start.17 = (bf16[72,1536]{1,0:T(8,128)(2,1)}, bf16[72,1536]{1,0:T(8,128)(2,1)S(1)}, u32[]{:S(2)}, u32[]{:S(2)}) collective-permute-start(bf16[72,1536]{1,0:T(8,128)(2,1)} %get-tuple-element.124), channel_id=1, source_target_pairs={{0,16},{16,32},{32,48},{48,0},{1,17},{17,33},{33,49},{49,1},{2,18}... | collective-permute-start | bytes 663560 | tf_op jit(solution)/shard_map/ppermute | solution.py:651
  503.5 2.7 collective-permute-start.15
  508.3 2.3 collective-permute-start.19
  511.5 3.3 collective-permute-done.19.refs_7_
  515.8 2.8 second_sum.1
  522.0 4.3 restore.1
  527.4 5.5 %owners.1 = (f32[17,1,4352]{2,1,0:T(1,128)}, f32[68,1,1088]{2,1,0:T(1,128)}, f32[17,1,1088]{2,1,0:T(1,128)}, f32[17,1,3264]{2,1,0:T(1,128)}, f32[17,64]{1,0:T(8,128)}) custom-call(s32[4]{0:T(128)} %pad_add_fusion.place_ref.place, bf16[1088,1088]{1,0:T(8,128)(2,1)} %constant.58.clone.refs_0_, bf16[1152,1088]{1,0:T(8,128)(2,1)} %constant.49.clone.refs_2_.order.refs_1_, ...), custom_call_target="tpu_custom_call" | custom-call | tf_op jit(solution)/shard_map/owners/pallas_call | solution.py:493
  (149 shorter events, 39.6 us)
Async XLA Ops:
  7.2 162.1 %all-gather.2.cloned.1.call-start = ((), (), s32[]{:S(2)}) async-start(), calls=%async_computation | async-start | bytes 30617600 | tf_op jit(solution)/shard_map/all_gather | solution.py:690
  179.1 17.0 %collective-permute-start = (bf16[128,1088]{1,0:T(8,128)(2,1)}, bf16[128,1088]{1,0:T(8,128)(2,1)S(1)}, u32[]{:S(2)}, u32[]{:S(2)}) collective-permute-start(bf16[128,1088]{1,0:T(8,128)(2,1)} %get-tuple-element.75.refs_3_), channel_id=1, source_target_pairs={{0,64},{1,65},{2,66},{3,67},{4,68},{5,69},{6,70},{7,71},{8,72},{9,... | collective-permute-start | bytes 835592 | tf_op jit(solution)/shard_map/ppermute | solution.py:716
  228.2 86.4 %collective-permute-start.1 = (bf16[128,1088]{1,0:T(8,128)(2,1)}, bf16[128,1088]{1,0:T(8,128)(2,1)S(1)}, u32[]{:S(2)}, u32[]{:S(2)}) collective-permute-start(bf16[128,1088]{1,0:T(8,128)(2,1)} %get-tuple-element.81.refs_3_), channel_id=1, source_target_pairs={{64,0},{65,1},{66,2},{67,3},{68,4},{69,5},{70,6},{71,7},{72,8},{73... | collective-permute-start | bytes 835592 | tf_op jit(solution)/shard_map/ppermute | solution.py:718
  310.5 115.7 %collective-permute-start.2 = (bf16[3,128,1152]{2,1,0:T(8,128)(2,1)}, bf16[3,128,1152]{2,1,0:T(8,128)(2,1)S(1)}, u32[]{:S(2)}, u32[]{:S(2)}) collective-permute-start(bf16[3,128,1152]{2,1,0:T(8,128)(2,1)} %get-tuple-element.94), channel_id=1, source_target_pairs={{0,1},{1,2},{2,3},{3,0},{4,5},{5,6},{6,7},{7,4},{8,9},{9,10},{10,1... | collective-permute-start | bytes 2654216 | tf_op jit(solution)/shard_map/ppermute | solution.py:651
  311.1 115.1 %collective-permute-start.3 = (bf16[3,128,1152]{2,1,0:T(8,128)(2,1)}, bf16[3,128,1152]{2,1,0:T(8,128)(2,1)S(1)}, u32[]{:S(2)}, u32[]{:S(2)}) collective-permute-start(bf16[3,128,1152]{2,1,0:T(8,128)(2,1)} %get-tuple-element.95), channel_id=1, source_target_pairs={{0,3},{1,0},{2,1},{3,2},{4,7},{5,4},{6,5},{7,6},{8,11},{9,8},{10,9... | collective-permute-start | bytes 2654216 | tf_op jit(solution)/shard_map/ppermute | solution.py:651
  313.2 113.0 %collective-permute-start.4 = (bf16[3,128,1152]{2,1,0:T(8,128)(2,1)}, bf16[3,128,1152]{2,1,0:T(8,128)(2,1)S(1)}, u32[]{:S(2)}, u32[]{:S(2)}) collective-permute-start(bf16[3,128,1152]{2,1,0:T(8,128)(2,1)} %get-tuple-element.96), channel_id=1, source_target_pairs={{0,2},{1,3},{2,0},{3,1},{4,6},{5,7},{6,4},{7,5},{8,10},{9,11},{10,... | collective-permute-start | bytes 2654216 | tf_op jit(solution)/shard_map/ppermute | solution.py:651
  426.2 22.9 %collective-permute-start.5 = (bf16[3,128,1152]{2,1,0:T(8,128)(2,1)}, bf16[3,128,1152]{2,1,0:T(8,128)(2,1)S(1)}, u32[]{:S(2)}, u32[]{:S(2)}) collective-permute-start(bf16[3,128,1152]{2,1,0:T(8,128)(2,1)} %get-tuple-element.105), channel_id=1, source_target_pairs={{0,1},{1,2},{2,3},{3,0},{4,5},{5,6},{6,7},{7,4},{8,9},{9,10},{10,1... | collective-permute-start | bytes 2654216 | tf_op jit(solution)/shard_map/ppermute | solution.py:651
  426.6 22.4 %collective-permute-start.6 = (bf16[3,128,1152]{2,1,0:T(8,128)(2,1)}, bf16[3,128,1152]{2,1,0:T(8,128)(2,1)S(1)}, u32[]{:S(2)}, u32[]{:S(2)}) collective-permute-start(bf16[3,128,1152]{2,1,0:T(8,128)(2,1)} %get-tuple-element.106), channel_id=1, source_target_pairs={{0,3},{1,0},{2,1},{3,2},{4,7},{5,4},{6,5},{7,6},{8,11},{9,8},{10,9... | collective-permute-start | bytes 2654216 | tf_op jit(solution)/shard_map/ppermute | solution.py:651
  428.9 20.1 %collective-permute-start.7 = (bf16[3,128,1152]{2,1,0:T(8,128)(2,1)}, bf16[3,128,1152]{2,1,0:T(8,128)(2,1)S(1)}, u32[]{:S(2)}, u32[]{:S(2)}) collective-permute-start(bf16[3,128,1152]{2,1,0:T(8,128)(2,1)} %get-tuple-element.107), channel_id=1, source_target_pairs={{0,2},{1,3},{2,0},{3,1},{4,6},{5,7},{6,4},{7,5},{8,10},{9,11},{10,... | collective-permute-start | bytes 2654216 | tf_op jit(solution)/shard_map/ppermute | solution.py:651
  460.9 13.4 %collective-permute-start.12 = (bf16[4,72,1536]{2,1,0:T(8,128)(2,1)}, bf16[4,72,1536]{2,1,0:T(8,128)(2,1)S(1)}, u32[]{:S(2)}, u32[]{:S(2)}) collective-permute-start(bf16[4,72,1536]{2,1,0:T(8,128)(2,1)} %get-tuple-element.116), channel_id=1, source_target_pairs={{0,4},{4,8},{8,12},{12,0},{1,5},{5,9},{9,13},{13,1},{2,6},{6,10},{... | collective-permute-start | bytes 2654216 | tf_op jit(solution)/shard_map/ppermute | solution.py:651
  462.1 22.6 %collective-permute-start.8 = (bf16[4,72,1920]{2,1,0:T(8,128)(2,1)}, bf16[4,72,1920]{2,1,0:T(8,128)(2,1)S(1)}, u32[]{:S(2)}, u32[]{:S(2)}) collective-permute-start(bf16[4,72,1920]{2,1,0:T(8,128)(2,1)} %get-tuple-element.110), channel_id=1, source_target_pairs={{0,32},{16,48},{32,0},{48,16},{1,33},{17,49},{33,1},{49,17},{2,34}... | collective-permute-start | bytes 3317768 | tf_op jit(solution)/shard_map/ppermute | solution.py:651
  464.3 25.7 %collective-permute-start.9 = (bf16[4,72,1920]{2,1,0:T(8,128)(2,1)}, bf16[4,72,1920]{2,1,0:T(8,128)(2,1)S(1)}, u32[]{:S(2)}, u32[]{:S(2)}) collective-permute-start(bf16[4,72,1920]{2,1,0:T(8,128)(2,1)} %get-tuple-element.111), channel_id=1, source_target_pairs={{0,16},{16,32},{32,48},{48,0},{1,17},{17,33},{33,49},{49,1},{2,18}... | collective-permute-start | bytes 3317768 | tf_op jit(solution)/shard_map/ppermute | solution.py:651
  464.3 25.7 %collective-permute-start.10 = (bf16[4,72,1920]{2,1,0:T(8,128)(2,1)}, bf16[4,72,1920]{2,1,0:T(8,128)(2,1)S(1)}, u32[]{:S(2)}, u32[]{:S(2)}) collective-permute-start(bf16[4,72,1920]{2,1,0:T(8,128)(2,1)} %get-tuple-element.112), channel_id=1, source_target_pairs={{0,48},{16,0},{32,16},{48,32},{1,49},{17,1},{33,17},{49,33},{2,50}... | collective-permute-start | bytes 3317768 | tf_op jit(solution)/shard_map/ppermute | solution.py:651
  466.9 17.7 %collective-permute-start.11 = (bf16[4,72,1536]{2,1,0:T(8,128)(2,1)}, bf16[4,72,1536]{2,1,0:T(8,128)(2,1)S(1)}, u32[]{:S(2)}, u32[]{:S(2)}) collective-permute-start(bf16[4,72,1536]{2,1,0:T(8,128)(2,1)} %get-tuple-element.114), channel_id=1, source_target_pairs={{0,8},{4,12},{8,0},{12,4},{1,9},{5,13},{9,1},{13,5},{2,10},{6,14},... | collective-permute-start | bytes 2654216 | tf_op jit(solution)/shard_map/ppermute | solution.py:651
  474.2 16.0 %collective-permute-start.13 = (bf16[4,72,1536]{2,1,0:T(8,128)(2,1)}, bf16[4,72,1536]{2,1,0:T(8,128)(2,1)S(1)}, u32[]{:S(2)}, u32[]{:S(2)}) collective-permute-start(bf16[4,72,1536]{2,1,0:T(8,128)(2,1)} %get-tuple-element.118), channel_id=1, source_target_pairs={{0,12},{4,0},{8,4},{12,8},{1,13},{5,1},{9,5},{13,9},{2,14},{6,2},{... | collective-permute-start | bytes 2654216 | tf_op jit(solution)/shard_map/ppermute | solution.py:651
  497.1 11.2 %collective-permute-start.17 = (bf16[72,1536]{1,0:T(8,128)(2,1)}, bf16[72,1536]{1,0:T(8,128)(2,1)S(1)}, u32[]{:S(2)}, u32[]{:S(2)}) collective-permute-start(bf16[72,1536]{1,0:T(8,128)(2,1)} %get-tuple-element.124), channel_id=1, source_target_pairs={{0,16},{16,32},{32,48},{48,0},{1,17},{17,33},{33,49},{49,1},{2,18}... | collective-permute-start | bytes 663560 | tf_op jit(solution)/shard_map/ppermute | solution.py:651
  503.5 11.3 %collective-permute-start.14 = (bf16[72,1920]{1,0:T(8,128)(2,1)}, bf16[72,1920]{1,0:T(8,128)(2,1)S(1)}, u32[]{:S(2)}, u32[]{:S(2)}) collective-permute-start(bf16[72,1920]{1,0:T(8,128)(2,1)} %get-tuple-element.120), channel_id=1, source_target_pairs={{0,4},{4,8},{8,12},{12,0},{1,5},{5,9},{9,13},{13,1},{2,6},{6,10},{... | collective-permute-start | bytes 829448 | tf_op jit(solution)/shard_map/ppermute | solution.py:651
  503.5 11.3 %collective-permute-start.15 = (bf16[72,1920]{1,0:T(8,128)(2,1)}, bf16[72,1920]{1,0:T(8,128)(2,1)S(1)}, u32[]{:S(2)}, u32[]{:S(2)}) collective-permute-start(bf16[72,1920]{1,0:T(8,128)(2,1)} %get-tuple-element.121), channel_id=1, source_target_pairs={{0,12},{4,0},{8,4},{12,8},{1,13},{5,1},{9,5},{13,9},{2,14},{6,2},{... | collective-permute-start | bytes 829448 | tf_op jit(solution)/shard_map/ppermute | solution.py:651
  506.2 8.6 %collective-permute-start.16 = (bf16[72,1920]{1,0:T(8,128)(2,1)}, bf16[72,1920]{1,0:T(8,128)(2,1)S(1)}, u32[]{:S(2)}, u32[]{:S(2)}) collective-permute-start(bf16[72,1920]{1,0:T(8,128)(2,1)} %get-tuple-element.122), channel_id=1, source_target_pairs={{0,8},{4,12},{8,0},{12,4},{1,9},{5,13},{9,1},{13,5},{2,10},{6,14},... | collective-permute-start | bytes 829448 | tf_op jit(solution)/shard_map/ppermute | solution.py:651
  506.2 5.3 collective-permute-start.18
  508.3 6.5 %collective-permute-start.19 = (bf16[72,1536]{1,0:T(8,128)(2,1)}, bf16[72,1536]{1,0:T(8,128)(2,1)S(1)}, u32[]{:S(2)}, u32[]{:S(2)}) collective-permute-start(bf16[72,1536]{1,0:T(8,128)(2,1)} %get-tuple-element.126), channel_id=1, source_target_pairs={{0,32},{16,48},{32,0},{48,16},{1,33},{17,49},{33,1},{49,17},{2,34}... | collective-permute-start | bytes 663560 | tf_op jit(solution)/shard_map/ppermute | solution.py:651
  518.5 7.7 %collective-permute-start.20 = (bf16[24,3456]{1,0:T(8,128)(2,1)}, bf16[24,3456]{1,0:T(8,128)(2,1)S(1)}, u32[]{:S(2)}, u32[]{:S(2)}) collective-permute-start(bf16[24,3456]{1,0:T(8,128)(2,1)} %get-tuple-element.128), channel_id=1, source_target_pairs={{0,1},{1,2},{2,3},{3,0},{4,5},{5,6},{6,7},{7,4},{8,9},{9,10},{10,1... | collective-permute-start | bytes 497672 | tf_op jit(solution)/shard_map/ppermute | solution.py:651
  518.5 7.7 %collective-permute-start.21 = (bf16[24,3456]{1,0:T(8,128)(2,1)}, bf16[24,3456]{1,0:T(8,128)(2,1)S(1)}, u32[]{:S(2)}, u32[]{:S(2)}) collective-permute-start(bf16[24,3456]{1,0:T(8,128)(2,1)} %get-tuple-element.129), channel_id=1, source_target_pairs={{0,2},{1,3},{2,0},{3,1},{4,6},{5,7},{6,4},{7,5},{8,10},{9,11},{10,... | collective-permute-start | bytes 497672 | tf_op jit(solution)/shard_map/ppermute | solution.py:651
  520.0 6.7 %collective-permute-start.22 = (bf16[24,3456]{1,0:T(8,128)(2,1)}, bf16[24,3456]{1,0:T(8,128)(2,1)S(1)}, u32[]{:S(2)}, u32[]{:S(2)}) collective-permute-start(bf16[24,3456]{1,0:T(8,128)(2,1)} %get-tuple-element.130), channel_id=1, source_target_pairs={{0,3},{1,0},{2,1},{3,2},{4,7},{5,4},{6,5},{7,6},{8,11},{9,8},{10,9... | collective-permute-start | bytes 497672 | tf_op jit(solution)/shard_map/ppermute | solution.py:651
  (33 other events, 163.5 us)
Sparse Core Ops, SparseCore 0:
  16.9 152.3 all-gather.1

commit v2 on v1

--- a/solution.py
+++ b/solution.py
@@ -31,7 +31,7 @@
 GELU_A = 0.044715
 BF = jnp.bfloat16
 F32 = jnp.float32
-WINDOW = 4
+WINDOW = 3
 VMEM_BYTES = 58 * 1024 * 1024
 
 
@@ -242,7 +242,6 @@
 def backward_part(w, wait, send, grad_ref, x_ref, place, pairs_ref, vecs, order, r):
     grad = grad_ref[...]
     dres = grad.astype(F32)
-    r["branch"][:, :D] = grad
     r["acc"][...] = jnp.zeros((ROWS, PAD), F32)
 
     def feed(a, carry):
@@ -336,7 +335,7 @@
     "hidden": ((4,) + ROW, F32),
 }
 EARLY = {f"early{d}": ((3,) + WIDEROW, BF) for d in range(4)}
-LATE = {f"late{d}": ((3,) + WIDEROW, BF) for d in range(4)}
+LATE = {f"late{d}": ((2,) + WIDEROW, BF) for d in range(4)}
 RESULT = {"result": (ROW, BF)}
 GRADS = {"dx": (ROW, BF), "small": ((16, D), F32)}
 FWD_WORK = {
@@ -347,7 +346,6 @@
 BWD_WORK = {
     "dhidden": ((4,) + WIDEROW, BF),
     "dpacked": ((4,) + WIDEROW, BF),
-    "branch": (WIDEROW, BF),
 }
 WORK = {"heads": (WIDEROW, BF), "acc": (WIDEROW, F32)}
 
@@ -402,10 +400,9 @@
                         sources = (r["second"], r["active"].at[z], r["attn_in"].at[z // 3])
                         moves += [(v, out[f"early{d}"].at[i]) for i, v in enumerate(sources)]
                     elif name == "late_first":
-                        moves.append((r["branch"], out[f"late{d}"].at[0]))
-                        moves.append((r["dhidden"].at[z], out[f"late{d}"].at[1]))
+                        moves.append((r["dhidden"].at[z], out[f"late{d}"].at[0]))
                     else:
-                        moves.append((r["dpacked"].at[z], out[f"late{d}"].at[2]))
+                        moves.append((r["dpacked"].at[z], out[f"late{d}"].at[1]))
             for source, target in moves:
                 copy = pltpu.make_async_copy(source, target, out_sems.at[len(sent)])
                 copy.start()
@@ -446,14 +443,25 @@
 
             @pl.when(place_ref[3] != section)
             def _():
-                copies = [
-                    pltpu.make_async_copy(old_refs[k], out[k], old_sems.at[i])
-                    for i, k in enumerate(passed)
-                ]
-                for copy in copies:
-                    copy.start()
-                for copy in copies:
-                    copy.wait()
+                into, back = [], []
+                for i, k in enumerate(passed):
+                    if k in near_out:
+                        into.append(pltpu.make_async_copy(old_refs[k], out[k], old_sems.at[i]))
+                        continue
+                    for j in range(passed[k][0][0]):
+                        held = buf.at[i, pl.ds(j * ROWS, ROWS)]
+                        n = len(back)
+                        into.append(
+                            pltpu.make_async_copy(old_refs[k].at[j], held, out_sems.at[n])
+                        )
+                        back.append(
+                            pltpu.make_async_copy(held, out[k].at[j], out_sems.at[16 + n])
+                        )
+                for copies in (into, back):
+                    for copy in copies:
+                        copy.start()
+                    for copy in copies:
+                        copy.wait()
 
     vm = pl.BlockSpec(memory_space=pltpu.VMEM)
     hbm = pl.BlockSpec(memory_space=pl.ANY)
@@ -483,8 +491,8 @@
 
 
 CHUNK = 72
-HALF = 768
-WIDE = (PAD + HALF, PAD + PAD - HALF)
+BLOCK = ((4, CHUNK, PAD), BF)
+WIDE = (PAD, 2 * PAD)
 
 
 def local_call(kernel, name, place, ins, out_shapes, scratch=(), far=(), far_out=False):
@@ -501,74 +509,65 @@
     )(place, *far, *ins)
 
 
+def product(a, b, held, outs, sems, place, axis):
+    last = t_dot(a[:, MAIN:], b)
+    nothing = jnp.zeros((4, PAD), F32)
+    for x in range(4):
+        main = t_dot(a[:, x * 256 : (x + 1) * 256], b)
+        for y in range(4):
+            at = (x * 4 + y) * 4
+            rows = [main[y * 64 : (y + 1) * 64], last[at : at + 4], nothing]
+            i, j = (x, y) if axis == 0 else (y, x)
+            held[i, j] = jnp.concatenate(rows, axis=0).astype(BF)
+    copies = []
+    for d in range(4):
+        source = held.at[lax.rem(place[axis] + d, 4)]
+        copies.append(pltpu.make_async_copy(source, outs[d], sems.at[d]))
+        copies[-1].start()
+    return copies
+
+
+def load(sources, held, sems):
+    copies = []
+    for d in range(4):
+        copies.append(pltpu.make_async_copy(sources[d], held.at[d], sems.at[d]))
+        copies[-1].start()
+
+    def rows():
+        for copy in copies:
+            copy.wait()
+        return jnp.concatenate([held[d, :, :D] for d in range(4)], axis=0)
+
+    return rows
+
+
+def wide(v):
+    return jnp.concatenate([v, jnp.zeros((v.shape[0], PAD - D), v.dtype)], axis=1)
+
+
+def down_products_kernel(place, *refs):
+    early, branch, outs = refs[:4], refs[4:8], refs[8:12]
+    block, a_held, b_held, sems = refs[12:]
+    a = load([e.at[1] for e in early], a_held, sems.at[0])
+    b = load(branch, b_held, sems.at[1])
+    for copy in product(a(), wide(b()), block, outs, sems.at[2], place, 1):
+        copy.wait()
+
+
 def products_kernel(place, *refs):
-    given, small, outs = refs[:8], refs[8], refs[9:17]
-    first, second, early, late, sems, out_sems = refs[17:]
-    copies = {}
-    for i, v in ((1, 0), (0, 1), (1, 1), (0, 0), (0, 2), (1, 2)):
-        held, source = ((early, given[:4]), (late, given[4:]))[i]
-        copies[i, v] = [
-            pltpu.make_async_copy(source[d].at[v], held.at[d, v], sems.at[i, v, d])
-            for d in range(4)
-        ]
-        for copy in copies[i, v]:
-            copy.start()
-
-    def rows_of(i, v):
-        for copy in copies[i, v]:
-            copy.wait()
-        return jnp.concatenate([(early, late)[i][d, v, :, :D] for d in range(4)], axis=0)
-
-    gap = jnp.zeros((4 * ROWS, PAD - D), BF)
+    early, late, small, outs = refs[:4], refs[4:8], refs[8], refs[9:17]
+    up, attn, held, sems = refs[17:]
+    a_up = load([e.at[0] for e in early], held.at[0], sems.at[0])
+    b_up = load([v.at[0] for v in late], held.at[1], sems.at[1])
+    a_attn = load([e.at[2] for e in early], held.at[2], sems.at[2])
+    b_attn = load([v.at[1] for v in late], held.at[3], sems.at[3])
     slot = lax.broadcasted_iota(jnp.int32, (16, PAD), 1) - D
     unit = (slot == lax.broadcasted_iota(jnp.int32, (16, PAD), 0)).astype(F32).astype(BF)
-    nothing = jnp.zeros((4, PAD), F32)
-
-    def product(a, b, store):
-        last = t_dot(a[:, MAIN:], b)
-        for x in range(4):
-            main = t_dot(a[:, x * 256 : (x + 1) * 256], b)
-            for y in range(4):
-                at = (x * 4 + y) * 4
-                rows = [main[y * 64 : (y + 1) * 64], last[at : at + 4], nothing]
-                store(x, y, jnp.concatenate(rows, axis=0).astype(BF))
-
-    def store_up(x, y, v):
-        first[x, y, :, :PAD] = v
-
-    def store_down(x, y, v):
-        second[y, x, :, :PAD] = v
-
-    def store_attn(x, y, v):
-        first[x, y, :, PAD:] = v[:, :HALF]
-        second[y, x, :, PAD:] = v[:, HALF:]
-
-    def wide(v):
-        return jnp.concatenate([v, gap], axis=1)
-
-    sent = []
-
-    def send(h, start, size):
-        held = (first, second)[h]
-        for d in range(4):
-            cols = pl.ds(start, size)
-            source = held.at[lax.rem(place[h] + d, 4), :, :, cols]
-            copy = pltpu.make_async_copy(
-                source, outs[4 * h + d].at[:, :, cols], out_sems.at[len(sent)]
-            )
-            copy.start()
-            sent.append(copy)
-
-    product(rows_of(0, 1), wide(rows_of(1, 0)), store_down)
-    send(1, 0, PAD)
-    product(rows_of(0, 0), wide(rows_of(1, 1)), store_up)
-    send(0, 0, PAD)
-    a = jnp.concatenate([rows_of(0, 2), small[...].astype(BF)], axis=0)
-    b = jnp.concatenate([wide(rows_of(1, 2)), unit], axis=0)
-    product(a, b, store_attn)
-    send(0, PAD, HALF)
-    send(1, PAD, PAD - HALF)
-    for copy in sent:
+    copies = product(a_up(), wide(b_up()), up, outs[:4], sems.at[4], place, 0)
+    a = jnp.concatenate([a_attn(), small[...].astype(BF)], axis=0)
+    b = jnp.concatenate([wide(b_attn()), unit], axis=0)
+    copies += product(a, b, attn, outs[4:], sems.at[5], place, 1)
+    for copy in copies:
         copy.wait()
 
 
@@ -577,24 +576,23 @@
 
 
 def first_sum_kernel(place, *refs):
-    given, outs, held, sems = refs[:8], refs[8:16], refs[16:18], refs[18]
+    given, outs, held, sems = refs[:12], refs[12:20], refs[20], refs[21]
     copies = {}
     for d in range(4):
-        for h, other in ((0, 1), (1, 0)):
+        for g, other in ((1, 0), (0, 1), (2, 0)):
             i = lax.rem(place[other] + d, 4)
-            copies[h, d] = [
-                pltpu.make_async_copy(
-                    given[4 * h + k].at[i], held[h].at[d, k], sems.at[h, d, k]
-                )
+            copies[g, d] = [
+                pltpu.make_async_copy(given[4 * g + k].at[i], held.at[g, d, k], sems.at[g, d, k])
                 for k in range(4)
             ]
-            for copy in copies[h, d]:
+            for copy in copies[g, d]:
                 copy.start()
     for d in range(4):
-        for h in range(2):
-            for copy in copies[h, d]:
+        for g, (h, start) in ((1, (1, 0)), (0, (0, 0)), (2, (1, PAD))):
+            for copy in copies[g, d]:
                 copy.wait()
-            outs[4 * h + d][...] = total([held[h][d, k] for k in range(4)]).astype(BF)
+            summed = total([held[g, d, k] for k in range(4)]).astype(BF)
+            outs[4 * h + d][:, start : start + PAD] = summed
 
 
 def second_sum_kernel(place, *refs):
@@ -631,10 +629,7 @@
     for i in range(SHARD):
         g_up[i] = up[i : i + 1]
     start = WIDE[0]
-    attn = [
-        jnp.concatenate([held[a, :, PAD:start], held[a, :, start + PAD :]], axis=1)
-        for a in range(4)
-    ]
+    attn = [held[a, :, start + PAD :] for a in range(4)]
     rows = [held[a, :, start : start + D] for a in range(4)] + [attn[3][:, :D]]
     order_copy.wait()
     rows = dot_t(jnp.concatenate(rows, axis=0), order[:D])
@@ -717,38 +712,53 @@
     top = call("both", x=arrived, grad=cot, old=first)
     coming = lax.ppermute(top["dx"], "section", [(1, 0)])
     early = [top["early0"]] + [ring(top[f"early{d}"], "z", d) for d in (1, 3, 2)]
+    coming, early[1], early[2] = lax.optimization_barrier((coming, early[1], early[2]))
+    branch = jnp.where(section == 0, coming, cot)
+    branches = [branch] + [ring(branch, "z", d) for d in (1, 3, 2)]
     kept = {k: first[k] for k in KEPT}
     old = {**{k: top[k] for k in (*GRADS, *LATE)}, **kept}
     bwd = call("bwd", x=x0, grad=coming, old=old)
     sends = [bwd[f"late{d}"] for d in (1, 3, 2)]
-    early, sends = lax.optimization_barrier((early, sends))
+    early, branches, sends = lax.optimization_barrier((early, branches, sends))
     late = [bwd["late0"]] + [ring(v, "z", d) for v, d in zip(sends, (1, 3, 2))]
 
     vmem, sem = pltpu.VMEM, pltpu.SemaphoreType.DMA
+    down = local_call(
+        down_products_kernel,
+        "down_products",
+        place,
+        [],
+        [BLOCK] * 4,
+        [vmem((4, 4, CHUNK, PAD), BF), vmem((4,) + WIDEROW, BF), vmem((4,) + ROW, BF), sem((3, 4))],
+        far=[*early, *branches],
+        far_out=True,
+    )
+    late, down = lax.optimization_barrier((late, down))
+    small, down = lax.optimization_barrier((bwd["small"], down))
+    down = [down[0]] + [ring(down[d], "y", d) for d in (2, 1, 3)]
     out = local_call(
         products_kernel,
         "products",
         place,
-        [bwd["small"]],
-        [((4, CHUNK, WIDE[h]), BF) for h in (0, 1) for _ in range(4)],
-        [vmem((4, 4, CHUNK, WIDE[h]), BF) for h in (0, 1)]
-        + [vmem((4, 3) + WIDEROW, BF)] * 2
-        + [sem((2, 3, 4)), sem((16,))],
+        [small],
+        [BLOCK] * 8,
+        [vmem((4, 4, CHUNK, PAD), BF)] * 2 + [vmem((4, 4) + WIDEROW, BF), sem((6, 4))],
         far=[*early, *late],
         far_out=True,
     )
-    got = [out[0]] + [ring(out[d], "x", d) for d in (2, 1, 3)]
+    down, out = lax.optimization_barrier((down, out))
+    up = [out[0]] + [ring(out[d], "x", d) for d in (2, 1, 3)]
     after = ring(out[5], "y", 1)
     held, after = lax.optimization_barrier((out[7], after))
-    got += [out[4], ring(out[6], "y", 2), after, ring(held, "y", 3)]
+    attn = [out[4], ring(out[6], "y", 2), after, ring(held, "y", 3)]
     out = local_call(
         first_sum_kernel,
         "first_sum",
         place,
         [],
         [((CHUNK, WIDE[h]), BF) for h in (0, 1) for _ in range(4)],
-        [vmem((4, 4, CHUNK, WIDE[h]), BF) for h in (0, 1)] + [sem((2, 4, 4))],
-        far=got,
+        [vmem((3, 4, 4, CHUNK, PAD), BF), sem((3, 4, 4))],
+        far=[*up, *down, *attn],
     )
     got = []
     for h, axis in ((0, "y"), (1, "x")):

time: 551 us -> 428 us (0.78)
  the two profiles are of different devices: /device:TPU:1 before, /device:TPU:0 now
where the time goes in v2:
time: 428 us; the launch traced here: 419 us
  waiting for transfers between devices  244 us (57%)
  Pallas kernels  88.8 us (21%)
  starting transfers between devices  50.3 us (12%)
  between operations  15.2 us (4%)
  local copies, waits for them, and re-layouts  12.8 us (3%)
  matrix products  5.57 us (1%)
    all_gather x1, waiting for transfers between devices, body(): whole = lax.all_gather(sent, ('x', 'y', 'z'), axis=0, tiled=True)  148 us
    ppermute x27, waiting for transfers between devices, ring(): return lax.ppermute(v, axis, [(i, (i + d) % 4) for i in range(4)])  71.7 us
    pallas_call x3, Pallas kernels, layer_call(): pl.pallas_call(kernel, in_specs=[pl.BlockSpec(memory_space=pltpu.SMEM)] +...  49.2 us
    ppermute x27, starting transfers between devices, ring(): return lax.ppermute(v, axis, [(i, (i + d) % 4) for i in range(4)])  47.5 us
    pallas_call x6, Pallas kernels, local_call(): pl.pallas_call(kernel, in_specs=[pl.BlockSpec(memory_space=pltpu.SMEM)] +...  32.2 us
    ppermute x1, waiting for transfers between devices, body(): coming = lax.ppermute(top['dx'], 'section', [(1, 0)])  24.4 us
  transfers between devices with their start and end apart: 30, of which 14 were waited for; matrix products, arithmetic and copies ran while one was open for 1% of the time, Pallas kernels for 10%

profile of v2, /device:TPU:0, one launch (start us, length us, event | category | flops | bytes accessed | tf_op | source)
XLA Modules:
  0.0 419.4 jit_solution(8898673818776880492)
XLA Ops:
  20.3 148.2 %all-gather.2.cloned.1.call-done.whole.refs_0_ = bf16[1024,14720]{1,0:T(8,128)(2,1)} async-done(((bf16[16,14720]{1,0:T(8,128)(2,1)}), bf16[1024,14720]{1,0:T(8,128)(2,1)}) %all-gather.2.cloned.1.call-update) | async-done | bytes 30146576 | tf_op jit(solution)/shard_map/all_gather | solution.py:685
  168.6 7.4 %unpack.1 = (bf16[64,14336]{1,0:T(8,128)(2,1)}, f32[16,1088]{1,0:T(8,128)}, f32[16,1152]{1,0:T(8,128)}) custom-call(bf16[1024,14720]{1,0:T(8,128)(2,1)} %all-gather.2.cloned.1.call-done.whole.refs_0_, bf16[16,256]{1,0:T(8,128)(2,1)} %constant.51.clone.pick, bf16[64,1088]{1,0:T(8,128)(2,1)} %constant.52.clone.spread, bf16[256,1088]{1,0:T(8,128)(2,1)} %constant.53.clone.keep, ...), custom_call_target="tpu_custom_call" | custom-call | tf_op jit(solution)/shard_map/unpack/pallas_call | solution.py:112
  176.0 16.3 %layer_fwd.1 = (bf16[128,1088]{1,0:T(8,128)(2,1)}, bf16[3,128,1152]{2,1,0:T(8,128)(2,1)}, bf16[3,128,1152]{2,1,0:T(8,128)(2,1)}, bf16[3,128,1152]{2,1,0:T(8,128)...) custom-call(s32[4]{0:T(128)} %pad_add_fusion.place_ref.place, ...), custom_call_target="tpu_custom_call" | custom-call | flops 4000000000 | bytes 30081024 | tf_op jit(solution)/shard_map/layer_fwd/pallas_call | solution.py:468
  196.1 6.9 %layer_both.1 = (bf16[128,1088]{1,0:T(8,128)(2,1)}, bf16[128,1088]{1,0:T(8,128)(2,1)}, f32[16,1088]{1,0:T(8,128)}, bf16[3,128,1152]{2,1,0:T(8,128)(2,1)}, bf16[3...) custom-call(s32[4]{0:T(128)} %pad_add_fusion.place_ref.place, ...), custom_call_target="tpu_custom_call" | custom-call | flops 12000000000 | bytes 30081024 | tf_op jit(solution)/shard_map/layer_both/pallas_call | solution.py:468
  209.2 24.4 %collective-permute-done.1.refs_16_ = bf16[128,1088]{1,0:T(8,128)(2,1)S(1)} collective-permute-done((bf16[128,1088]{1,0:T(8,128)(2,1)}, bf16[128,1088]{1,0:T(8,128)(2,1)S(1)}, u32[]{:S(2)}, u32[]{:S(2)}) %collective-permute-start.1) | collective-permute-done | bytes 278560 | tf_op jit(solution)/shard_map/ppermute | solution.py:713
  237.0 25.9 %layer_bwd.1 = (bf16[128,1088]{1,0:T(8,128)(2,1)}, f32[16,1088]{1,0:T(8,128)}, bf16[2,128,1152]{2,1,0:T(8,128)(2,1)}, bf16[2,128,1152]{2,1,0:T(8,128)(2,1)}, bf1...) custom-call(s32[4]{0:T(128)} %pad_add_fusion.place_ref.place, ...), custom_call_target="tpu_custom_call" | custom-call | flops 8000000000 | bytes 30081024 | tf_op jit(solution)/shard_map/layer_bwd/pallas_call | solution.py:468
  263.8 2.6 collective-permute-start.9
  267.5 5.6 %down_products.1 = (bf16[4,72,1152]{2,1,0:T(8,128)(2,1)}, bf16[4,72,1152]{2,1,0:T(8,128)(2,1)}, bf16[4,72,1152]{2,1,0:T(8,128)(2,1)}, bf16[4,72,1152]{2,1,0:T(8,128)(2,1)}) custom-call(s32[4]{0:T(128)} %pad_add_fusion.place_ref.place, bf16[3,128,1152]{2,1,0:T(8,128)(2,1)} %get-tuple-element.144.refs_0_, bf16[3,128,1152]{2,1,0:T(8,128)(2,1)} %copy-done.2, ...), custom_call_target="tpu_custom_call" | custom-call | tf_op jit(solution)/shard_map/down_products/pallas_call | solution.py:501
  277.1 12.5 %collective-permute-done.10.refs_7_ = bf16[2,128,1152]{2,1,0:T(8,128)(2,1)S(1)} collective-permute-done((bf16[2,128,1152]{2,1,0:T(8,128)(2,1)}, bf16[2,128,1152]{2,1,0:T(8,128)(2,1)S(1)}, u32[]{:S(2)}, u32[]{:S(2)}) %collective-permute-start.10) | collective-permute-done | bytes 589856 | tf_op jit(solution)/shard_map/ppermute | solution.py:646
  289.6 2.9 collective-permute-start.11
  293.3 2.7 collective-permute-start.13
  296.0 8.2 %products.1 = (bf16[4,72,1152]{2,1,0:T(8,128)(2,1)}, bf16[4,72,1152]{2,1,0:T(8,128)(2,1)}, bf16[4,72,1152]{2,1,0:T(8,128)(2,1)}, bf16[4,72,1152]{2,1,0:T(8,128)(...) custom-call(s32[4]{0:T(128)} %pad_add_fusion.place_ref.place, ...), custom_call_target="tpu_custom_call" | custom-call | tf_op jit(solution)/shard_map/products/pallas_call | solution.py:501
  306.0 17.3 %collective-permute-done.12.refs_6_ = bf16[4,72,1152]{2,1,0:T(8,128)(2,1)S(1)} collective-permute-done((bf16[4,72,1152]{2,1,0:T(8,128)(2,1)}, bf16[4,72,1152]{2,1,0:T(8,128)(2,1)S(1)}, u32[]{:S(2)}, u32[]{:S(2)}) %collective-permute-start.12) | collective-permute-done | bytes 663584 | tf_op jit(solution)/shard_map/ppermute | solution.py:646
  326.9 2.7 collective-permute-start.16
  332.1 9.6 %collective-permute-done.18.refs_10_ = bf16[4,72,1152]{2,1,0:T(8,128)(2,1)S(1)} collective-permute-done((bf16[4,72,1152]{2,1,0:T(8,128)(2,1)}, bf16[4,72,1152]{2,1,0:T(8,128)(2,1)S(1)}, u32[]{:S(2)}, u32[]{:S(2)}) %collective-permute-start.18) | collective-permute-done | bytes 663584 | tf_op jit(solution)/shard_map/ppermute | solution.py:646
  344.2 13.1 %collective-permute-done.15.refs_2_ = bf16[4,72,1152]{2,1,0:T(8,128)(2,1)S(1)} collective-permute-done((bf16[4,72,1152]{2,1,0:T(8,128)(2,1)}, bf16[4,72,1152]{2,1,0:T(8,128)(2,1)S(1)}, u32[]{:S(2)}, u32[]{:S(2)}) %collective-permute-start.15) | collective-permute-done | bytes 663584 | tf_op jit(solution)/shard_map/ppermute | solution.py:646
  357.3 4.6 %collective-permute-done.19.refs_11_ = bf16[4,72,1152]{2,1,0:T(8,128)(2,1)S(1)} collective-permute-done((bf16[4,72,1152]{2,1,0:T(8,128)(2,1)}, bf16[4,72,1152]{2,1,0:T(8,128)(2,1)S(1)}, u32[]{:S(2)}, u32[]{:S(2)}) %collective-permute-start.19) | collective-permute-done | bytes 663584 | tf_op jit(solution)/shard_map/ppermute | solution.py:646
  362.8 5.7 %first_sum.1 = (bf16[72,1152]{1,0:T(8,128)(2,1)}, bf16[72,1152]{1,0:T(8,128)(2,1)}, bf16[72,1152]{1,0:T(8,128)(2,1)}, bf16[72,1152]{1,0:T(8,128)(2,1)}, bf16[72,...) custom-call(s32[4]{0:T(128)} %pad_add_fusion.place_ref.place, ...), custom_call_target="tpu_custom_call" | custom-call | tf_op jit(solution)/shard_map/first_sum/pallas_call | solution.py:501
  369.4 5.6 %collective-permute-start.23 = (bf16[72,2304]{1,0:T(8,128)(2,1)}, bf16[72,2304]{1,0:T(8,128)(2,1)S(1)}, u32[]{:S(2)}, u32[]{:S(2)}) collective-permute-start(bf16[72,2304]{1,0:T(8,128)(2,1)} %get-tuple-element.196), channel_id=1, source_target_pairs={{0,16},{16,32},{32,48},{48,0},{1,17},{17,33},{33,49},{49,1},{2,18}... | collective-permute-start | bytes 995336 | tf_op jit(solution)/shard_map/ppermute | solution.py:646
  378.6 3.2 collective-permute-start.21
  381.8 4.9 %collective-permute-done.21.refs_2_ = bf16[72,1152]{1,0:T(8,128)(2,1)S(1)} collective-permute-done((bf16[72,1152]{1,0:T(8,128)(2,1)}, bf16[72,1152]{1,0:T(8,128)(2,1)S(1)}, u32[]{:S(2)}, u32[]{:S(2)}) %collective-permute-start.21) | collective-permute-done | bytes 165920 | tf_op jit(solution)/shard_map/ppermute | solution.py:646
  389.8 2.9 second_sum.1
  397.3 4.3 %restore.1 = (bf16[128,1088]{1,0:T(8,128)(2,1)}, bf16[128,1088]{1,0:T(8,128)(2,1)}) custom-call(s32[4]{0:T(128)} %pad_add_fusion.place_ref.place, bf16[1152,1088]{1,0:T(8,128)(2,1)} %constant.49.clone.refs_2_.order.refs_1_, bf16[128,1088]{1,0:T(8,128)(2,1)} %get-tuple-element.116.result, bf16[128,1088]{1,0:T(8,128)(2,1)} %get-tuple-element.129.dx), custom_call_target="tpu_custom_call" | custom-call | tf_op jit(solution)/shard_map/restore/pallas_call | solution.py:501
  403.8 5.5 %owners.1 = (f32[17,1,4352]{2,1,0:T(1,128)}, f32[68,1,1088]{2,1,0:T(1,128)}, f32[17,1,1088]{2,1,0:T(1,128)}, f32[17,1,3264]{2,1,0:T(1,128)}, f32[17,64]{1,0:T(8,128)}) custom-call(s32[4]{0:T(128)} %pad_add_fusion.place_ref.place, bf16[1088,1088]{1,0:T(8,128)(2,1)} %constant.58.clone.refs_0_, bf16[1152,1088]{1,0:T(8,128)(2,1)} %constant.49.clone.refs_2_.order.refs_1_, ...), custom_call_target="tpu_custom_call" | custom-call | tf_op jit(solution)/shard_map/owners/pallas_call | solution.py:501
  (179 shorter events, 61.3 us)
Async XLA Ops:
  7.2 161.4 %all-gather.2.cloned.1.call-start = ((), (), s32[]{:S(2)}) async-start(), calls=%async_computation | async-start | bytes 30617600 | tf_op jit(solution)/shard_map/all_gather | solution.py:685
  203.1 30.5 %collective-permute-start.2 = (bf16[3,128,1152]{2,1,0:T(8,128)(2,1)}, bf16[3,128,1152]{2,1,0:T(8,128)(2,1)S(1)}, u32[]{:S(2)}, u32[]{:S(2)}) collective-permute-start(bf16[3,128,1152]{2,1,0:T(8,128)(2,1)} %get-tuple-element.126), channel_id=1, source_target_pairs={{0,1},{1,2},{2,3},{3,0},{4,5},{5,6},{6,7},{7,4},{8,9},{9,10},{10,1... | collective-permute-start | bytes 2654216 | tf_op jit(solution)/shard_map/ppermute | solution.py:646
  204.0 29.6 %collective-permute-start.3 = (bf16[3,128,1152]{2,1,0:T(8,128)(2,1)}, bf16[3,128,1152]{2,1,0:T(8,128)(2,1)S(1)}, u32[]{:S(2)}, u32[]{:S(2)}) collective-permute-start(bf16[3,128,1152]{2,1,0:T(8,128)(2,1)} %get-tuple-element.127), channel_id=1, source_target_pairs={{0,3},{1,0},{2,1},{3,2},{4,7},{5,4},{6,5},{7,6},{8,11},{9,8},{10,9... | collective-permute-start | bytes 2654216 | tf_op jit(solution)/shard_map/ppermute | solution.py:646
  206.4 27.2 %collective-permute-start.1 = (bf16[128,1088]{1,0:T(8,128)(2,1)}, bf16[128,1088]{1,0:T(8,128)(2,1)S(1)}, u32[]{:S(2)}, u32[]{:S(2)}) collective-permute-start(bf16[128,1088]{1,0:T(8,128)(2,1)} %get-tuple-element.117.refs_3_), channel_id=1, source_target_pairs={{64,0},{65,1},{66,2},{67,3},{68,4},{69,5},{70,6},{71,7},{72,8},{73... | collective-permute-start | bytes 835592 | tf_op jit(solution)/shard_map/ppermute | solution.py:713
  207.9 55.2 %collective-permute-start.4 = (bf16[3,128,1152]{2,1,0:T(8,128)(2,1)}, bf16[3,128,1152]{2,1,0:T(8,128)(2,1)S(1)}, u32[]{:S(2)}, u32[]{:S(2)}) collective-permute-start(bf16[3,128,1152]{2,1,0:T(8,128)(2,1)} %get-tuple-element.137), channel_id=1, source_target_pairs={{0,2},{1,3},{2,0},{3,1},{4,6},{5,7},{6,4},{7,5},{8,10},{9,11},{10,... | collective-permute-start | bytes 2654216 | tf_op jit(solution)/shard_map/ppermute | solution.py:646
  233.7 29.3 %collective-permute-start.7 = (bf16[128,1088]{1,0:T(8,128)(2,1)S(1)}, bf16[128,1088]{1,0:T(8,128)(2,1)S(1)}, u32[]{:S(2)}, u32[]{:S(2)}) collective-permute-start(bf16[128,1088]{1,0:T(8,128)(2,1)S(1)} %broadcast_select_fusion.refs_4_), channel_id=1, source_target_pairs={{0,2},{1,3},{2,0},{3,1},{4,6},{5,7},{6,4},{7,5},{8,10},{9,11},{10,... | collective-permute-start | bytes 835592 | tf_op jit(solution)/shard_map/ppermute | solution.py:646
  235.0 28.0 %collective-permute-start.6 = (bf16[128,1088]{1,0:T(8,128)(2,1)S(1)}, bf16[128,1088]{1,0:T(8,128)(2,1)S(1)}, u32[]{:S(2)}, u32[]{:S(2)}) collective-permute-start(bf16[128,1088]{1,0:T(8,128)(2,1)S(1)} %broadcast_select_fusion.refs_4_), channel_id=1, source_target_pairs={{0,3},{1,0},{2,1},{3,2},{4,7},{5,4},{6,5},{7,6},{8,11},{9,8},{10,9... | collective-permute-start | bytes 835592 | tf_op jit(solution)/shard_map/ppermute | solution.py:646
  236.1 27.0 %collective-permute-start.5 = (bf16[128,1088]{1,0:T(8,128)(2,1)S(1)}, bf16[128,1088]{1,0:T(8,128)(2,1)S(1)}, u32[]{:S(2)}, u32[]{:S(2)}) collective-permute-start(bf16[128,1088]{1,0:T(8,128)(2,1)S(1)} %broadcast_select_fusion.refs_4_), channel_id=1, source_target_pairs={{0,1},{1,2},{2,3},{3,0},{4,5},{5,6},{6,7},{7,4},{8,9},{9,10},{10,1... | collective-permute-start | bytes 835592 | tf_op jit(solution)/shard_map/ppermute | solution.py:646
  263.1 12.5 %collective-permute-start.8 = (bf16[2,128,1152]{2,1,0:T(8,128)(2,1)}, bf16[2,128,1152]{2,1,0:T(8,128)(2,1)S(1)}, u32[]{:S(2)}, u32[]{:S(2)}) collective-permute-start(bf16[2,128,1152]{2,1,0:T(8,128)(2,1)} %get-tuple-element.141), channel_id=1, source_target_pairs={{0,1},{1,2},{2,3},{3,0},{4,5},{5,6},{6,7},{7,4},{8,9},{9,10},{10,1... | collective-permute-start | bytes 1769480 | tf_op jit(solution)/shard_map/ppermute | solution.py:646
  263.8 13.3 %collective-permute-start.9 = (bf16[2,128,1152]{2,1,0:T(8,128)(2,1)}, bf16[2,128,1152]{2,1,0:T(8,128)(2,1)S(1)}, u32[]{:S(2)}, u32[]{:S(2)}) collective-permute-start(bf16[2,128,1152]{2,1,0:T(8,128)(2,1)} %get-tuple-element.142), channel_id=1, source_target_pairs={{0,3},{1,0},{2,1},{3,2},{4,7},{5,4},{6,5},{7,6},{8,11},{9,8},{10,9... | collective-permute-start | bytes 1769480 | tf_op jit(solution)/shard_map/ppermute | solution.py:646
  266.4 23.2 %collective-permute-start.10 = (bf16[2,128,1152]{2,1,0:T(8,128)(2,1)}, bf16[2,128,1152]{2,1,0:T(8,128)(2,1)S(1)}, u32[]{:S(2)}, u32[]{:S(2)}) collective-permute-start(bf16[2,128,1152]{2,1,0:T(8,128)(2,1)} %get-tuple-element.143), channel_id=1, source_target_pairs={{0,2},{1,3},{2,0},{3,1},{4,6},{5,7},{6,4},{7,5},{8,10},{9,11},{10,... | collective-permute-start | bytes 1769480 | tf_op jit(solution)/shard_map/ppermute | solution.py:646
  289.6 16.3 %collective-permute-start.11 = (bf16[4,72,1152]{2,1,0:T(8,128)(2,1)}, bf16[4,72,1152]{2,1,0:T(8,128)(2,1)S(1)}, u32[]{:S(2)}, u32[]{:S(2)}) collective-permute-start(bf16[4,72,1152]{2,1,0:T(8,128)(2,1)} %get-tuple-element.161), channel_id=1, source_target_pairs={{0,8},{4,12},{8,0},{12,4},{1,9},{5,13},{9,1},{13,5},{2,10},{6,14},... | collective-permute-start | bytes 1990664 | tf_op jit(solution)/shard_map/ppermute | solution.py:646
  292.5 30.7 %collective-permute-start.12 = (bf16[4,72,1152]{2,1,0:T(8,128)(2,1)}, bf16[4,72,1152]{2,1,0:T(8,128)(2,1)S(1)}, u32[]{:S(2)}, u32[]{:S(2)}) collective-permute-start(bf16[4,72,1152]{2,1,0:T(8,128)(2,1)} %get-tuple-element.162), channel_id=1, source_target_pairs={{0,4},{4,8},{8,12},{12,0},{1,5},{5,9},{9,13},{13,1},{2,6},{6,10},{... | collective-permute-start | bytes 1990664 | tf_op jit(solution)/shard_map/ppermute | solution.py:646
  293.3 29.9 %collective-permute-start.13 = (bf16[4,72,1152]{2,1,0:T(8,128)(2,1)}, bf16[4,72,1152]{2,1,0:T(8,128)(2,1)S(1)}, u32[]{:S(2)}, u32[]{:S(2)}) collective-permute-start(bf16[4,72,1152]{2,1,0:T(8,128)(2,1)} %get-tuple-element.163), channel_id=1, source_target_pairs={{0,12},{4,0},{8,4},{12,8},{1,13},{5,1},{9,5},{13,9},{2,14},{6,2},{... | collective-permute-start | bytes 1990664 | tf_op jit(solution)/shard_map/ppermute | solution.py:646
  323.2 18.4 %collective-permute-start.18 = (bf16[4,72,1152]{2,1,0:T(8,128)(2,1)}, bf16[4,72,1152]{2,1,0:T(8,128)(2,1)S(1)}, u32[]{:S(2)}, u32[]{:S(2)}) collective-permute-start(bf16[4,72,1152]{2,1,0:T(8,128)(2,1)} %get-tuple-element.188), channel_id=1, source_target_pairs={{0,4},{4,8},{8,12},{12,0},{1,5},{5,9},{9,13},{13,1},{2,6},{6,10},{... | collective-permute-start | bytes 1990664 | tf_op jit(solution)/shard_map/ppermute | solution.py:646
  324.6 19.5 %collective-permute-start.14 = (bf16[4,72,1152]{2,1,0:T(8,128)(2,1)}, bf16[4,72,1152]{2,1,0:T(8,128)(2,1)S(1)}, u32[]{:S(2)}, u32[]{:S(2)}) collective-permute-start(bf16[4,72,1152]{2,1,0:T(8,128)(2,1)} %get-tuple-element.178), channel_id=1, source_target_pairs={{0,32},{16,48},{32,0},{48,16},{1,33},{17,49},{33,1},{49,17},{2,34}... | collective-permute-start | bytes 1990664 | tf_op jit(solution)/shard_map/ppermute | solution.py:646
  326.4 30.9 %collective-permute-start.15 = (bf16[4,72,1152]{2,1,0:T(8,128)(2,1)}, bf16[4,72,1152]{2,1,0:T(8,128)(2,1)S(1)}, u32[]{:S(2)}, u32[]{:S(2)}) collective-permute-start(bf16[4,72,1152]{2,1,0:T(8,128)(2,1)} %get-tuple-element.179), channel_id=1, source_target_pairs={{0,16},{16,32},{32,48},{48,0},{1,17},{17,33},{33,49},{49,1},{2,18}... | collective-permute-start | bytes 1990664 | tf_op jit(solution)/shard_map/ppermute | solution.py:646
  326.9 30.3 %collective-permute-start.16 = (bf16[4,72,1152]{2,1,0:T(8,128)(2,1)}, bf16[4,72,1152]{2,1,0:T(8,128)(2,1)S(1)}, u32[]{:S(2)}, u32[]{:S(2)}) collective-permute-start(bf16[4,72,1152]{2,1,0:T(8,128)(2,1)} %get-tuple-element.180), channel_id=1, source_target_pairs={{0,48},{16,0},{32,16},{48,32},{1,49},{17,1},{33,17},{49,33},{2,50}... | collective-permute-start | bytes 1990664 | tf_op jit(solution)/shard_map/ppermute | solution.py:646
  329.6 27.7 %collective-permute-start.17 = (bf16[4,72,1152]{2,1,0:T(8,128)(2,1)}, bf16[4,72,1152]{2,1,0:T(8,128)(2,1)S(1)}, u32[]{:S(2)}, u32[]{:S(2)}) collective-permute-start(bf16[4,72,1152]{2,1,0:T(8,128)(2,1)} %get-tuple-element.186), channel_id=1, source_target_pairs={{0,8},{4,12},{8,0},{12,4},{1,9},{5,13},{9,1},{13,5},{2,10},{6,14},... | collective-permute-start | bytes 1990664 | tf_op jit(solution)/shard_map/ppermute | solution.py:646
  341.7 20.2 %collective-permute-start.19 = (bf16[4,72,1152]{2,1,0:T(8,128)(2,1)}, bf16[4,72,1152]{2,1,0:T(8,128)(2,1)S(1)}, u32[]{:S(2)}, u32[]{:S(2)}) collective-permute-start(bf16[4,72,1152]{2,1,0:T(8,128)(2,1)} %get-tuple-element.190), channel_id=1, source_target_pairs={{0,12},{4,0},{8,4},{12,8},{1,13},{5,1},{9,5},{13,9},{2,14},{6,2},{... | collective-permute-start | bytes 1990664 | tf_op jit(solution)/shard_map/ppermute | solution.py:646
  368.6 13.2 %collective-permute-start.20 = (bf16[72,1152]{1,0:T(8,128)(2,1)}, bf16[72,1152]{1,0:T(8,128)(2,1)S(1)}, u32[]{:S(2)}, u32[]{:S(2)}) collective-permute-start(bf16[72,1152]{1,0:T(8,128)(2,1)} %get-tuple-element.192), channel_id=1, source_target_pairs={{0,4},{4,8},{8,12},{12,0},{1,5},{5,9},{9,13},{13,1},{2,6},{6,10},{... | collective-permute-start | bytes 497672 | tf_op jit(solution)/shard_map/ppermute | solution.py:646
  369.4 19.4 %collective-permute-start.23 = (bf16[72,2304]{1,0:T(8,128)(2,1)}, bf16[72,2304]{1,0:T(8,128)(2,1)S(1)}, u32[]{:S(2)}, u32[]{:S(2)}) collective-permute-start(bf16[72,2304]{1,0:T(8,128)(2,1)} %get-tuple-element.196), channel_id=1, source_target_pairs={{0,16},{16,32},{32,48},{48,0},{1,17},{17,33},{33,49},{49,1},{2,18}... | collective-permute-start | bytes 995336 | tf_op jit(solution)/shard_map/ppermute | solution.py:646
  375.1 13.8 %collective-permute-start.24 = (bf16[72,2304]{1,0:T(8,128)(2,1)}, bf16[72,2304]{1,0:T(8,128)(2,1)S(1)}, u32[]{:S(2)}, u32[]{:S(2)}) collective-permute-start(bf16[72,2304]{1,0:T(8,128)(2,1)} %get-tuple-element.197), channel_id=1, source_target_pairs={{0,48},{16,0},{32,16},{48,32},{1,49},{17,1},{33,17},{49,33},{2,50}... | collective-permute-start | bytes 995336 | tf_op jit(solution)/shard_map/ppermute | solution.py:646
  376.4 12.5 %collective-permute-start.25 = (bf16[72,2304]{1,0:T(8,128)(2,1)}, bf16[72,2304]{1,0:T(8,128)(2,1)S(1)}, u32[]{:S(2)}, u32[]{:S(2)}) collective-permute-start(bf16[72,2304]{1,0:T(8,128)(2,1)} %get-tuple-element.198), channel_id=1, source_target_pairs={{0,32},{16,48},{32,0},{48,16},{1,33},{17,49},{33,1},{49,17},{2,34}... | collective-permute-start | bytes 995336 | tf_op jit(solution)/shard_map/ppermute | solution.py:646
  (47 other events, 494.4 us)
Sparse Core Ops, SparseCore 0:
  16.9 151.5 all-gather.1

commit v3 on v2

--- a/solution.py
+++ b/solution.py
@@ -94,34 +94,50 @@
     return jnp.sum(v, axis=0, keepdims=True)
 
 
-def unpack_kernel(whole, pick, spread, keep, spread_nat, keep_nat, turn, tails, vecs, nat, raw, sem):
-    copy = pltpu.make_async_copy(whole.at[:, pl.ds(TAIL0, TAILW)], raw, sem)
-    copy.start()
-    copy.wait()
+def unpack_kernel(whole, *refs):
+    given, (tails, vecs, nat), (raw, table, *held), sems = refs[:6], refs[6:9], refs[9:17], refs[17]
+    copies = [pltpu.make_async_copy(whole.at[:, pl.ds(TAIL0, TAILW)], raw, sems.at[0])]
+    for i, (source, target) in enumerate(zip(given, held)):
+        copies.append(pltpu.make_async_copy(source, target, sems.at[1 + i]))
+    for copy in copies:
+        copy.start()
+    turn, pick, spread, keep, spread_nat, keep_nat = held
+    copies[0].wait()
+    copies[1].wait()
     turned = matmul(turn[...], raw[...]).astype(BF)
     for j in range(16):
-        tails[:, j * TAILW : (j + 1) * TAILW] = turned[j * NDP : (j + 1) * NDP]
-    small = tails[:, TAIL0 : TAIL0 + SMALLS]
-    for out, s, k in ((vecs, spread, keep), (nat, spread_nat, keep_nat)):
-        wide = t_dot(small, s[...]) * k[...].astype(F32)
-        out[...] = matmul(pick[...], wide.astype(BF))
+        table[:, j * TAILW : (j + 1) * TAILW] = turned[j * NDP : (j + 1) * NDP]
+    out = pltpu.make_async_copy(table, tails, sems.at[7])
+    out.start()
+    for copy in copies[2:]:
+        copy.wait()
+    small = table[:, TAIL0 : TAIL0 + SMALLS]
+    for result, s, k in ((vecs, spread, keep), (nat, spread_nat, keep_nat)):
+        wide_rows = t_dot(small, s[...]) * k[...].astype(F32)
+        result[...] = matmul(pick[...], wide_rows.astype(BF))
+    out.wait()
 
 
 def unpack(whole, c):
     vm = pl.BlockSpec(memory_space=pltpu.VMEM)
+    hbm = pl.BlockSpec(memory_space=pl.ANY)
+    consts = [c[k] for k in ("turn", "pick", "spread", "keep", "spread_nat", "keep_nat")]
+    table = (NDP, 16 * TAILW)
     return pl.pallas_call(
         unpack_kernel,
-        in_specs=[pl.BlockSpec(memory_space=pl.ANY)] + [vm] * 6,
-        out_specs=[vm] * 3,
+        in_specs=[hbm] * 7,
+        out_specs=[hbm, vm, vm],
         out_shape=[
-            jax.ShapeDtypeStruct((NDP, 16 * TAILW), BF),
+            jax.ShapeDtypeStruct(table, BF),
             jax.ShapeDtypeStruct((16, D), F32),
             jax.ShapeDtypeStruct((16, PAD), F32),
         ],
-        scratch_shapes=[pltpu.VMEM((MAIN, TAILW), BF), pltpu.SemaphoreType.DMA],
+        scratch_shapes=[pltpu.VMEM((MAIN, TAILW), BF), pltpu.VMEM(table, BF)]
+        + [pltpu.VMEM(v.shape, BF) for v in consts]
+        + [pltpu.SemaphoreType.DMA((8,))],
         compiler_params=pltpu.CompilerParams(vmem_limit_bytes=VMEM_BYTES),
         name="unpack",
-    )(whole, c["pick"], c["spread"], c["keep"], c["spread_nat"], c["keep_nat"], c["turn"])
+    )(whole, *consts)
 
 
 class Weights:
@@ -491,8 +507,12 @@
 
 
 CHUNK = 72
-BLOCK = ((4, CHUNK, PAD), BF)
-WIDE = (PAD, 2 * PAD)
+PART = 384
+WIDE = (PAD + PART, PAD + PAD - PART)
+
+
+def block(width):
+    return ((4, CHUNK, width), BF)
 
 
 def local_call(kernel, name, place, ins, out_shapes, scratch=(), far=(), far_out=False):
@@ -509,7 +529,7 @@
     )(place, *far, *ins)
 
 
-def product(a, b, held, outs, sems, place, axis):
+def product(a, b, store):
     last = t_dot(a[:, MAIN:], b)
     nothing = jnp.zeros((4, PAD), F32)
     for x in range(4):
@@ -517,12 +537,16 @@
         for y in range(4):
             at = (x * 4 + y) * 4
             rows = [main[y * 64 : (y + 1) * 64], last[at : at + 4], nothing]
-            i, j = (x, y) if axis == 0 else (y, x)
-            held[i, j] = jnp.concatenate(rows, axis=0).astype(BF)
+            store(x, y, jnp.concatenate(rows, axis=0).astype(BF))
+
+
+def send_blocks(held, first, outs, sems, cols=None):
     copies = []
     for d in range(4):
-        source = held.at[lax.rem(place[axis] + d, 4)]
-        copies.append(pltpu.make_async_copy(source, outs[d], sems.at[d]))
+        source, target = held.at[lax.rem(first + d, 4)], outs[d]
+        if cols is not None:
+            source, target = source.at[:, :, cols], target.at[:, :, cols]
+        copies.append(pltpu.make_async_copy(source, target, sems.at[d]))
         copies[-1].start()
     return copies
 
@@ -547,26 +571,42 @@
 
 def down_products_kernel(place, *refs):
     early, branch, outs = refs[:4], refs[4:8], refs[8:12]
-    block, a_held, b_held, sems = refs[12:]
+    held, a_held, b_held, sems = refs[12:]
     a = load([e.at[1] for e in early], a_held, sems.at[0])
     b = load(branch, b_held, sems.at[1])
-    for copy in product(a(), wide(b()), block, outs, sems.at[2], place, 1):
+
+    def store(x, y, v):
+        held[y, x] = v
+
+    product(a(), wide(b()), store)
+    for copy in send_blocks(held, place[1], outs, sems.at[2]):
         copy.wait()
 
 
 def products_kernel(place, *refs):
     early, late, small, outs = refs[:4], refs[4:8], refs[8], refs[9:17]
-    up, attn, held, sems = refs[17:]
+    first, second, held, sems = refs[17:]
     a_up = load([e.at[0] for e in early], held.at[0], sems.at[0])
     b_up = load([v.at[0] for v in late], held.at[1], sems.at[1])
     a_attn = load([e.at[2] for e in early], held.at[2], sems.at[2])
     b_attn = load([v.at[1] for v in late], held.at[3], sems.at[3])
     slot = lax.broadcasted_iota(jnp.int32, (16, PAD), 1) - D
     unit = (slot == lax.broadcasted_iota(jnp.int32, (16, PAD), 0)).astype(F32).astype(BF)
-    copies = product(a_up(), wide(b_up()), up, outs[:4], sems.at[4], place, 0)
+
+    def store_up(x, y, v):
+        first[x, y, :, :PAD] = v
+
+    def store_attn(x, y, v):
+        first[x, y, :, PAD:] = v[:, :PART]
+        second[y, x] = v[:, PART:]
+
+    product(a_up(), wide(b_up()), store_up)
+    copies = send_blocks(first, place[0], outs[:4], sems.at[4], pl.ds(0, PAD))
     a = jnp.concatenate([a_attn(), small[...].astype(BF)], axis=0)
     b = jnp.concatenate([wide(b_attn()), unit], axis=0)
-    copies += product(a, b, attn, outs[4:], sems.at[5], place, 1)
+    product(a, b, store_attn)
+    copies += send_blocks(first, place[0], outs[:4], sems.at[5], pl.ds(PAD, PART))
+    copies += send_blocks(second, place[1], outs[4:], sems.at[6])
     for copy in copies:
         copy.wait()
 
@@ -576,23 +616,23 @@
 
 
 def first_sum_kernel(place, *refs):
-    given, outs, held, sems = refs[:12], refs[12:20], refs[20], refs[21]
+    given, outs, held, sems = refs[:12], refs[12:20], refs[20:23], refs[23]
     copies = {}
     for d in range(4):
         for g, other in ((1, 0), (0, 1), (2, 0)):
             i = lax.rem(place[other] + d, 4)
             copies[g, d] = [
-                pltpu.make_async_copy(given[4 * g + k].at[i], held.at[g, d, k], sems.at[g, d, k])
+                pltpu.make_async_copy(given[4 * g + k].at[i], held[g].at[d, k], sems.at[g, d, k])
                 for k in range(4)
             ]
             for copy in copies[g, d]:
                 copy.start()
     for d in range(4):
-        for g, (h, start) in ((1, (1, 0)), (0, (0, 0)), (2, (1, PAD))):
+        for g, h, start in ((1, 1, 0), (0, 0, 0), (2, 1, PAD)):
             for copy in copies[g, d]:
                 copy.wait()
-            summed = total([held[g, d, k] for k in range(4)]).astype(BF)
-            outs[4 * h + d][:, start : start + PAD] = summed
+            summed = total([held[g][d, k] for k in range(4)]).astype(BF)
+            outs[4 * h + d][:, start : start + summed.shape[1]] = summed
 
 
 def second_sum_kernel(place, *refs):
@@ -629,7 +669,10 @@
     for i in range(SHARD):
         g_up[i] = up[i : i + 1]
     start = WIDE[0]
-    attn = [held[a, :, start + PAD :] for a in range(4)]
+    attn = [
+        jnp.concatenate([held[a, :, PAD:start], held[a, :, start + PAD :]], axis=1)
+        for a in range(4)
+    ]
     rows = [held[a, :, start : start + D] for a in range(4)] + [attn[3][:, :D]]
     order_copy.wait()
     rows = dot_t(jnp.concatenate(rows, axis=0), order[:D])
@@ -712,14 +755,14 @@
     top = call("both", x=arrived, grad=cot, old=first)
     coming = lax.ppermute(top["dx"], "section", [(1, 0)])
     early = [top["early0"]] + [ring(top[f"early{d}"], "z", d) for d in (1, 3, 2)]
-    coming, early[1], early[2] = lax.optimization_barrier((coming, early[1], early[2]))
     branch = jnp.where(section == 0, coming, cot)
-    branches = [branch] + [ring(branch, "z", d) for d in (1, 3, 2)]
+    branches = [branch] + [ring(branch, "z", d) for d in (1, 3)]
     kept = {k: first[k] for k in KEPT}
     old = {**{k: top[k] for k in (*GRADS, *LATE)}, **kept}
     bwd = call("bwd", x=x0, grad=coming, old=old)
     sends = [bwd[f"late{d}"] for d in (1, 3, 2)]
     early, branches, sends = lax.optimization_barrier((early, branches, sends))
+    branches.append(ring(branches[0], "z", 2))
     late = [bwd["late0"]] + [ring(v, "z", d) for v, d in zip(sends, (1, 3, 2))]
 
     vmem, sem = pltpu.VMEM, pltpu.SemaphoreType.DMA
@@ -728,7 +771,7 @@
         "down_products",
         place,
         [],
-        [BLOCK] * 4,
+        [block(PAD)] * 4,
         [vmem((4, 4, CHUNK, PAD), BF), vmem((4,) + WIDEROW, BF), vmem((4,) + ROW, BF), sem((3, 4))],
         far=[*early, *branches],
         far_out=True,
@@ -741,23 +784,25 @@
         "products",
         place,
         [small],
-        [BLOCK] * 8,
-        [vmem((4, 4, CHUNK, PAD), BF)] * 2 + [vmem((4, 4) + WIDEROW, BF), sem((6, 4))],
+        [block(WIDE[0])] * 4 + [block(PAD - PART)] * 4,
+        [vmem((4, 4, CHUNK, width), BF) for width in (WIDE[0], PAD - PART)]
+        + [vmem((4, 4) + WIDEROW, BF), sem((7, 4))],
         far=[*early, *late],
         far_out=True,
     )
-    down, out = lax.optimization_barrier((down, out))
-    up = [out[0]] + [ring(out[d], "x", d) for d in (2, 1, 3)]
-    after = ring(out[5], "y", 1)
-    held, after = lax.optimization_barrier((out[7], after))
-    attn = [out[4], ring(out[6], "y", 2), after, ring(held, "y", 3)]
+    xs, ys = out[:4], out[4:]
+    down[1], xs = lax.optimization_barrier((down[1], xs))
+    down, ys = lax.optimization_barrier((down, ys))
+    up = [xs[0]] + [ring(xs[d], "x", d) for d in (2, 1, 3)]
+    attn = [ys[0]] + [ring(ys[d], "y", d) for d in (2, 1, 3)]
     out = local_call(
         first_sum_kernel,
         "first_sum",
         place,
         [],
         [((CHUNK, WIDE[h]), BF) for h in (0, 1) for _ in range(4)],
-        [vmem((3, 4, 4, CHUNK, PAD), BF), sem((3, 4, 4))],
+        [vmem((4, 4, CHUNK, width), BF) for width in (WIDE[0], PAD, PAD - PART)]
+        + [sem((3, 4, 4))],
         far=[*up, *down, *attn],
     )
     got = []

time: 428 us -> 442 us (1.033)
  waiting for transfers between devices: 244 us -> 260 us
    ppermute x27, waiting for transfers between devices: 71.7 us -> 90.4 us  [ring(): return lax.ppermute(v, axis, [(i, (i + d) % 4) for i in range(4)])]
  transfers between devices with their start and end apart: 30 -> 30, of which waited for: 14 -> 18; matrix products, arithmetic and copies ran while one was open for 1% -> 1% of each run, Pallas kernels for 10% -> 10%
where the time goes in v3:
time: 442 us; the launch traced here: 434 us
  waiting for transfers between devices  260 us (59%)
  Pallas kernels  87.7 us (20%)
  starting transfers between devices  48.1 us (11%)
  between operations  15.1 us (3%)
  local copies, waits for them, and re-layouts  14.6 us (3%)
  matrix products  5.57 us (1%)
    all_gather x1, waiting for transfers between devices, body(): whole = lax.all_gather(sent, ('x', 'y', 'z'), axis=0, tiled=True)  148 us
    ppermute x27, waiting for transfers between devices, ring(): return lax.ppermute(v, axis, [(i, (i + d) % 4) for i in range(4)])  90.4 us
    pallas_call x3, Pallas kernels, layer_call(): pl.pallas_call(kernel, in_specs=[pl.BlockSpec(memory_space=pltpu.SMEM)] +...  49.2 us
    ppermute x27, starting transfers between devices, ring(): return lax.ppermute(v, axis, [(i, (i + d) % 4) for i in range(4)])  45.5 us
    pallas_call x6, Pallas kernels, local_call(): pl.pallas_call(kernel, in_specs=[pl.BlockSpec(memory_space=pltpu.SMEM)] +...  32.1 us
    ppermute x1, waiting for transfers between devices, body(): coming = lax.ppermute(top['dx'], 'section', [(1, 0)])  21.6 us
  transfers between devices with their start and end apart: 30, of which 18 were waited for; matrix products, arithmetic and copies ran while one was open for 1% of the time, Pallas kernels for 10%

profile of v3, /device:TPU:0, one launch (start us, length us, event | category | flops | bytes accessed | tf_op | source)
XLA Modules:
  0.0 433.9 jit_solution(4571815147374926566)
XLA Ops:
  20.3 148.2 %all-gather.2.cloned.1.call-done.whole.refs_0_ = bf16[1024,14720]{1,0:T(8,128)(2,1)} async-done(((bf16[16,14720]{1,0:T(8,128)(2,1)}), bf16[1024,14720]{1,0:T(8,128)(2,1)}) %all-gather.2.cloned.1.call-update) | async-done | bytes 30146576 | tf_op jit(solution)/shard_map/all_gather | solution.py:728
  168.6 6.4 %unpack.1 = (bf16[64,14336]{1,0:T(8,128)(2,1)}, f32[16,1088]{1,0:T(8,128)}, f32[16,1152]{1,0:T(8,128)}) custom-call(bf16[1024,14720]{1,0:T(8,128)(2,1)} %all-gather.2.cloned.1.call-done.whole.refs_0_, bf16[1024,1024]{1,0:T(8,128)(2,1)} %constant.56.clone.refs_0_, bf16[16,256]{1,0:T(8,128)(2,1)} %constant.51.clone.refs_1_, ...), custom_call_target="tpu_custom_call" | custom-call | tf_op jit(solution)/shard_map/unpack/pallas_call | solution.py:126
  175.0 16.3 %layer_fwd.1 = (bf16[128,1088]{1,0:T(8,128)(2,1)}, bf16[3,128,1152]{2,1,0:T(8,128)(2,1)}, bf16[3,128,1152]{2,1,0:T(8,128)(2,1)}, bf16[3,128,1152]{2,1,0:T(8,128)...) custom-call(s32[4]{0:T(128)} %pad_add_fusion.place_ref.place, ...), custom_call_target="tpu_custom_call" | custom-call | flops 4000000000 | bytes 30081024 | tf_op jit(solution)/shard_map/layer_fwd/pallas_call | solution.py:484
  195.2 6.9 %layer_both.1 = (bf16[128,1088]{1,0:T(8,128)(2,1)}, bf16[128,1088]{1,0:T(8,128)(2,1)}, f32[16,1088]{1,0:T(8,128)}, bf16[3,128,1152]{2,1,0:T(8,128)(2,1)}, bf16[3...) custom-call(s32[4]{0:T(128)} %pad_add_fusion.place_ref.place, ...), custom_call_target="tpu_custom_call" | custom-call | flops 12000000000 | bytes 30081024 | tf_op jit(solution)/shard_map/layer_both/pallas_call | solution.py:484
  204.4 3.3 collective-permute-start.3
  208.3 21.6 %collective-permute-done.1.refs_16_ = bf16[128,1088]{1,0:T(8,128)(2,1)S(1)} collective-permute-done((bf16[128,1088]{1,0:T(8,128)(2,1)}, bf16[128,1088]{1,0:T(8,128)(2,1)S(1)}, u32[]{:S(2)}, u32[]{:S(2)}) %collective-permute-start.1) | collective-permute-done | bytes 278560 | tf_op jit(solution)/shard_map/ppermute | solution.py:756
  232.3 25.9 %layer_bwd.1 = (bf16[128,1088]{1,0:T(8,128)(2,1)}, f32[16,1088]{1,0:T(8,128)}, bf16[2,128,1152]{2,1,0:T(8,128)(2,1)}, bf16[2,128,1152]{2,1,0:T(8,128)(2,1)}, bf1...) custom-call(s32[4]{0:T(128)} %pad_add_fusion.place_ref.place, ...), custom_call_target="tpu_custom_call" | custom-call | flops 8000000000 | bytes 30081024 | tf_op jit(solution)/shard_map/layer_bwd/pallas_call | solution.py:484
  259.0 2.7 collective-permute-start.8
  265.3 29.7 %collective-permute-done.10.refs_7_ = bf16[128,1088]{1,0:T(8,128)(2,1)S(1)} collective-permute-done((bf16[128,1088]{1,0:T(8,128)(2,1)S(1)}, bf16[128,1088]{1,0:T(8,128)(2,1)S(1)}, u32[]{:S(2)}, u32[]{:S(2)}) %collective-permute-start.10) | collective-permute-done | bytes 278560 | tf_op jit(solution)/shard_map/ppermute | solution.py:689
  295.7 5.7 %down_products.1 = (bf16[4,72,1152]{2,1,0:T(8,128)(2,1)}, bf16[4,72,1152]{2,1,0:T(8,128)(2,1)}, bf16[4,72,1152]{2,1,0:T(8,128)(2,1)}, bf16[4,72,1152]{2,1,0:T(8,128)(2,1)}) custom-call(s32[4]{0:T(128)} %pad_add_fusion.place_ref.place, bf16[3,128,1152]{2,1,0:T(8,128)(2,1)} %get-tuple-element.136.refs_0_, bf16[3,128,1152]{2,1,0:T(8,128)(2,1)} %copy-done.2, ...), custom_call_target="tpu_custom_call" | custom-call | tf_op jit(solution)/shard_map/down_products/pallas_call | solution.py:521
  302.3 3.0 collective-permute-start.11
  308.8 8.0 %products.1 = (bf16[4,72,1536]{2,1,0:T(8,128)(2,1)}, bf16[4,72,1536]{2,1,0:T(8,128)(2,1)}, bf16[4,72,1536]{2,1,0:T(8,128)(2,1)}, bf16[4,72,1536]{2,1,0:T(8,128)(...) custom-call(s32[4]{0:T(128)} %pad_add_fusion.place_ref.place, ...), custom_call_target="tpu_custom_call" | custom-call | tf_op jit(solution)/shard_map/products/pallas_call | solution.py:521
  316.8 5.1 %collective-permute-done.11.refs_5_ = bf16[4,72,1152]{2,1,0:T(8,128)(2,1)S(1)} collective-permute-done((bf16[4,72,1152]{2,1,0:T(8,128)(2,1)}, bf16[4,72,1152]{2,1,0:T(8,128)(2,1)S(1)}, u32[]{:S(2)}, u32[]{:S(2)}) %collective-permute-start.11) | collective-permute-done | bytes 663584 | tf_op jit(solution)/shard_map/ppermute | solution.py:689
  321.9 11.7 %collective-permute-done.15.refs_6_ = bf16[4,72,1152]{2,1,0:T(8,128)(2,1)S(1)} collective-permute-done((bf16[4,72,1152]{2,1,0:T(8,128)(2,1)}, bf16[4,72,1152]{2,1,0:T(8,128)(2,1)S(1)}, u32[]{:S(2)}, u32[]{:S(2)}) %collective-permute-start.15) | collective-permute-done | bytes 663584 | tf_op jit(solution)/shard_map/ppermute | solution.py:689
  336.1 3.9 collective-permute-start.12
  344.4 4.1 collective-permute-done.17.refs_9_
  350.2 6.8 %collective-permute-done.18.refs_10_ = bf16[4,72,768]{2,1,0:T(8,128)(2,1)S(1)} collective-permute-done((bf16[4,72,768]{2,1,0:T(8,128)(2,1)}, bf16[4,72,768]{2,1,0:T(8,128)(2,1)S(1)}, u32[]{:S(2)}, u32[]{:S(2)}) %collective-permute-start.18) | collective-permute-done | bytes 442400 | tf_op jit(solution)/shard_map/ppermute | solution.py:689
  360.8 17.2 %collective-permute-done.13.refs_2_ = bf16[4,72,1536]{2,1,0:T(8,128)(2,1)S(1)} collective-permute-done((bf16[4,72,1536]{2,1,0:T(8,128)(2,1)}, bf16[4,72,1536]{2,1,0:T(8,128)(2,1)S(1)}, u32[]{:S(2)}, u32[]{:S(2)}) %collective-permute-start.13) | collective-permute-done | bytes 884768 | tf_op jit(solution)/shard_map/ppermute | solution.py:689
  379.8 5.7 %first_sum.1 = (bf16[72,1536]{1,0:T(8,128)(2,1)}, bf16[72,1536]{1,0:T(8,128)(2,1)}, bf16[72,1536]{1,0:T(8,128)(2,1)}, bf16[72,1536]{1,0:T(8,128)(2,1)}, bf16[72,...) custom-call(s32[4]{0:T(128)} %pad_add_fusion.place_ref.place, ...), custom_call_target="tpu_custom_call" | custom-call | tf_op jit(solution)/shard_map/first_sum/pallas_call | solution.py:521
  395.4 4.0 collective-permute-done.21.refs_2_
  399.4 3.2 collective-permute-done.22.refs_3_
  404.2 2.9 second_sum.1
  410.9 4.3 restore.1
  418.3 5.5 %owners.1 = (f32[17,1,4352]{2,1,0:T(1,128)}, f32[68,1,1088]{2,1,0:T(1,128)}, f32[17,1,1088]{2,1,0:T(1,128)}, f32[17,1,3264]{2,1,0:T(1,128)}, f32[17,64]{1,0:T(8,128)}) custom-call(s32[4]{0:T(128)} %pad_add_fusion.place_ref.place, bf16[1088,1088]{1,0:T(8,128)(2,1)} %constant.58.clone.refs_0_, bf16[1152,1088]{1,0:T(8,128)(2,1)} %constant.49.clone.refs_2_.order.refs_1_, ...), custom_call_target="tpu_custom_call" | custom-call | tf_op jit(solution)/shard_map/owners/pallas_call | solution.py:521
  (179 shorter events, 66.6 us)
Async XLA Ops:
  7.2 161.4 %all-gather.2.cloned.1.call-start = ((), (), s32[]{:S(2)}) async-start(), calls=%async_computation | async-start | bytes 30617600 | tf_op jit(solution)/shard_map/all_gather | solution.py:728
  202.1 27.8 %collective-permute-start.1 = (bf16[128,1088]{1,0:T(8,128)(2,1)}, bf16[128,1088]{1,0:T(8,128)(2,1)S(1)}, u32[]{:S(2)}, u32[]{:S(2)}) collective-permute-start(bf16[128,1088]{1,0:T(8,128)(2,1)} %get-tuple-element.112.refs_3_), channel_id=1, source_target_pairs={{64,0},{65,1},{66,2},{67,3},{68,4},{69,5},{70,6},{71,7},{72,8},{73... | collective-permute-start | bytes 835592 | tf_op jit(solution)/shard_map/ppermute | solution.py:756
  203.4 54.8 %collective-permute-start.2 = (bf16[3,128,1152]{2,1,0:T(8,128)(2,1)}, bf16[3,128,1152]{2,1,0:T(8,128)(2,1)S(1)}, u32[]{:S(2)}, u32[]{:S(2)}) collective-permute-start(bf16[3,128,1152]{2,1,0:T(8,128)(2,1)} %get-tuple-element.127), channel_id=1, source_target_pairs={{0,1},{1,2},{2,3},{3,0},{4,5},{5,6},{6,7},{7,4},{8,9},{9,10},{10,1... | collective-permute-start | bytes 2654216 | tf_op jit(solution)/shard_map/ppermute | solution.py:689
  204.4 53.9 %collective-permute-start.3 = (bf16[3,128,1152]{2,1,0:T(8,128)(2,1)}, bf16[3,128,1152]{2,1,0:T(8,128)(2,1)S(1)}, u32[]{:S(2)}, u32[]{:S(2)}) collective-permute-start(bf16[3,128,1152]{2,1,0:T(8,128)(2,1)} %get-tuple-element.128), channel_id=1, source_target_pairs={{0,3},{1,0},{2,1},{3,2},{4,7},{5,4},{6,5},{7,6},{8,11},{9,8},{10,9... | collective-permute-start | bytes 2654216 | tf_op jit(solution)/shard_map/ppermute | solution.py:689
  207.7 50.7 %collective-permute-start.4 = (bf16[3,128,1152]{2,1,0:T(8,128)(2,1)}, bf16[3,128,1152]{2,1,0:T(8,128)(2,1)S(1)}, u32[]{:S(2)}, u32[]{:S(2)}) collective-permute-start(bf16[3,128,1152]{2,1,0:T(8,128)(2,1)} %get-tuple-element.129), channel_id=1, source_target_pairs={{0,2},{1,3},{2,0},{3,1},{4,6},{5,7},{6,4},{7,5},{8,10},{9,11},{10,... | collective-permute-start | bytes 2654216 | tf_op jit(solution)/shard_map/ppermute | solution.py:689
  230.0 28.2 %collective-permute-start.6 = (bf16[128,1088]{1,0:T(8,128)(2,1)S(1)}, bf16[128,1088]{1,0:T(8,128)(2,1)S(1)}, u32[]{:S(2)}, u32[]{:S(2)}) collective-permute-start(bf16[128,1088]{1,0:T(8,128)(2,1)S(1)} %broadcast_select_fusion.refs_4_), channel_id=1, source_target_pairs={{0,3},{1,0},{2,1},{3,2},{4,7},{5,4},{6,5},{7,6},{8,11},{9,8},{10,9... | collective-permute-start | bytes 835592 | tf_op jit(solution)/shard_map/ppermute | solution.py:689
  232.3 26.0 %collective-permute-start.5 = (bf16[128,1088]{1,0:T(8,128)(2,1)S(1)}, bf16[128,1088]{1,0:T(8,128)(2,1)S(1)}, u32[]{:S(2)}, u32[]{:S(2)}) collective-permute-start(bf16[128,1088]{1,0:T(8,128)(2,1)S(1)} %broadcast_select_fusion.refs_4_), channel_id=1, source_target_pairs={{0,1},{1,2},{2,3},{3,0},{4,5},{5,6},{6,7},{7,4},{8,9},{9,10},{10,1... | collective-permute-start | bytes 835592 | tf_op jit(solution)/shard_map/ppermute | solution.py:689
  258.3 43.0 %collective-permute-start.7 = (bf16[2,128,1152]{2,1,0:T(8,128)(2,1)}, bf16[2,128,1152]{2,1,0:T(8,128)(2,1)S(1)}, u32[]{:S(2)}, u32[]{:S(2)}) collective-permute-start(bf16[2,128,1152]{2,1,0:T(8,128)(2,1)} %get-tuple-element.133), channel_id=1, source_target_pairs={{0,1},{1,2},{2,3},{3,0},{4,5},{5,6},{6,7},{7,4},{8,9},{9,10},{10,1... | collective-permute-start | bytes 1769480 | tf_op jit(solution)/shard_map/ppermute | solution.py:689
  259.0 42.4 %collective-permute-start.8 = (bf16[2,128,1152]{2,1,0:T(8,128)(2,1)}, bf16[2,128,1152]{2,1,0:T(8,128)(2,1)S(1)}, u32[]{:S(2)}, u32[]{:S(2)}) collective-permute-start(bf16[2,128,1152]{2,1,0:T(8,128)(2,1)} %get-tuple-element.134), channel_id=1, source_target_pairs={{0,3},{1,0},{2,1},{3,2},{4,7},{5,4},{6,5},{7,6},{8,11},{9,8},{10,9... | collective-permute-start | bytes 1769480 | tf_op jit(solution)/shard_map/ppermute | solution.py:689
  261.7 39.7 %collective-permute-start.9 = (bf16[2,128,1152]{2,1,0:T(8,128)(2,1)}, bf16[2,128,1152]{2,1,0:T(8,128)(2,1)S(1)}, u32[]{:S(2)}, u32[]{:S(2)}) collective-permute-start(bf16[2,128,1152]{2,1,0:T(8,128)(2,1)} %get-tuple-element.135), channel_id=1, source_target_pairs={{0,2},{1,3},{2,0},{3,1},{4,6},{5,7},{6,4},{7,5},{8,10},{9,11},{10,... | collective-permute-start | bytes 1769480 | tf_op jit(solution)/shard_map/ppermute | solution.py:689
  263.1 31.8 %collective-permute-start.10 = (bf16[128,1088]{1,0:T(8,128)(2,1)S(1)}, bf16[128,1088]{1,0:T(8,128)(2,1)S(1)}, u32[]{:S(2)}, u32[]{:S(2)}) collective-permute-start(bf16[128,1088]{1,0:T(8,128)(2,1)S(1)} %broadcast_select_fusion.refs_4_), channel_id=1, source_target_pairs={{0,2},{1,3},{2,0},{3,1},{4,6},{5,7},{6,4},{7,5},{8,10},{9,11},{10,... | collective-permute-start | bytes 835592 | tf_op jit(solution)/shard_map/ppermute | solution.py:689
  302.3 19.6 %collective-permute-start.11 = (bf16[4,72,1152]{2,1,0:T(8,128)(2,1)}, bf16[4,72,1152]{2,1,0:T(8,128)(2,1)S(1)}, u32[]{:S(2)}, u32[]{:S(2)}) collective-permute-start(bf16[4,72,1152]{2,1,0:T(8,128)(2,1)} %get-tuple-element.151), channel_id=1, source_target_pairs={{0,8},{4,12},{8,0},{12,4},{1,9},{5,13},{9,1},{13,5},{2,10},{6,14},... | collective-permute-start | bytes 1990664 | tf_op jit(solution)/shard_map/ppermute | solution.py:689
  305.3 28.3 %collective-permute-start.15 = (bf16[4,72,1152]{2,1,0:T(8,128)(2,1)}, bf16[4,72,1152]{2,1,0:T(8,128)(2,1)S(1)}, u32[]{:S(2)}, u32[]{:S(2)}) collective-permute-start(bf16[4,72,1152]{2,1,0:T(8,128)(2,1)} %get-tuple-element.167), channel_id=1, source_target_pairs={{0,4},{4,8},{8,12},{12,0},{1,5},{5,9},{9,13},{13,1},{2,6},{6,10},{... | collective-permute-start | bytes 1990664 | tf_op jit(solution)/shard_map/ppermute | solution.py:689
  306.1 27.7 %collective-permute-start.16 = (bf16[4,72,1152]{2,1,0:T(8,128)(2,1)}, bf16[4,72,1152]{2,1,0:T(8,128)(2,1)S(1)}, u32[]{:S(2)}, u32[]{:S(2)}) collective-permute-start(bf16[4,72,1152]{2,1,0:T(8,128)(2,1)} %get-tuple-element.168), channel_id=1, source_target_pairs={{0,12},{4,0},{8,4},{12,8},{1,13},{5,1},{9,5},{13,9},{2,14},{6,2},{... | collective-permute-start | bytes 1990664 | tf_op jit(solution)/shard_map/ppermute | solution.py:689
  333.8 14.8 %collective-permute-start.17 = (bf16[4,72,768]{2,1,0:T(8,128)(2,1)}, bf16[4,72,768]{2,1,0:T(8,128)(2,1)S(1)}, u32[]{:S(2)}, u32[]{:S(2)}) collective-permute-start(bf16[4,72,768]{2,1,0:T(8,128)(2,1)} %get-tuple-element.178), channel_id=1, source_target_pairs={{0,8},{4,12},{8,0},{12,4},{1,9},{5,13},{9,1},{13,5},{2,10},{6,14},... | collective-permute-start | bytes 1327112 | tf_op jit(solution)/shard_map/ppermute | solution.py:689
  336.1 24.7 %collective-permute-start.12 = (bf16[4,72,1536]{2,1,0:T(8,128)(2,1)}, bf16[4,72,1536]{2,1,0:T(8,128)(2,1)S(1)}, u32[]{:S(2)}, u32[]{:S(2)}) collective-permute-start(bf16[4,72,1536]{2,1,0:T(8,128)(2,1)} %get-tuple-element.162), channel_id=1, source_target_pairs={{0,32},{16,48},{32,0},{48,16},{1,33},{17,49},{33,1},{49,17},{2,34}... | collective-permute-start | bytes 2654216 | tf_op jit(solution)/shard_map/ppermute | solution.py:689
  340.0 38.0 %collective-permute-start.13 = (bf16[4,72,1536]{2,1,0:T(8,128)(2,1)}, bf16[4,72,1536]{2,1,0:T(8,128)(2,1)S(1)}, u32[]{:S(2)}, u32[]{:S(2)}) collective-permute-start(bf16[4,72,1536]{2,1,0:T(8,128)(2,1)} %get-tuple-element.163), channel_id=1, source_target_pairs={{0,16},{16,32},{32,48},{48,0},{1,17},{17,33},{33,49},{49,1},{2,18}... | collective-permute-start | bytes 2654216 | tf_op jit(solution)/shard_map/ppermute | solution.py:689
  340.5 37.8 %collective-permute-start.14 = (bf16[4,72,1536]{2,1,0:T(8,128)(2,1)}, bf16[4,72,1536]{2,1,0:T(8,128)(2,1)S(1)}, u32[]{:S(2)}, u32[]{:S(2)}) collective-permute-start(bf16[4,72,1536]{2,1,0:T(8,128)(2,1)} %get-tuple-element.164), channel_id=1, source_target_pairs={{0,48},{16,0},{32,16},{48,32},{1,49},{17,1},{33,17},{49,33},{2,50}... | collective-permute-start | bytes 2654216 | tf_op jit(solution)/shard_map/ppermute | solution.py:689
  343.2 13.8 %collective-permute-start.18 = (bf16[4,72,768]{2,1,0:T(8,128)(2,1)}, bf16[4,72,768]{2,1,0:T(8,128)(2,1)S(1)}, u32[]{:S(2)}, u32[]{:S(2)}) collective-permute-start(bf16[4,72,768]{2,1,0:T(8,128)(2,1)} %get-tuple-element.179), channel_id=1, source_target_pairs={{0,4},{4,8},{8,12},{12,0},{1,5},{5,9},{9,13},{13,1},{2,6},{6,10},{... | collective-permute-start | bytes 1327112 | tf_op jit(solution)/shard_map/ppermute | solution.py:689
  348.5 10.8 %collective-permute-start.19 = (bf16[4,72,768]{2,1,0:T(8,128)(2,1)}, bf16[4,72,768]{2,1,0:T(8,128)(2,1)S(1)}, u32[]{:S(2)}, u32[]{:S(2)}) collective-permute-start(bf16[4,72,768]{2,1,0:T(8,128)(2,1)} %get-tuple-element.180), channel_id=1, source_target_pairs={{0,12},{4,0},{8,4},{12,8},{1,13},{5,1},{9,5},{13,9},{2,14},{6,2},{... | collective-permute-start | bytes 1327112 | tf_op jit(solution)/shard_map/ppermute | solution.py:689
  387.5 15.1 %collective-permute-start.23 = (bf16[72,1920]{1,0:T(8,128)(2,1)}, bf16[72,1920]{1,0:T(8,128)(2,1)S(1)}, u32[]{:S(2)}, u32[]{:S(2)}) collective-permute-start(bf16[72,1920]{1,0:T(8,128)(2,1)} %get-tuple-element.186), channel_id=1, source_target_pairs={{0,16},{16,32},{32,48},{48,0},{1,17},{17,33},{33,49},{49,1},{2,18}... | collective-permute-start | bytes 829448 | tf_op jit(solution)/shard_map/ppermute | solution.py:689
  389.3 13.3 %collective-permute-start.24 = (bf16[72,1920]{1,0:T(8,128)(2,1)}, bf16[72,1920]{1,0:T(8,128)(2,1)S(1)}, u32[]{:S(2)}, u32[]{:S(2)}) collective-permute-start(bf16[72,1920]{1,0:T(8,128)(2,1)} %get-tuple-element.187), channel_id=1, source_target_pairs={{0,48},{16,0},{32,16},{48,32},{1,49},{17,1},{33,17},{49,33},{2,50}... | collective-permute-start | bytes 829448 | tf_op jit(solution)/shard_map/ppermute | solution.py:689
  390.8 12.7 %collective-permute-start.25 = (bf16[72,1920]{1,0:T(8,128)(2,1)}, bf16[72,1920]{1,0:T(8,128)(2,1)S(1)}, u32[]{:S(2)}, u32[]{:S(2)}) collective-permute-start(bf16[72,1920]{1,0:T(8,128)(2,1)} %get-tuple-element.188), channel_id=1, source_target_pairs={{0,32},{16,48},{32,0},{48,16},{1,33},{17,49},{33,1},{49,17},{2,34}... | collective-permute-start | bytes 829448 | tf_op jit(solution)/shard_map/ppermute | solution.py:689
  407.0 10.0 %collective-permute-start.26 = (bf16[24,3456]{1,0:T(8,128)(2,1)}, bf16[24,3456]{1,0:T(8,128)(2,1)S(1)}, u32[]{:S(2)}, u32[]{:S(2)}) collective-permute-start(bf16[24,3456]{1,0:T(8,128)(2,1)} %get-tuple-element.190), channel_id=1, source_target_pairs={{0,1},{1,2},{2,3},{3,0},{4,5},{5,6},{6,7},{7,4},{8,9},{9,10},{10,1... | collective-permute-start | bytes 497672 | tf_op jit(solution)/shard_map/ppermute | solution.py:689
  (47 other events, 627.0 us)
Sparse Core Ops, SparseCore 0:
  16.9 151.5 all-gather.1

commit v4 on v3

--- a/solution.py
+++ b/solution.py
@@ -551,11 +551,15 @@
     return copies
 
 
-def load(sources, held, sems):
+def load(sources, held, sems, other=None, use_other=None):
     copies = []
     for d in range(4):
         copies.append(pltpu.make_async_copy(sources[d], held.at[d], sems.at[d]))
-        copies[-1].start()
+        if other is None:
+            copies[d].start()
+            continue
+        pl.when(jnp.logical_not(use_other))(copies[d].start)
+        pl.when(use_other)(pltpu.make_async_copy(other[d], held.at[d], sems.at[d]).start)
 
     def rows():
         for copy in copies:
@@ -570,10 +574,10 @@
 
 
 def down_products_kernel(place, *refs):
-    early, branch, outs = refs[:4], refs[4:8], refs[8:12]
-    held, a_held, b_held, sems = refs[12:]
+    early, branch, cots, outs = refs[:4], refs[4:8], refs[8:12], refs[12:16]
+    held, a_held, b_held, sems = refs[16:]
     a = load([e.at[1] for e in early], a_held, sems.at[0])
-    b = load(branch, b_held, sems.at[1])
+    b = load(branch, b_held, sems.at[1], cots, place[3] == 1)
 
     def store(x, y, v):
         held[y, x] = v
@@ -689,6 +693,10 @@
     return lax.ppermute(v, axis, [(i, (i + d) % 4) for i in range(4)])
 
 
+def ring_of_first(v, d):
+    return lax.ppermute(v, ("section", "z"), [(i, (i + d) % 4) for i in range(4)])
+
+
 def restore_kernel(place, order, result, dx, acts, grads):
     acts[...] = dot_t(result[...], order[:D]).astype(BF)
     grads[...] = dot_t(dx[...], order[:D]).astype(BF)
@@ -726,6 +734,10 @@
     tail = jnp.pad(tail, (0, 16 * TAILW - tail.shape[0])).reshape(16, TAILW)
     sent = jnp.concatenate([shard[:16], tail], axis=1)
     whole = lax.all_gather(sent, ("x", "y", "z"), axis=0, tiled=True)
+    order_d = c["order_d"]
+    cot = matmul(cotangent.reshape(n, D), order_d).astype(BF)
+    cots = [cot] + [ring(cot, "z", d) for d in (1, 3, 2)]
+    whole, cots = lax.optimization_barrier((whole, cots))
     tails, vecs, nat = unpack(whole, c)
 
     ends = jnp.cumsum(lengths[:, 0], axis=1)
@@ -735,9 +747,7 @@
     at = jnp.arange(n, dtype=jnp.int32)
     pairs = ((seg[:, None] == seg[None, :]) & (at[:, None] >= at[None, :])).astype(F32)
 
-    order_d = c["order_d"]
     x0 = matmul(inputs.reshape(n, D), order_d).astype(BF)
-    cot = matmul(cotangent.reshape(n, D), order_d).astype(BF)
     place = jnp.stack([lax.axis_index("x"), lax.axis_index("y"), lax.axis_index("z"), section])
     call = functools.partial(
         layer_call,
@@ -755,14 +765,14 @@
     top = call("both", x=arrived, grad=cot, old=first)
     coming = lax.ppermute(top["dx"], "section", [(1, 0)])
     early = [top["early0"]] + [ring(top[f"early{d}"], "z", d) for d in (1, 3, 2)]
-    branch = jnp.where(section == 0, coming, cot)
-    branches = [branch] + [ring(branch, "z", d) for d in (1, 3)]
+    branches = [coming] + [ring_of_first(coming, d) for d in (1, 3)]
+    early[1], held = lax.optimization_barrier((early[1], coming))
+    branches.append(ring_of_first(held, 2))
     kept = {k: first[k] for k in KEPT}
     old = {**{k: top[k] for k in (*GRADS, *LATE)}, **kept}
     bwd = call("bwd", x=x0, grad=coming, old=old)
     sends = [bwd[f"late{d}"] for d in (1, 3, 2)]
     early, branches, sends = lax.optimization_barrier((early, branches, sends))
-    branches.append(ring(branches[0], "z", 2))
     late = [bwd["late0"]] + [ring(v, "z", d) for v, d in zip(sends, (1, 3, 2))]
 
     vmem, sem = pltpu.VMEM, pltpu.SemaphoreType.DMA
@@ -773,7 +783,7 @@
         [],
         [block(PAD)] * 4,
         [vmem((4, 4, CHUNK, PAD), BF), vmem((4,) + WIDEROW, BF), vmem((4,) + ROW, BF), sem((3, 4))],
-        far=[*early, *branches],
+        far=[*early, *branches, *cots],
         far_out=True,
     )
     late, down = lax.optimization_barrier((late, down))

time: 442 us -> 423 us (0.957); the launches traced: 434 us -> 422 us
  waiting for transfers between devices: 260 us -> 228 us
  Pallas kernels: 87.7 us -> 98.8 us
  starting transfers between devices: 48.1 us -> 57.4 us
    ppermute x27, waiting for transfers between devices: 90.4 us -> 72.6 us  [ring(): return lax.ppermute(v, axis, [(i, (i + d) % 4) for i in range(4)])]
    all_gather x1, waiting for transfers between devices: 148 us -> 132 us  [body(): whole = lax.all_gather(sent, ('x', 'y', 'z'), axis=0, tiled=True)]
    pallas_call x3, Pallas kernels: 49.2 us -> 60.2 us  [layer_call(): pl.pallas_call(kernel, in_specs=[pl.BlockSpec(memory_space=pltpu.SMEM)] +...]
    ppermute x0 -> x3, starting transfers between devices: none -> 10.6 us  [ring_of_first(): lax.ppermute(v, ('section', 'z'), [(i, (i + d) % 4) for i in range(4)])]
  transfers between devices with their start and end apart: 30 -> 33, of which waited for: 18 -> 19; matrix products, arithmetic and copies ran while one was open for 1% -> 2% of each run, Pallas kernels for 10% -> 10%
where the time goes in v4:
time: 423 us; the launch traced here: 422 us
  waiting for transfers between devices  228 us (54%)
  Pallas kernels  98.8 us (23%)
  starting transfers between devices  57.4 us (14%)
  between operations  14.9 us (4%)
  local copies, waits for them, and re-layouts  13.5 us (3%)
  matrix products  7.24 us (2%)
    all_gather x1, waiting for transfers between devices, body(): whole = lax.all_gather(sent, ('x', 'y', 'z'), axis=0, tiled=True)  132 us
    ppermute x27, waiting for transfers between devices, ring(): return lax.ppermute(v, axis, [(i, (i + d) % 4) for i in range(4)])  72.6 us
    pallas_call x3, Pallas kernels, layer_call(): pl.pallas_call(kernel, in_specs=[pl.BlockSpec(memory_space=pltpu.SMEM)] +...  60.2 us
    ppermute x27, starting transfers between devices, ring(): return lax.ppermute(v, axis, [(i, (i + d) % 4) for i in range(4)])  44.1 us
    pallas_call x6, Pallas kernels, local_call(): pl.pallas_call(kernel, in_specs=[pl.BlockSpec(memory_space=pltpu.SMEM)] +...  32.1 us
    ppermute x1, waiting for transfers between devices, body(): coming = lax.ppermute(top['dx'], 'section', [(1, 0)])  22.5 us
    ppermute x3, starting transfers between devices, ring_of_first(): lax.ppermute(v, ('section', 'z'), [(i, (i + d) % 4) for i in range(4)])  10.6 us
  transfers between devices with their start and end apart: 33, of which 19 were waited for; matrix products, arithmetic and copies ran while one was open for 2% of the time, Pallas kernels for 10%

profile of v4, /device:TPU:0, one launch (start us, length us, event | category | flops | bytes accessed | tf_op | source)
XLA Modules:
  0.0 422.4 jit_solution(2141896633438587894)
XLA Ops:
  17.9 4.0 collective-permute-start.2
  30.2 7.9 %collective-permute-done.1.refs_10_ = bf16[128,1088]{1,0:T(8,128)(2,1)S(1)} collective-permute-done((bf16[128,1088]{1,0:T(8,128)(2,1)S(1)}, bf16[128,1088]{1,0:T(8,128)(2,1)S(1)}, u32[]{:S(2)}, u32[]{:S(2)}) %collective-permute-start.1) | collective-permute-done | bytes 278560 | tf_op jit(solution)/shard_map/ppermute | solution.py:693
  38.1 131.6 %all-gather.2.cloned.1.call-done.whole.refs_0_ = bf16[1024,14720]{1,0:T(8,128)(2,1)} async-done(((bf16[16,14720]{1,0:T(8,128)(2,1)}), bf16[1024,14720]{1,0:T(8,128)(2,1)}) %all-gather.2.cloned.1.call-update) | async-done | bytes 30146576 | tf_op jit(solution)/shard_map/all_gather | solution.py:736
  169.6 6.4 %unpack.1 = (bf16[64,14336]{1,0:T(8,128)(2,1)}, f32[16,1088]{1,0:T(8,128)}, f32[16,1152]{1,0:T(8,128)}) custom-call(bf16[1024,14720]{1,0:T(8,128)(2,1)} %all-gather.2.cloned.1.call-done.whole.refs_0_, bf16[1024,1024]{1,0:T(8,128)(2,1)} %constant.56.clone.refs_0_, bf16[16,256]{1,0:T(8,128)(2,1)} %constant.51.clone.refs_1_, ...), custom_call_target="tpu_custom_call" | custom-call | tf_op jit(solution)/shard_map/unpack/pallas_call | solution.py:126
  176.1 27.9 %layer_fwd.1 = (bf16[128,1088]{1,0:T(8,128)(2,1)}, bf16[3,128,1152]{2,1,0:T(8,128)(2,1)}, bf16[3,128,1152]{2,1,0:T(8,128)(2,1)}, bf16[3,128,1152]{2,1,0:T(8,128)...) custom-call(s32[4]{0:T(128)} %pad_add_fusion.place_ref.place, ...), custom_call_target="tpu_custom_call" | custom-call | flops 4000000000 | bytes 30081024 | tf_op jit(solution)/shard_map/layer_fwd/pallas_call | solution.py:484
  207.4 6.4 %layer_both.1 = (bf16[128,1088]{1,0:T(8,128)(2,1)}, bf16[128,1088]{1,0:T(8,128)(2,1)}, f32[16,1088]{1,0:T(8,128)}, bf16[3,128,1152]{2,1,0:T(8,128)(2,1)}, bf16[3...) custom-call(s32[4]{0:T(128)} %pad_add_fusion.place_ref.place, ...), custom_call_target="tpu_custom_call" | custom-call | flops 12000000000 | bytes 30081024 | tf_op jit(solution)/shard_map/layer_both/pallas_call | solution.py:484
  220.1 22.5 %collective-permute-done.4.refs_16_.refs_4_ = bf16[128,1088]{1,0:T(8,128)(2,1)S(1)} collective-permute-done((bf16[128,1088]{1,0:T(8,128)(2,1)}, bf16[128,1088]{1,0:T(8,128)(2,1)S(1)}, u32[]{:S(2)}, u32[]{:S(2)}) %collective-permute-start.4) | collective-permute-done | bytes 278560 | tf_op jit(solution)/shard_map/ppermute | solution.py:766
  242.7 4.3 %collective-permute-start.9 = (bf16[128,1088]{1,0:T(8,128)(2,1)S(1)}, bf16[128,1088]{1,0:T(8,128)(2,1)S(1)}, u32[]{:S(2)}, u32[]{:S(2)}) collective-permute-start(bf16[128,1088]{1,0:T(8,128)(2,1)S(1)} %collective-permute-done.4.refs_16_.refs_4_), channel_id=1, source_target_pairs={{0,3},{1,0},{2,1},{3,2},{4,7},{5,4},{6,5},{7,6},{8,11},{9,8},{10,9... | collective-permute-start | bytes 835592 | tf_op jit(solution)/shard_map/ppermute | solution.py:697
  248.9 4.4 %collective-permute-start.10 = (bf16[128,1088]{1,0:T(8,128)(2,1)S(1)}, bf16[128,1088]{1,0:T(8,128)(2,1)S(1)}, u32[]{:S(2)}, u32[]{:S(2)}) collective-permute-start(bf16[128,1088]{1,0:T(8,128)(2,1)S(1)} %collective-permute-done.4.refs_16_.refs_4_), channel_id=1, source_target_pairs={{0,2},{1,3},{2,0},{3,1},{4,6},{5,7},{6,4},{7,5},{8,10},{9,11},{10,... | collective-permute-start | bytes 835592 | tf_op jit(solution)/shard_map/ppermute | solution.py:697
  253.3 25.9 %layer_bwd.1 = (bf16[128,1088]{1,0:T(8,128)(2,1)}, f32[16,1088]{1,0:T(8,128)}, bf16[2,128,1152]{2,1,0:T(8,128)(2,1)}, bf16[2,128,1152]{2,1,0:T(8,128)(2,1)}, bf1...) custom-call(s32[4]{0:T(128)} %pad_add_fusion.place_ref.place, ...), custom_call_target="tpu_custom_call" | custom-call | flops 8000000000 | bytes 30081024 | tf_op jit(solution)/shard_map/layer_bwd/pallas_call | solution.py:484
  283.2 5.7 %down_products.1 = (bf16[4,72,1152]{2,1,0:T(8,128)(2,1)}, bf16[4,72,1152]{2,1,0:T(8,128)(2,1)}, bf16[4,72,1152]{2,1,0:T(8,128)(2,1)}, bf16[4,72,1152]{2,1,0:T(8,128)(2,1)}) custom-call(s32[4]{0:T(128)} %pad_add_fusion.place_ref.place, bf16[3,128,1152]{2,1,0:T(8,128)(2,1)} %get-tuple-element.147.refs_0_, bf16[3,128,1152]{2,1,0:T(8,128)(2,1)} %copy-done.2, ...), custom_call_target="tpu_custom_call" | custom-call | tf_op jit(solution)/shard_map/down_products/pallas_call | solution.py:521
  288.9 12.3 %collective-permute-done.11.refs_5_ = bf16[2,128,1152]{2,1,0:T(8,128)(2,1)S(1)} collective-permute-done((bf16[2,128,1152]{2,1,0:T(8,128)(2,1)}, bf16[2,128,1152]{2,1,0:T(8,128)(2,1)S(1)}, u32[]{:S(2)}, u32[]{:S(2)}) %collective-permute-start.11) | collective-permute-done | bytes 589856 | tf_op jit(solution)/shard_map/ppermute | solution.py:693
  301.2 3.1 collective-permute-start.14
  307.7 8.0 %products.1 = (bf16[4,72,1536]{2,1,0:T(8,128)(2,1)}, bf16[4,72,1536]{2,1,0:T(8,128)(2,1)}, bf16[4,72,1536]{2,1,0:T(8,128)(2,1)}, bf16[4,72,1536]{2,1,0:T(8,128)(...) custom-call(s32[4]{0:T(128)} %pad_add_fusion.place_ref.place, ...), custom_call_target="tpu_custom_call" | custom-call | tf_op jit(solution)/shard_map/products/pallas_call | solution.py:521
  318.3 7.0 %collective-permute-done.18.refs_6_ = bf16[4,72,1152]{2,1,0:T(8,128)(2,1)S(1)} collective-permute-done((bf16[4,72,1152]{2,1,0:T(8,128)(2,1)}, bf16[4,72,1152]{2,1,0:T(8,128)(2,1)S(1)}, u32[]{:S(2)}, u32[]{:S(2)}) %collective-permute-start.18) | collective-permute-done | bytes 663584 | tf_op jit(solution)/shard_map/ppermute | solution.py:693
  327.5 3.5 collective-permute-start.15
  338.8 6.2 %collective-permute-done.21.refs_10_ = bf16[4,72,768]{2,1,0:T(8,128)(2,1)S(1)} collective-permute-done((bf16[4,72,768]{2,1,0:T(8,128)(2,1)}, bf16[4,72,768]{2,1,0:T(8,128)(2,1)S(1)}, u32[]{:S(2)}, u32[]{:S(2)}) %collective-permute-start.21) | collective-permute-done | bytes 442400 | tf_op jit(solution)/shard_map/ppermute | solution.py:693
  346.1 5.7 %collective-permute-done.15.refs_1_ = bf16[4,72,1536]{2,1,0:T(8,128)(2,1)S(1)} collective-permute-done((bf16[4,72,1536]{2,1,0:T(8,128)(2,1)}, bf16[4,72,1536]{2,1,0:T(8,128)(2,1)S(1)}, u32[]{:S(2)}, u32[]{:S(2)}) %collective-permute-start.15) | collective-permute-done | bytes 884768 | tf_op jit(solution)/shard_map/ppermute | solution.py:693
  351.8 16.0 %collective-permute-done.16.refs_2_ = bf16[4,72,1536]{2,1,0:T(8,128)(2,1)S(1)} collective-permute-done((bf16[4,72,1536]{2,1,0:T(8,128)(2,1)}, bf16[4,72,1536]{2,1,0:T(8,128)(2,1)S(1)}, u32[]{:S(2)}, u32[]{:S(2)}) %collective-permute-start.16) | collective-permute-done | bytes 884768 | tf_op jit(solution)/shard_map/ppermute | solution.py:693
  369.6 5.7 %first_sum.1 = (bf16[72,1536]{1,0:T(8,128)(2,1)}, bf16[72,1536]{1,0:T(8,128)(2,1)}, bf16[72,1536]{1,0:T(8,128)(2,1)}, bf16[72,1536]{1,0:T(8,128)(2,1)}, bf16[72,...) custom-call(s32[4]{0:T(128)} %pad_add_fusion.place_ref.place, ...), custom_call_target="tpu_custom_call" | custom-call | tf_op jit(solution)/shard_map/first_sum/pallas_call | solution.py:521
  379.9 3.2 collective-permute-start.24
  384.2 7.4 %collective-permute-done.24.refs_2_ = bf16[72,1536]{1,0:T(8,128)(2,1)S(1)} collective-permute-done((bf16[72,1536]{1,0:T(8,128)(2,1)}, bf16[72,1536]{1,0:T(8,128)(2,1)S(1)}, u32[]{:S(2)}, u32[]{:S(2)}) %collective-permute-start.24) | collective-permute-done | bytes 221216 | tf_op jit(solution)/shard_map/ppermute | solution.py:693
  400.0 4.3 %restore.1 = (bf16[128,1088]{1,0:T(8,128)(2,1)}, bf16[128,1088]{1,0:T(8,128)(2,1)}) custom-call(s32[4]{0:T(128)} %pad_add_fusion.place_ref.place, bf16[1152,1088]{1,0:T(8,128)(2,1)} %constant.49.clone.refs_2_.order.refs_1_, bf16[128,1088]{1,0:T(8,128)(2,1)} %get-tuple-element.120.result, bf16[128,1088]{1,0:T(8,128)(2,1)} %get-tuple-element.130.dx), custom_call_target="tpu_custom_call" | custom-call | tf_op jit(solution)/shard_map/restore/pallas_call | solution.py:521
  407.0 5.5 %owners.1 = (f32[17,1,4352]{2,1,0:T(1,128)}, f32[68,1,1088]{2,1,0:T(1,128)}, f32[17,1,1088]{2,1,0:T(1,128)}, f32[17,1,3264]{2,1,0:T(1,128)}, f32[17,64]{1,0:T(8,128)}) custom-call(s32[4]{0:T(128)} %pad_add_fusion.place_ref.place, bf16[1088,1088]{1,0:T(8,128)(2,1)} %constant.58.clone.refs_0_, bf16[1152,1088]{1,0:T(8,128)(2,1)} %constant.49.clone.refs_2_.order.refs_1_, ...), custom_call_target="tpu_custom_call" | custom-call | tf_op jit(solution)/shard_map/owners/pallas_call | solution.py:521
  (184 shorter events, 72.7 us)
Async XLA Ops:
  7.2 162.4 %all-gather.2.cloned.1.call-start = ((), (), s32[]{:S(2)}) async-start(), calls=%async_computation | async-start | bytes 30617600 | tf_op jit(solution)/shard_map/all_gather | solution.py:736
  17.9 12.2 %collective-permute-start.2 = (bf16[128,1088]{1,0:T(8,128)(2,1)S(1)}, bf16[128,1088]{1,0:T(8,128)(2,1)S(1)}, u32[]{:S(2)}, u32[]{:S(2)}) collective-permute-start(bf16[128,1088]{1,0:T(8,128)(2,1)S(1)} %bitcast.42), channel_id=1, source_target_pairs={{0,2},{1,3},{2,0},{3,1},{4,6},{5,7},{6,4},{7,5},{8,10},{9,11},{10,... | collective-permute-start | bytes 835592 | tf_op jit(solution)/shard_map/ppermute | solution.py:693
  22.0 16.1 %collective-permute-start.1 = (bf16[128,1088]{1,0:T(8,128)(2,1)S(1)}, bf16[128,1088]{1,0:T(8,128)(2,1)S(1)}, u32[]{:S(2)}, u32[]{:S(2)}) collective-permute-start(bf16[128,1088]{1,0:T(8,128)(2,1)S(1)} %bitcast.43), channel_id=1, source_target_pairs={{0,3},{1,0},{2,1},{3,2},{4,7},{5,4},{6,5},{7,6},{8,11},{9,8},{10,9... | collective-permute-start | bytes 835592 | tf_op jit(solution)/shard_map/ppermute | solution.py:693
  22.7 15.4 %collective-permute-start = (bf16[128,1088]{1,0:T(8,128)(2,1)S(1)}, bf16[128,1088]{1,0:T(8,128)(2,1)}, u32[]{:S(2)}, u32[]{:S(2)}) collective-permute-start(bf16[128,1088]{1,0:T(8,128)(2,1)S(1)} %bitcast.44), channel_id=1, source_target_pairs={{0,1},{1,2},{2,3},{3,0},{4,5},{5,6},{6,7},{7,4},{8,9},{9,10},{10,1... | collective-permute-start | bytes 835592 | tf_op jit(solution)/shard_map/ppermute | solution.py:693
  213.8 35.1 %collective-permute-start.5 = (bf16[3,128,1152]{2,1,0:T(8,128)(2,1)}, bf16[3,128,1152]{2,1,0:T(8,128)(2,1)S(1)}, u32[]{:S(2)}, u32[]{:S(2)}) collective-permute-start(bf16[3,128,1152]{2,1,0:T(8,128)(2,1)} %get-tuple-element.136), channel_id=1, source_target_pairs={{0,1},{1,2},{2,3},{3,0},{4,5},{5,6},{6,7},{7,4},{8,9},{9,10},{10,1... | collective-permute-start | bytes 2654216 | tf_op jit(solution)/shard_map/ppermute | solution.py:693
  214.7 27.9 %collective-permute-start.4 = (bf16[128,1088]{1,0:T(8,128)(2,1)}, bf16[128,1088]{1,0:T(8,128)(2,1)S(1)}, u32[]{:S(2)}, u32[]{:S(2)}) collective-permute-start(bf16[128,1088]{1,0:T(8,128)(2,1)} %get-tuple-element.121.refs_3_), channel_id=1, source_target_pairs={{64,0},{65,1},{66,2},{67,3},{68,4},{69,5},{70,6},{71,7},{72,8},{73... | collective-permute-start | bytes 835592 | tf_op jit(solution)/shard_map/ppermute | solution.py:766
  216.0 63.3 %collective-permute-start.6 = (bf16[3,128,1152]{2,1,0:T(8,128)(2,1)}, bf16[3,128,1152]{2,1,0:T(8,128)(2,1)S(1)}, u32[]{:S(2)}, u32[]{:S(2)}) collective-permute-start(bf16[3,128,1152]{2,1,0:T(8,128)(2,1)} %get-tuple-element.138), channel_id=1, source_target_pairs={{0,3},{1,0},{2,1},{3,2},{4,7},{5,4},{6,5},{7,6},{8,11},{9,8},{10,9... | collective-permute-start | bytes 2654216 | tf_op jit(solution)/shard_map/ppermute | solution.py:693
  218.9 60.4 %collective-permute-start.7 = (bf16[3,128,1152]{2,1,0:T(8,128)(2,1)}, bf16[3,128,1152]{2,1,0:T(8,128)(2,1)S(1)}, u32[]{:S(2)}, u32[]{:S(2)}) collective-permute-start(bf16[3,128,1152]{2,1,0:T(8,128)(2,1)} %get-tuple-element.139), channel_id=1, source_target_pairs={{0,2},{1,3},{2,0},{3,1},{4,6},{5,7},{6,4},{7,5},{8,10},{9,11},{10,... | collective-permute-start | bytes 2654216 | tf_op jit(solution)/shard_map/ppermute | solution.py:693
  242.7 36.6 %collective-permute-start.9 = (bf16[128,1088]{1,0:T(8,128)(2,1)S(1)}, bf16[128,1088]{1,0:T(8,128)(2,1)S(1)}, u32[]{:S(2)}, u32[]{:S(2)}) collective-permute-start(bf16[128,1088]{1,0:T(8,128)(2,1)S(1)} %collective-permute-done.4.refs_16_.refs_4_), channel_id=1, source_target_pairs={{0,3},{1,0},{2,1},{3,2},{4,7},{5,4},{6,5},{7,6},{8,11},{9,8},{10,9... | collective-permute-start | bytes 835592 | tf_op jit(solution)/shard_map/ppermute | solution.py:697
  247.0 32.3 %collective-permute-start.8 = (bf16[128,1088]{1,0:T(8,128)(2,1)S(1)}, bf16[128,1088]{1,0:T(8,128)(2,1)S(1)}, u32[]{:S(2)}, u32[]{:S(2)}) collective-permute-start(bf16[128,1088]{1,0:T(8,128)(2,1)S(1)} %collective-permute-done.4.refs_16_.refs_4_), channel_id=1, source_target_pairs={{0,1},{1,2},{2,3},{3,0},{4,5},{5,6},{6,7},{7,4},{8,9},{9,10},{10,1... | collective-permute-start | bytes 835592 | tf_op jit(solution)/shard_map/ppermute | solution.py:697
  248.9 30.4 %collective-permute-start.10 = (bf16[128,1088]{1,0:T(8,128)(2,1)S(1)}, bf16[128,1088]{1,0:T(8,128)(2,1)S(1)}, u32[]{:S(2)}, u32[]{:S(2)}) collective-permute-start(bf16[128,1088]{1,0:T(8,128)(2,1)S(1)} %collective-permute-done.4.refs_16_.refs_4_), channel_id=1, source_target_pairs={{0,2},{1,3},{2,0},{3,1},{4,6},{5,7},{6,4},{7,5},{8,10},{9,11},{10,... | collective-permute-start | bytes 835592 | tf_op jit(solution)/shard_map/ppermute | solution.py:697
  279.4 21.8 %collective-permute-start.11 = (bf16[2,128,1152]{2,1,0:T(8,128)(2,1)}, bf16[2,128,1152]{2,1,0:T(8,128)(2,1)S(1)}, u32[]{:S(2)}, u32[]{:S(2)}) collective-permute-start(bf16[2,128,1152]{2,1,0:T(8,128)(2,1)} %get-tuple-element.144), channel_id=1, source_target_pairs={{0,1},{1,2},{2,3},{3,0},{4,5},{5,6},{6,7},{7,4},{8,9},{9,10},{10,1... | collective-permute-start | bytes 1769480 | tf_op jit(solution)/shard_map/ppermute | solution.py:693
  281.1 20.1 %collective-permute-start.12 = (bf16[2,128,1152]{2,1,0:T(8,128)(2,1)}, bf16[2,128,1152]{2,1,0:T(8,128)(2,1)S(1)}, u32[]{:S(2)}, u32[]{:S(2)}) collective-permute-start(bf16[2,128,1152]{2,1,0:T(8,128)(2,1)} %get-tuple-element.145), channel_id=1, source_target_pairs={{0,3},{1,0},{2,1},{3,2},{4,7},{5,4},{6,5},{7,6},{8,11},{9,8},{10,9... | collective-permute-start | bytes 1769480 | tf_op jit(solution)/shard_map/ppermute | solution.py:693
  282.7 18.5 %collective-permute-start.13 = (bf16[2,128,1152]{2,1,0:T(8,128)(2,1)}, bf16[2,128,1152]{2,1,0:T(8,128)(2,1)S(1)}, u32[]{:S(2)}, u32[]{:S(2)}) collective-permute-start(bf16[2,128,1152]{2,1,0:T(8,128)(2,1)} %get-tuple-element.146), channel_id=1, source_target_pairs={{0,2},{1,3},{2,0},{3,1},{4,6},{5,7},{6,4},{7,5},{8,10},{9,11},{10,... | collective-permute-start | bytes 1769480 | tf_op jit(solution)/shard_map/ppermute | solution.py:693
  301.2 17.1 %collective-permute-start.14 = (bf16[4,72,1152]{2,1,0:T(8,128)(2,1)}, bf16[4,72,1152]{2,1,0:T(8,128)(2,1)S(1)}, u32[]{:S(2)}, u32[]{:S(2)}) collective-permute-start(bf16[4,72,1152]{2,1,0:T(8,128)(2,1)} %get-tuple-element.167), channel_id=1, source_target_pairs={{0,8},{4,12},{8,0},{12,4},{1,9},{5,13},{9,1},{13,5},{2,10},{6,14},... | collective-permute-start | bytes 1990664 | tf_op jit(solution)/shard_map/ppermute | solution.py:693
  304.3 20.9 %collective-permute-start.18 = (bf16[4,72,1152]{2,1,0:T(8,128)(2,1)}, bf16[4,72,1152]{2,1,0:T(8,128)(2,1)S(1)}, u32[]{:S(2)}, u32[]{:S(2)}) collective-permute-start(bf16[4,72,1152]{2,1,0:T(8,128)(2,1)} %get-tuple-element.183), channel_id=1, source_target_pairs={{0,4},{4,8},{8,12},{12,0},{1,5},{5,9},{9,13},{13,1},{2,6},{6,10},{... | collective-permute-start | bytes 1990664 | tf_op jit(solution)/shard_map/ppermute | solution.py:693
  304.9 20.5 %collective-permute-start.19 = (bf16[4,72,1152]{2,1,0:T(8,128)(2,1)}, bf16[4,72,1152]{2,1,0:T(8,128)(2,1)S(1)}, u32[]{:S(2)}, u32[]{:S(2)}) collective-permute-start(bf16[4,72,1152]{2,1,0:T(8,128)(2,1)} %get-tuple-element.184), channel_id=1, source_target_pairs={{0,12},{4,0},{8,4},{12,8},{1,13},{5,1},{9,5},{13,9},{2,14},{6,2},{... | collective-permute-start | bytes 1990664 | tf_op jit(solution)/shard_map/ppermute | solution.py:693
  325.4 12.2 %collective-permute-start.20 = (bf16[4,72,768]{2,1,0:T(8,128)(2,1)}, bf16[4,72,768]{2,1,0:T(8,128)(2,1)S(1)}, u32[]{:S(2)}, u32[]{:S(2)}) collective-permute-start(bf16[4,72,768]{2,1,0:T(8,128)(2,1)} %get-tuple-element.194), channel_id=1, source_target_pairs={{0,8},{4,12},{8,0},{12,4},{1,9},{5,13},{9,1},{13,5},{2,10},{6,14},... | collective-permute-start | bytes 1327112 | tf_op jit(solution)/shard_map/ppermute | solution.py:693
  327.5 24.4 %collective-permute-start.15 = (bf16[4,72,1536]{2,1,0:T(8,128)(2,1)}, bf16[4,72,1536]{2,1,0:T(8,128)(2,1)S(1)}, u32[]{:S(2)}, u32[]{:S(2)}) collective-permute-start(bf16[4,72,1536]{2,1,0:T(8,128)(2,1)} %get-tuple-element.178), channel_id=1, source_target_pairs={{0,32},{16,48},{32,0},{48,16},{1,33},{17,49},{33,1},{49,17},{2,34}... | collective-permute-start | bytes 2654216 | tf_op jit(solution)/shard_map/ppermute | solution.py:693
  331.0 36.8 %collective-permute-start.16 = (bf16[4,72,1536]{2,1,0:T(8,128)(2,1)}, bf16[4,72,1536]{2,1,0:T(8,128)(2,1)S(1)}, u32[]{:S(2)}, u32[]{:S(2)}) collective-permute-start(bf16[4,72,1536]{2,1,0:T(8,128)(2,1)} %get-tuple-element.179), channel_id=1, source_target_pairs={{0,16},{16,32},{32,48},{48,0},{1,17},{17,33},{33,49},{49,1},{2,18}... | collective-permute-start | bytes 2654216 | tf_op jit(solution)/shard_map/ppermute | solution.py:693
  331.6 36.6 %collective-permute-start.17 = (bf16[4,72,1536]{2,1,0:T(8,128)(2,1)}, bf16[4,72,1536]{2,1,0:T(8,128)(2,1)S(1)}, u32[]{:S(2)}, u32[]{:S(2)}) collective-permute-start(bf16[4,72,1536]{2,1,0:T(8,128)(2,1)} %get-tuple-element.180), channel_id=1, source_target_pairs={{0,48},{16,0},{32,16},{48,32},{1,49},{17,1},{33,17},{49,33},{2,50}... | collective-permute-start | bytes 2654216 | tf_op jit(solution)/shard_map/ppermute | solution.py:693
  375.5 17.0 %collective-permute-start.26 = (bf16[72,1920]{1,0:T(8,128)(2,1)}, bf16[72,1920]{1,0:T(8,128)(2,1)S(1)}, u32[]{:S(2)}, u32[]{:S(2)}) collective-permute-start(bf16[72,1920]{1,0:T(8,128)(2,1)} %get-tuple-element.202), channel_id=1, source_target_pairs={{0,16},{16,32},{32,48},{48,0},{1,17},{17,33},{33,49},{49,1},{2,18}... | collective-permute-start | bytes 829448 | tf_op jit(solution)/shard_map/ppermute | solution.py:693
  377.3 15.1 %collective-permute-start.27 = (bf16[72,1920]{1,0:T(8,128)(2,1)}, bf16[72,1920]{1,0:T(8,128)(2,1)S(1)}, u32[]{:S(2)}, u32[]{:S(2)}) collective-permute-start(bf16[72,1920]{1,0:T(8,128)(2,1)} %get-tuple-element.203), channel_id=1, source_target_pairs={{0,48},{16,0},{32,16},{48,32},{1,49},{17,1},{33,17},{49,33},{2,50}... | collective-permute-start | bytes 829448 | tf_op jit(solution)/shard_map/ppermute | solution.py:693
  378.8 13.7 %collective-permute-start.28 = (bf16[72,1920]{1,0:T(8,128)(2,1)}, bf16[72,1920]{1,0:T(8,128)(2,1)S(1)}, u32[]{:S(2)}, u32[]{:S(2)}) collective-permute-start(bf16[72,1920]{1,0:T(8,128)(2,1)} %get-tuple-element.204), channel_id=1, source_target_pairs={{0,32},{16,48},{32,0},{48,16},{1,33},{17,49},{33,1},{49,17},{2,34}... | collective-permute-start | bytes 829448 | tf_op jit(solution)/shard_map/ppermute | solution.py:693
  (50 other events, 742.8 us)
Sparse Core Ops, SparseCore 0:
  16.9 152.6 all-gather.1

commit v5 on v4

--- a/solution.py
+++ b/solution.py
@@ -540,13 +540,11 @@
             store(x, y, jnp.concatenate(rows, axis=0).astype(BF))
 
 
-def send_blocks(held, first, outs, sems, cols=None):
+def send_blocks(held, first, outs, sems):
     copies = []
     for d in range(4):
-        source, target = held.at[lax.rem(first + d, 4)], outs[d]
-        if cols is not None:
-            source, target = source.at[:, :, cols], target.at[:, :, cols]
-        copies.append(pltpu.make_async_copy(source, target, sems.at[d]))
+        source = held.at[lax.rem(first + d, 4)]
+        copies.append(pltpu.make_async_copy(source, outs[d], sems.at[d]))
         copies[-1].start()
     return copies
 
@@ -587,30 +585,37 @@
         copy.wait()
 
 
-def products_kernel(place, *refs):
+def up_products_kernel(place, *refs):
+    early, late, outs = refs[:4], refs[4:8], refs[8:12]
+    held, a_held, b_held, sems = refs[12:]
+    a = load([e.at[0] for e in early], a_held, sems.at[0])
+    b = load([v.at[0] for v in late], b_held, sems.at[1])
+
+    def store(x, y, v):
+        held[x, y] = v
+
+    product(a(), wide(b()), store)
+    for copy in send_blocks(held, place[0], outs, sems.at[2]):
+        copy.wait()
+
+
+def attn_products_kernel(place, *refs):
     early, late, small, outs = refs[:4], refs[4:8], refs[8], refs[9:17]
-    first, second, held, sems = refs[17:]
-    a_up = load([e.at[0] for e in early], held.at[0], sems.at[0])
-    b_up = load([v.at[0] for v in late], held.at[1], sems.at[1])
-    a_attn = load([e.at[2] for e in early], held.at[2], sems.at[2])
-    b_attn = load([v.at[1] for v in late], held.at[3], sems.at[3])
+    first, second, a_held, b_held, sems = refs[17:]
+    a = load([e.at[2] for e in early], a_held, sems.at[0])
+    b = load([v.at[1] for v in late], b_held, sems.at[1])
     slot = lax.broadcasted_iota(jnp.int32, (16, PAD), 1) - D
     unit = (slot == lax.broadcasted_iota(jnp.int32, (16, PAD), 0)).astype(F32).astype(BF)
 
-    def store_up(x, y, v):
-        first[x, y, :, :PAD] = v
-
-    def store_attn(x, y, v):
-        first[x, y, :, PAD:] = v[:, :PART]
+    def store(x, y, v):
+        first[x, y] = v[:, :PART]
         second[y, x] = v[:, PART:]
 
-    product(a_up(), wide(b_up()), store_up)
-    copies = send_blocks(first, place[0], outs[:4], sems.at[4], pl.ds(0, PAD))
-    a = jnp.concatenate([a_attn(), small[...].astype(BF)], axis=0)
-    b = jnp.concatenate([wide(b_attn()), unit], axis=0)
-    product(a, b, store_attn)
-    copies += send_blocks(first, place[0], outs[:4], sems.at[5], pl.ds(PAD, PART))
-    copies += send_blocks(second, place[1], outs[4:], sems.at[6])
+    a = jnp.concatenate([a(), small[...].astype(BF)], axis=0)
+    b = jnp.concatenate([wide(b()), unit], axis=0)
+    product(a, b, store)
+    copies = send_blocks(first, place[0], outs[:4], sems.at[2])
+    copies += send_blocks(second, place[1], outs[4:], sems.at[3])
     for copy in copies:
         copy.wait()
 
@@ -620,10 +625,10 @@
 
 
 def first_sum_kernel(place, *refs):
-    given, outs, held, sems = refs[:12], refs[12:20], refs[20:23], refs[23]
+    given, outs, held, sems = refs[:16], refs[16:24], refs[24:28], refs[28]
     copies = {}
     for d in range(4):
-        for g, other in ((1, 0), (0, 1), (2, 0)):
+        for g, other in ((1, 0), (0, 1), (3, 0), (2, 1)):
             i = lax.rem(place[other] + d, 4)
             copies[g, d] = [
                 pltpu.make_async_copy(given[4 * g + k].at[i], held[g].at[d, k], sems.at[g, d, k])
@@ -632,7 +637,7 @@
             for copy in copies[g, d]:
                 copy.start()
     for d in range(4):
-        for g, h, start in ((1, 1, 0), (0, 0, 0), (2, 1, PAD)):
+        for g, h, start in ((1, 1, 0), (0, 0, 0), (3, 1, PAD), (2, 0, PAD)):
             for copy in copies[g, d]:
                 copy.wait()
             summed = total([held[g][d, k] for k in range(4)]).astype(BF)
@@ -693,10 +698,6 @@
     return lax.ppermute(v, axis, [(i, (i + d) % 4) for i in range(4)])
 
 
-def ring_of_first(v, d):
-    return lax.ppermute(v, ("section", "z"), [(i, (i + d) % 4) for i in range(4)])
-
-
 def restore_kernel(place, order, result, dx, acts, grads):
     acts[...] = dot_t(result[...], order[:D]).astype(BF)
     grads[...] = dot_t(dx[...], order[:D]).astype(BF)
@@ -765,9 +766,9 @@
     top = call("both", x=arrived, grad=cot, old=first)
     coming = lax.ppermute(top["dx"], "section", [(1, 0)])
     early = [top["early0"]] + [ring(top[f"early{d}"], "z", d) for d in (1, 3, 2)]
-    branches = [coming] + [ring_of_first(coming, d) for d in (1, 3)]
+    branches = [coming] + [ring(coming, "z", d) for d in (1, 3)]
     early[1], held = lax.optimization_barrier((early[1], coming))
-    branches.append(ring_of_first(held, 2))
+    branches.append(ring(held, "z", 2))
     kept = {k: first[k] for k in KEPT}
     old = {**{k: top[k] for k in (*GRADS, *LATE)}, **kept}
     bwd = call("bwd", x=x0, grad=coming, old=old)
@@ -787,33 +788,44 @@
         far_out=True,
     )
     late, down = lax.optimization_barrier((late, down))
-    small, down = lax.optimization_barrier((bwd["small"], down))
     down = [down[0]] + [ring(down[d], "y", d) for d in (2, 1, 3)]
-    out = local_call(
-        products_kernel,
-        "products",
+    up = local_call(
+        up_products_kernel,
+        "up_products",
         place,
-        [small],
-        [block(WIDE[0])] * 4 + [block(PAD - PART)] * 4,
-        [vmem((4, 4, CHUNK, width), BF) for width in (WIDE[0], PAD - PART)]
-        + [vmem((4, 4) + WIDEROW, BF), sem((7, 4))],
+        [],
+        [block(PAD)] * 4,
+        [vmem((4, 4, CHUNK, PAD), BF)] + [vmem((4,) + WIDEROW, BF)] * 2 + [sem((3, 4))],
         far=[*early, *late],
         far_out=True,
     )
+    up = [up[0]] + [ring(up[d], "x", d) for d in (2, 1, 3)]
+    out = local_call(
+        attn_products_kernel,
+        "attn_products",
+        place,
+        [bwd["small"]],
+        [block(PART)] * 4 + [block(PAD - PART)] * 4,
+        [vmem((4, 4, CHUNK, width), BF) for width in (PART, PAD - PART)]
+        + [vmem((4,) + WIDEROW, BF)] * 2
+        + [sem((4, 4))],
+        far=[*early, *late],
+        far_out=True,
+    )
     xs, ys = out[:4], out[4:]
-    down[1], xs = lax.optimization_barrier((down[1], xs))
-    down, ys = lax.optimization_barrier((down, ys))
-    up = [xs[0]] + [ring(xs[d], "x", d) for d in (2, 1, 3)]
-    attn = [ys[0]] + [ring(ys[d], "y", d) for d in (2, 1, 3)]
+    up[1], xs = lax.optimization_barrier((up[1], xs))
+    down[1], ys = lax.optimization_barrier((down[1], ys))
+    attn_x = [xs[0]] + [ring(xs[d], "x", d) for d in (2, 1, 3)]
+    attn_y = [ys[0]] + [ring(ys[d], "y", d) for d in (2, 1, 3)]
     out = local_call(
         first_sum_kernel,
         "first_sum",
         place,
         [],
         [((CHUNK, WIDE[h]), BF) for h in (0, 1) for _ in range(4)],
-        [vmem((4, 4, CHUNK, width), BF) for width in (WIDE[0], PAD, PAD - PART)]
-        + [sem((3, 4, 4))],
-        far=[*up, *down, *attn],
+        [vmem((4, 4, CHUNK, width), BF) for width in (PAD, PAD, PART, PAD - PART)]
+        + [sem((4, 4, 4))],
+        far=[*up, *down, *attn_x, *attn_y],
     )
     got = []
     for h, axis in ((0, "y"), (1, "x")):

time: 423 us -> 413 us (0.976)
  waiting for transfers between devices: 228 us -> 208 us
  starting transfers between devices: 57.4 us -> 64.3 us
    ppermute x27 -> x33, waiting for transfers between devices: 72.6 us -> 52 us  [ring(): return lax.ppermute(v, axis, [(i, (i + d) % 4) for i in range(4)])]
    ppermute x27 -> x33, starting transfers between devices: 44.1 us -> 61.7 us  [ring(): return lax.ppermute(v, axis, [(i, (i + d) % 4) for i in range(4)])]
    ppermute x3 -> x0, starting transfers between devices: 10.6 us -> none  [ring_of_first(): lax.ppermute(v, ('section', 'z'), [(i, (i + d) % 4) for i in range(4)])]
    pallas_call x6 -> x7, Pallas kernels: 32.1 us -> 35.9 us  [local_call(): pl.pallas_call(kernel, in_specs=[pl.BlockSpec(memory_space=pltpu.SMEM)] +...]
  transfers between devices with their start and end apart: 33 -> 36, of which waited for: 19 -> 17; matrix products, arithmetic and copies ran while one was open for 2% -> 2% of each run, Pallas kernels for 10% -> 12%
where the time goes in v5:
time: 413 us; the launch traced here: 412 us
  waiting for transfers between devices  208 us (50%)
  Pallas kernels  103 us (25%)
  starting transfers between devices  64.3 us (16%)
  between operations  14.9 us (4%)
  local copies, waits for them, and re-layouts  12.9 us (3%)
  matrix products  7.24 us (2%)
    all_gather x1, waiting for transfers between devices, body(): whole = lax.all_gather(sent, ('x', 'y', 'z'), axis=0, tiled=True)  132 us
    ppermute x33, starting transfers between devices, ring(): return lax.ppermute(v, axis, [(i, (i + d) % 4) for i in range(4)])  61.7 us
    pallas_call x3, Pallas kernels, layer_call(): pl.pallas_call(kernel, in_specs=[pl.BlockSpec(memory_space=pltpu.SMEM)] +...  60.2 us
    ppermute x33, waiting for transfers between devices, ring(): return lax.ppermute(v, axis, [(i, (i + d) % 4) for i in range(4)])  52 us
    pallas_call x7, Pallas kernels, local_call(): pl.pallas_call(kernel, in_specs=[pl.BlockSpec(memory_space=pltpu.SMEM)] +...  35.9 us
    ppermute x1, waiting for transfers between devices, body(): coming = lax.ppermute(top['dx'], 'section', [(1, 0)])  22.5 us
  transfers between devices with their start and end apart: 36, of which 17 were waited for; matrix products, arithmetic and copies ran while one was open for 2% of the time, Pallas kernels for 12%

profile of v5, /device:TPU:0, one launch (start us, length us, event | category | flops | bytes accessed | tf_op | source)
XLA Modules:
  0.0 411.9 jit_solution(13191982978600366276)
XLA Ops:
  17.9 4.0 collective-permute-start.2
  30.1 7.9 %collective-permute-done.1.refs_10_ = bf16[128,1088]{1,0:T(8,128)(2,1)S(1)} collective-permute-done((bf16[128,1088]{1,0:T(8,128)(2,1)S(1)}, bf16[128,1088]{1,0:T(8,128)(2,1)S(1)}, u32[]{:S(2)}, u32[]{:S(2)}) %collective-permute-start.1) | collective-permute-done | bytes 278560 | tf_op jit(solution)/shard_map/ppermute | solution.py:698
  38.1 131.6 %all-gather.2.cloned.1.call-done.whole.refs_0_ = bf16[1024,14720]{1,0:T(8,128)(2,1)} async-done(((bf16[16,14720]{1,0:T(8,128)(2,1)}), bf16[1024,14720]{1,0:T(8,128)(2,1)}) %all-gather.2.cloned.1.call-update) | async-done | bytes 30146576 | tf_op jit(solution)/shard_map/all_gather | solution.py:737
  169.6 6.5 %unpack.1 = (bf16[64,14336]{1,0:T(8,128)(2,1)}, f32[16,1088]{1,0:T(8,128)}, f32[16,1152]{1,0:T(8,128)}) custom-call(bf16[1024,14720]{1,0:T(8,128)(2,1)} %all-gather.2.cloned.1.call-done.whole.refs_0_, bf16[1024,1024]{1,0:T(8,128)(2,1)} %constant.56.clone.refs_0_, bf16[16,256]{1,0:T(8,128)(2,1)} %constant.51.clone.refs_1_, ...), custom_call_target="tpu_custom_call" | custom-call | tf_op jit(solution)/shard_map/unpack/pallas_call | solution.py:126
  176.1 27.9 %layer_fwd.1 = (bf16[128,1088]{1,0:T(8,128)(2,1)}, bf16[3,128,1152]{2,1,0:T(8,128)(2,1)}, bf16[3,128,1152]{2,1,0:T(8,128)(2,1)}, bf16[3,128,1152]{2,1,0:T(8,128)...) custom-call(s32[4]{0:T(128)} %pad_add_fusion.place_ref.place, ...), custom_call_target="tpu_custom_call" | custom-call | flops 4000000000 | bytes 30081024 | tf_op jit(solution)/shard_map/layer_fwd/pallas_call | solution.py:484
  207.4 6.4 %layer_both.1 = (bf16[128,1088]{1,0:T(8,128)(2,1)}, bf16[128,1088]{1,0:T(8,128)(2,1)}, f32[16,1088]{1,0:T(8,128)}, bf16[3,128,1152]{2,1,0:T(8,128)(2,1)}, bf16[3...) custom-call(s32[4]{0:T(128)} %pad_add_fusion.place_ref.place, ...), custom_call_target="tpu_custom_call" | custom-call | flops 12000000000 | bytes 30081024 | tf_op jit(solution)/shard_map/layer_both/pallas_call | solution.py:484
  220.1 22.5 %collective-permute-done.4.refs_16_.refs_4_ = bf16[128,1088]{1,0:T(8,128)(2,1)S(1)} collective-permute-done((bf16[128,1088]{1,0:T(8,128)(2,1)}, bf16[128,1088]{1,0:T(8,128)(2,1)S(1)}, u32[]{:S(2)}, u32[]{:S(2)}) %collective-permute-start.4) | collective-permute-done | bytes 278560 | tf_op jit(solution)/shard_map/ppermute | solution.py:767
  247.6 25.9 %layer_bwd.1 = (bf16[128,1088]{1,0:T(8,128)(2,1)}, f32[16,1088]{1,0:T(8,128)}, bf16[2,128,1152]{2,1,0:T(8,128)(2,1)}, bf16[2,128,1152]{2,1,0:T(8,128)(2,1)}, bf1...) custom-call(s32[4]{0:T(128)} %pad_add_fusion.place_ref.place, ...), custom_call_target="tpu_custom_call" | custom-call | flops 8000000000 | bytes 30081024 | tf_op jit(solution)/shard_map/layer_bwd/pallas_call | solution.py:484
  277.5 5.7 %down_products.1 = (bf16[4,72,1152]{2,1,0:T(8,128)(2,1)}, bf16[4,72,1152]{2,1,0:T(8,128)(2,1)}, bf16[4,72,1152]{2,1,0:T(8,128)(2,1)}, bf16[4,72,1152]{2,1,0:T(8,128)(2,1)}) custom-call(s32[4]{0:T(128)} %pad_add_fusion.place_ref.place, bf16[3,128,1152]{2,1,0:T(8,128)(2,1)} %get-tuple-element.138.refs_0_, bf16[3,128,1152]{2,1,0:T(8,128)(2,1)} %copy-done.2, ...), custom_call_target="tpu_custom_call" | custom-call | tf_op jit(solution)/shard_map/down_products/pallas_call | solution.py:521
  283.2 7.8 %collective-permute-done.11.refs_5_ = bf16[2,128,1152]{2,1,0:T(8,128)(2,1)S(1)} collective-permute-done((bf16[2,128,1152]{2,1,0:T(8,128)(2,1)}, bf16[2,128,1152]{2,1,0:T(8,128)(2,1)S(1)}, u32[]{:S(2)}, u32[]{:S(2)}) %collective-permute-start.11) | collective-permute-done | bytes 589856 | tf_op jit(solution)/shard_map/ppermute | solution.py:698
  291.0 8.8 %collective-permute-done.13.refs_7_ = bf16[2,128,1152]{2,1,0:T(8,128)(2,1)S(1)} collective-permute-done((bf16[2,128,1152]{2,1,0:T(8,128)(2,1)}, bf16[2,128,1152]{2,1,0:T(8,128)(2,1)S(1)}, u32[]{:S(2)}, u32[]{:S(2)}) %collective-permute-start.13) | collective-permute-done | bytes 589856 | tf_op jit(solution)/shard_map/ppermute | solution.py:698
  303.0 5.6 %up_products.1 = (bf16[4,72,1152]{2,1,0:T(8,128)(2,1)}, bf16[4,72,1152]{2,1,0:T(8,128)(2,1)}, bf16[4,72,1152]{2,1,0:T(8,128)(2,1)}, bf16[4,72,1152]{2,1,0:T(8,128)(2,1)}) custom-call(s32[4]{0:T(128)} %pad_add_fusion.place_ref.place, bf16[3,128,1152]{2,1,0:T(8,128)(2,1)} %get-tuple-element.138.refs_0_, bf16[3,128,1152]{2,1,0:T(8,128)(2,1)} %copy-done.2, ...), custom_call_target="tpu_custom_call" | custom-call | tf_op jit(solution)/shard_map/up_products/pallas_call | solution.py:521
  308.6 3.8 collective-permute-start.14
  316.2 4.2 %collective-permute-start.16 = (bf16[4,72,1152]{2,1,0:T(8,128)(2,1)}, bf16[4,72,1152]{2,1,0:T(8,128)(2,1)S(1)}, u32[]{:S(2)}, u32[]{:S(2)}) collective-permute-start(bf16[4,72,1152]{2,1,0:T(8,128)(2,1)} %get-tuple-element.171), channel_id=1, source_target_pairs={{0,48},{16,0},{32,16},{48,32},{1,49},{17,1},{33,17},{49,33},{2,50}... | collective-permute-start | bytes 1990664 | tf_op jit(solution)/shard_map/ppermute | solution.py:698
  320.3 6.0 %attn_products.1 = (bf16[4,72,384]{2,1,0:T(8,128)(2,1)}, bf16[4,72,384]{2,1,0:T(8,128)(2,1)}, bf16[4,72,384]{2,1,0:T(8,128)(2,1)}, bf16[4,72,384]{2,1,0:T(8,128)...) custom-call(s32[4]{0:T(128)} %pad_add_fusion.place_ref.place, ...), custom_call_target="tpu_custom_call" | custom-call | tf_op jit(solution)/shard_map/attn_products/pallas_call | solution.py:521
  326.6 3.8 collective-permute-start.23
  330.4 4.1 %collective-permute-done.18.refs_6_ = bf16[4,72,1152]{2,1,0:T(8,128)(2,1)S(1)} collective-permute-done((bf16[4,72,1152]{2,1,0:T(8,128)(2,1)}, bf16[4,72,1152]{2,1,0:T(8,128)(2,1)S(1)}, u32[]{:S(2)}, u32[]{:S(2)}) %collective-permute-start.18) | collective-permute-done | bytes 663584 | tf_op jit(solution)/shard_map/ppermute | solution.py:698
  338.9 6.0 %collective-permute-done.15.refs_2_ = bf16[4,72,1152]{2,1,0:T(8,128)(2,1)S(1)} collective-permute-done((bf16[4,72,1152]{2,1,0:T(8,128)(2,1)}, bf16[4,72,1152]{2,1,0:T(8,128)(2,1)S(1)}, u32[]{:S(2)}, u32[]{:S(2)}) %collective-permute-start.15) | collective-permute-done | bytes 663584 | tf_op jit(solution)/shard_map/ppermute | solution.py:698
  349.5 5.6 %collective-permute-done.21.refs_10_ = bf16[4,72,384]{2,1,0:T(8,128)(2,1)S(1)} collective-permute-done((bf16[4,72,384]{2,1,0:T(8,128)(2,1)}, bf16[4,72,384]{2,1,0:T(8,128)(2,1)S(1)}, u32[]{:S(2)}, u32[]{:S(2)}) %collective-permute-start.21) | collective-permute-done | bytes 221216 | tf_op jit(solution)/shard_map/ppermute | solution.py:698
  358.1 5.9 %first_sum.1 = (bf16[72,1536]{1,0:T(8,128)(2,1)}, bf16[72,1536]{1,0:T(8,128)(2,1)}, bf16[72,1536]{1,0:T(8,128)(2,1)}, bf16[72,1536]{1,0:T(8,128)(2,1)}, bf16[72,...) custom-call(s32[4]{0:T(128)} %pad_add_fusion.place_ref.place, ...), custom_call_target="tpu_custom_call" | custom-call | tf_op jit(solution)/shard_map/first_sum/pallas_call | solution.py:521
  373.1 7.5 %collective-permute-done.27.refs_2_ = bf16[72,1536]{1,0:T(8,128)(2,1)S(1)} collective-permute-done((bf16[72,1536]{1,0:T(8,128)(2,1)}, bf16[72,1536]{1,0:T(8,128)(2,1)S(1)}, u32[]{:S(2)}, u32[]{:S(2)}) %collective-permute-start.27) | collective-permute-done | bytes 221216 | tf_op jit(solution)/shard_map/ppermute | solution.py:698
  386.1 3.9 collective-permute-start.33
  390.6 4.3 %restore.1 = (bf16[128,1088]{1,0:T(8,128)(2,1)}, bf16[128,1088]{1,0:T(8,128)(2,1)}) custom-call(s32[4]{0:T(128)} %pad_add_fusion.place_ref.place, bf16[1152,1088]{1,0:T(8,128)(2,1)} %constant.49.clone.refs_2_.order.refs_1_, bf16[128,1088]{1,0:T(8,128)(2,1)} %get-tuple-element.116.result, bf16[128,1088]{1,0:T(8,128)(2,1)} %get-tuple-element.126.dx), custom_call_target="tpu_custom_call" | custom-call | tf_op jit(solution)/shard_map/restore/pallas_call | solution.py:521
  396.5 5.5 %owners.1 = (f32[17,1,4352]{2,1,0:T(1,128)}, f32[68,1,1088]{2,1,0:T(1,128)}, f32[17,1,1088]{2,1,0:T(1,128)}, f32[17,1,3264]{2,1,0:T(1,128)}, f32[17,64]{1,0:T(8,128)}) custom-call(s32[4]{0:T(128)} %pad_add_fusion.place_ref.place, bf16[1088,1088]{1,0:T(8,128)(2,1)} %constant.58.clone.refs_0_, bf16[1152,1088]{1,0:T(8,128)(2,1)} %constant.49.clone.refs_2_.order.refs_1_, ...), custom_call_target="tpu_custom_call" | custom-call | tf_op jit(solution)/shard_map/owners/pallas_call | solution.py:521
  (199 shorter events, 75.9 us)
Async XLA Ops:
  7.2 162.4 %all-gather.2.cloned.1.call-start = ((), (), s32[]{:S(2)}) async-start(), calls=%async_computation | async-start | bytes 30617600 | tf_op jit(solution)/shard_map/all_gather | solution.py:737
  22.0 16.1 %collective-permute-start.1 = (bf16[128,1088]{1,0:T(8,128)(2,1)S(1)}, bf16[128,1088]{1,0:T(8,128)(2,1)S(1)}, u32[]{:S(2)}, u32[]{:S(2)}) collective-permute-start(bf16[128,1088]{1,0:T(8,128)(2,1)S(1)} %bitcast.43), channel_id=1, source_target_pairs={{0,3},{1,0},{2,1},{3,2},{4,7},{5,4},{6,5},{7,6},{8,11},{9,8},{10,9... | collective-permute-start | bytes 835592 | tf_op jit(solution)/shard_map/ppermute | solution.py:698
  22.7 15.4 %collective-permute-start = (bf16[128,1088]{1,0:T(8,128)(2,1)S(1)}, bf16[128,1088]{1,0:T(8,128)(2,1)}, u32[]{:S(2)}, u32[]{:S(2)}) collective-permute-start(bf16[128,1088]{1,0:T(8,128)(2,1)S(1)} %bitcast.44), channel_id=1, source_target_pairs={{0,1},{1,2},{2,3},{3,0},{4,5},{5,6},{6,7},{7,4},{8,9},{9,10},{10,1... | collective-permute-start | bytes 835592 | tf_op jit(solution)/shard_map/ppermute | solution.py:698
  213.9 31.2 %collective-permute-start.5 = (bf16[3,128,1152]{2,1,0:T(8,128)(2,1)}, bf16[3,128,1152]{2,1,0:T(8,128)(2,1)S(1)}, u32[]{:S(2)}, u32[]{:S(2)}) collective-permute-start(bf16[3,128,1152]{2,1,0:T(8,128)(2,1)} %get-tuple-element.130), channel_id=1, source_target_pairs={{0,1},{1,2},{2,3},{3,0},{4,5},{5,6},{6,7},{7,4},{8,9},{9,10},{10,1... | collective-permute-start | bytes 2654216 | tf_op jit(solution)/shard_map/ppermute | solution.py:698
  214.8 27.9 %collective-permute-start.4 = (bf16[128,1088]{1,0:T(8,128)(2,1)}, bf16[128,1088]{1,0:T(8,128)(2,1)S(1)}, u32[]{:S(2)}, u32[]{:S(2)}) collective-permute-start(bf16[128,1088]{1,0:T(8,128)(2,1)} %get-tuple-element.117.refs_3_), channel_id=1, source_target_pairs={{64,0},{65,1},{66,2},{67,3},{68,4},{69,5},{70,6},{71,7},{72,8},{73... | collective-permute-start | bytes 835592 | tf_op jit(solution)/shard_map/ppermute | solution.py:767
  216.1 57.5 %collective-permute-start.6 = (bf16[3,128,1152]{2,1,0:T(8,128)(2,1)}, bf16[3,128,1152]{2,1,0:T(8,128)(2,1)S(1)}, u32[]{:S(2)}, u32[]{:S(2)}) collective-permute-start(bf16[3,128,1152]{2,1,0:T(8,128)(2,1)} %get-tuple-element.132), channel_id=1, source_target_pairs={{0,3},{1,0},{2,1},{3,2},{4,7},{5,4},{6,5},{7,6},{8,11},{9,8},{10,9... | collective-permute-start | bytes 2654216 | tf_op jit(solution)/shard_map/ppermute | solution.py:698
  218.9 54.7 %collective-permute-start.7 = (bf16[3,128,1152]{2,1,0:T(8,128)(2,1)}, bf16[3,128,1152]{2,1,0:T(8,128)(2,1)S(1)}, u32[]{:S(2)}, u32[]{:S(2)}) collective-permute-start(bf16[3,128,1152]{2,1,0:T(8,128)(2,1)} %get-tuple-element.133), channel_id=1, source_target_pairs={{0,2},{1,3},{2,0},{3,1},{4,6},{5,7},{6,4},{7,5},{8,10},{9,11},{10,... | collective-permute-start | bytes 2654216 | tf_op jit(solution)/shard_map/ppermute | solution.py:698
  242.7 30.8 %collective-permute-start.9 = (bf16[128,1088]{1,0:T(8,128)(2,1)S(1)}, bf16[128,1088]{1,0:T(8,128)(2,1)S(1)}, u32[]{:S(2)}, u32[]{:S(2)}) collective-permute-start(bf16[128,1088]{1,0:T(8,128)(2,1)S(1)} %collective-permute-done.4.refs_16_.refs_4_), channel_id=1, source_target_pairs={{0,3},{1,0},{2,1},{3,2},{4,7},{5,4},{6,5},{7,6},{8,11},{9,8},{10,9... | collective-permute-start | bytes 835592 | tf_op jit(solution)/shard_map/ppermute | solution.py:698
  245.1 28.5 %collective-permute-start.8 = (bf16[128,1088]{1,0:T(8,128)(2,1)S(1)}, bf16[128,1088]{1,0:T(8,128)(2,1)S(1)}, u32[]{:S(2)}, u32[]{:S(2)}) collective-permute-start(bf16[128,1088]{1,0:T(8,128)(2,1)S(1)} %collective-permute-done.4.refs_16_.refs_4_), channel_id=1, source_target_pairs={{0,1},{1,2},{2,3},{3,0},{4,5},{5,6},{6,7},{7,4},{8,9},{9,10},{10,1... | collective-permute-start | bytes 835592 | tf_op jit(solution)/shard_map/ppermute | solution.py:698
  245.1 28.5 %collective-permute-start.10 = (bf16[128,1088]{1,0:T(8,128)(2,1)S(1)}, bf16[128,1088]{1,0:T(8,128)(2,1)S(1)}, u32[]{:S(2)}, u32[]{:S(2)}) collective-permute-start(bf16[128,1088]{1,0:T(8,128)(2,1)S(1)} %collective-permute-done.4.refs_16_.refs_4_), channel_id=1, source_target_pairs={{0,2},{1,3},{2,0},{3,1},{4,6},{5,7},{6,4},{7,5},{8,10},{9,11},{10,... | collective-permute-start | bytes 835592 | tf_op jit(solution)/shard_map/ppermute | solution.py:698
  273.6 17.3 %collective-permute-start.11 = (bf16[2,128,1152]{2,1,0:T(8,128)(2,1)}, bf16[2,128,1152]{2,1,0:T(8,128)(2,1)S(1)}, u32[]{:S(2)}, u32[]{:S(2)}) collective-permute-start(bf16[2,128,1152]{2,1,0:T(8,128)(2,1)} %get-tuple-element.143), channel_id=1, source_target_pairs={{0,1},{1,2},{2,3},{3,0},{4,5},{5,6},{6,7},{7,4},{8,9},{9,10},{10,1... | collective-permute-start | bytes 1769480 | tf_op jit(solution)/shard_map/ppermute | solution.py:698
  275.3 15.7 %collective-permute-start.12 = (bf16[2,128,1152]{2,1,0:T(8,128)(2,1)}, bf16[2,128,1152]{2,1,0:T(8,128)(2,1)S(1)}, u32[]{:S(2)}, u32[]{:S(2)}) collective-permute-start(bf16[2,128,1152]{2,1,0:T(8,128)(2,1)} %get-tuple-element.144), channel_id=1, source_target_pairs={{0,3},{1,0},{2,1},{3,2},{4,7},{5,4},{6,5},{7,6},{8,11},{9,8},{10,9... | collective-permute-start | bytes 1769480 | tf_op jit(solution)/shard_map/ppermute | solution.py:698
  276.9 22.8 %collective-permute-start.13 = (bf16[2,128,1152]{2,1,0:T(8,128)(2,1)}, bf16[2,128,1152]{2,1,0:T(8,128)(2,1)S(1)}, u32[]{:S(2)}, u32[]{:S(2)}) collective-permute-start(bf16[2,128,1152]{2,1,0:T(8,128)(2,1)} %get-tuple-element.145), channel_id=1, source_target_pairs={{0,2},{1,3},{2,0},{3,1},{4,6},{5,7},{6,4},{7,5},{8,10},{9,11},{10,... | collective-permute-start | bytes 1769480 | tf_op jit(solution)/shard_map/ppermute | solution.py:698
  299.8 16.4 %collective-permute-start.17 = (bf16[4,72,1152]{2,1,0:T(8,128)(2,1)}, bf16[4,72,1152]{2,1,0:T(8,128)(2,1)S(1)}, u32[]{:S(2)}, u32[]{:S(2)}) collective-permute-start(bf16[4,72,1152]{2,1,0:T(8,128)(2,1)} %get-tuple-element.173), channel_id=1, source_target_pairs={{0,8},{4,12},{8,0},{12,4},{1,9},{5,13},{9,1},{13,5},{2,10},{6,14},... | collective-permute-start | bytes 1990664 | tf_op jit(solution)/shard_map/ppermute | solution.py:698
  308.6 18.0 %collective-permute-start.14 = (bf16[4,72,1152]{2,1,0:T(8,128)(2,1)}, bf16[4,72,1152]{2,1,0:T(8,128)(2,1)S(1)}, u32[]{:S(2)}, u32[]{:S(2)}) collective-permute-start(bf16[4,72,1152]{2,1,0:T(8,128)(2,1)} %get-tuple-element.163), channel_id=1, source_target_pairs={{0,32},{16,48},{32,0},{48,16},{1,33},{17,49},{33,1},{49,17},{2,34}... | collective-permute-start | bytes 1990664 | tf_op jit(solution)/shard_map/ppermute | solution.py:698
  312.3 22.2 %collective-permute-start.18 = (bf16[4,72,1152]{2,1,0:T(8,128)(2,1)}, bf16[4,72,1152]{2,1,0:T(8,128)(2,1)S(1)}, u32[]{:S(2)}, u32[]{:S(2)}) collective-permute-start(bf16[4,72,1152]{2,1,0:T(8,128)(2,1)} %get-tuple-element.179), channel_id=1, source_target_pairs={{0,4},{4,8},{8,12},{12,0},{1,5},{5,9},{9,13},{13,1},{2,6},{6,10},{... | collective-permute-start | bytes 1990664 | tf_op jit(solution)/shard_map/ppermute | solution.py:698
  312.9 24.6 %collective-permute-start.19 = (bf16[4,72,1152]{2,1,0:T(8,128)(2,1)S(1)}, bf16[4,72,1152]{2,1,0:T(8,128)(2,1)S(1)}, u32[]{:S(2)}, u32[]{:S(2)}) collective-permute-start(bf16[4,72,1152]{2,1,0:T(8,128)(2,1)S(1)} %copy-done.43), channel_id=1, source_target_pairs={{0,12},{4,0},{8,4},{12,8},{1,13},{5,1},{9,5},{13,9},{2,14},{6,2},{... | collective-permute-start | bytes 1990664 | tf_op jit(solution)/shard_map/ppermute | solution.py:698
  315.6 29.3 %collective-permute-start.15 = (bf16[4,72,1152]{2,1,0:T(8,128)(2,1)}, bf16[4,72,1152]{2,1,0:T(8,128)(2,1)S(1)}, u32[]{:S(2)}, u32[]{:S(2)}) collective-permute-start(bf16[4,72,1152]{2,1,0:T(8,128)(2,1)} %get-tuple-element.170), channel_id=1, source_target_pairs={{0,16},{16,32},{32,48},{48,0},{1,17},{17,33},{33,49},{49,1},{2,18}... | collective-permute-start | bytes 1990664 | tf_op jit(solution)/shard_map/ppermute | solution.py:698
  316.2 30.0 %collective-permute-start.16 = (bf16[4,72,1152]{2,1,0:T(8,128)(2,1)}, bf16[4,72,1152]{2,1,0:T(8,128)(2,1)S(1)}, u32[]{:S(2)}, u32[]{:S(2)}) collective-permute-start(bf16[4,72,1152]{2,1,0:T(8,128)(2,1)} %get-tuple-element.171), channel_id=1, source_target_pairs={{0,48},{16,0},{32,16},{48,32},{1,49},{17,1},{33,17},{49,33},{2,50}... | collective-permute-start | bytes 1990664 | tf_op jit(solution)/shard_map/ppermute | solution.py:698
  326.6 28.9 %collective-permute-start.23 = (bf16[4,72,768]{2,1,0:T(8,128)(2,1)}, bf16[4,72,768]{2,1,0:T(8,128)(2,1)S(1)}, u32[]{:S(2)}, u32[]{:S(2)}) collective-permute-start(bf16[4,72,768]{2,1,0:T(8,128)(2,1)} %get-tuple-element.186), channel_id=1, source_target_pairs={{0,8},{4,12},{8,0},{12,4},{1,9},{5,13},{9,1},{13,5},{2,10},{6,14},... | collective-permute-start | bytes 1327112 | tf_op jit(solution)/shard_map/ppermute | solution.py:698
  337.5 19.6 %collective-permute-start.24 = (bf16[4,72,768]{2,1,0:T(8,128)(2,1)}, bf16[4,72,768]{2,1,0:T(8,128)(2,1)S(1)}, u32[]{:S(2)}, u32[]{:S(2)}) collective-permute-start(bf16[4,72,768]{2,1,0:T(8,128)(2,1)} %get-tuple-element.187), channel_id=1, source_target_pairs={{0,4},{4,8},{8,12},{12,0},{1,5},{5,9},{9,13},{13,1},{2,6},{6,10},{... | collective-permute-start | bytes 1327112 | tf_op jit(solution)/shard_map/ppermute | solution.py:698
  364.7 15.9 %collective-permute-start.29 = (bf16[72,1920]{1,0:T(8,128)(2,1)}, bf16[72,1920]{1,0:T(8,128)(2,1)S(1)}, u32[]{:S(2)}, u32[]{:S(2)}) collective-permute-start(bf16[72,1920]{1,0:T(8,128)(2,1)} %get-tuple-element.194), channel_id=1, source_target_pairs={{0,16},{16,32},{32,48},{48,0},{1,17},{17,33},{33,49},{49,1},{2,18}... | collective-permute-start | bytes 829448 | tf_op jit(solution)/shard_map/ppermute | solution.py:698
  364.7 15.9 %collective-permute-start.30 = (bf16[72,1920]{1,0:T(8,128)(2,1)}, bf16[72,1920]{1,0:T(8,128)(2,1)S(1)}, u32[]{:S(2)}, u32[]{:S(2)}) collective-permute-start(bf16[72,1920]{1,0:T(8,128)(2,1)} %get-tuple-element.195), channel_id=1, source_target_pairs={{0,48},{16,0},{32,16},{48,32},{1,49},{17,1},{33,17},{49,33},{2,50}... | collective-permute-start | bytes 829448 | tf_op jit(solution)/shard_map/ppermute | solution.py:698
  368.0 12.7 %collective-permute-start.31 = (bf16[72,1920]{1,0:T(8,128)(2,1)}, bf16[72,1920]{1,0:T(8,128)(2,1)S(1)}, u32[]{:S(2)}, u32[]{:S(2)}) collective-permute-start(bf16[72,1920]{1,0:T(8,128)(2,1)} %get-tuple-element.196), channel_id=1, source_target_pairs={{0,32},{16,48},{32,0},{48,16},{1,33},{17,49},{33,1},{49,17},{2,34}... | collective-permute-start | bytes 829448 | tf_op jit(solution)/shard_map/ppermute | solution.py:698
  (57 other events, 682.0 us)
Sparse Core Ops, SparseCore 0:
  16.9 152.6 all-gather.1
